TPU v7x, 256 devices: a whole 4x4x8 slice. The times are simulated.
256 devices in a mesh: image: 4 (over y), swarm: 16 (over z_hi, x), domain: 4 (over z_lo, core).
Axes of the slice: x: 4, y: 4, z: 8 (z_hi: 4, z_lo: 2; z = z_hi * 2 + z_lo), core: 2. Of those that a mesh axis runs over, the one named last changes fastest.
Arguments:
- configuration: float32 [4, 3, 4, 16384], P('image', None, 'domain', 'swarm'), may hold values from -1 to 1
- velocities: float32 [4, 3, 4, 16, 16384], P('image', None, 'domain', None, 'swarm'), may hold values from -6 to 6
- pairs: int32 [4, 128, 2], P('domain'), may hold values from 0 to 191, as said below
- cv_atoms: int32 [128, 16], replicated, may hold values from 0 to 65535
Outputs:
- final_positions: float32 [4, 16, 3, 4, 16384], P('image', 'swarm', None, 'domain')
- new_string: float32 [4, 3, 128], P('image')
Inputs may be any that keep to these rules, and one draw needn't show every extreme that they name: pairs[d, t] names 2 different extended tiles, none of them t + 32 itself, each within 32 tiles of it.
All inputs are finite; a program needn't handle non-finite values.
Results may differ from a plain program's by a relative error of at most 0.000064.
Values sent between devices are 32-bit elements; how exact they have to be, the bound alone decides.
No kernel may reach another device: no remote copies, remote signals or barrier semaphores. Data moves between devices by JAX's collectives and lax.ppermute only.
A program may use at most 128 MiB of HBM per device.

v0:
```python
import math

import jax
import jax.numpy as jnp
from jax import lax
from jax.sharding import PartitionSpec as P

HALO = 4096
GSIZE = 16


time_step = 0.25
cutoff_sq = 2.0
strength = 0.1
smoothing = 0.25


def extended_2(block, sides, width):
    for axis, dim in sides:
        count = lax.axis_size(axis)
        forward = [(i, i + 1) for i in range(count - 1)]
        backward = [(target, source) for source, target in forward]
        low = lax.ppermute(
            lax.slice_in_dim(block, block.shape[dim] - width, None, axis=dim), axis, forward
        )
        high = lax.ppermute(lax.slice_in_dim(block, 0, width, axis=dim), axis, backward)
        block = jnp.concatenate([low, block, high], axis=dim)
    return block


def from_behind(value, axis, steps):
    count = lax.axis_size(axis)
    leading, last = (max(0, -steps), min(count, count - steps))
    return lax.ppermute(value, axis, [(source, source + steps) for source in range(leading, last)])


def tile_forces(extended, partners, first_tile, tile_count):
    halo_tiles = HALO // 128
    tile_view = extended.reshape(3, extended.shape[1] // 128, 128)
    block_size = math.gcd(16, tile_count)

    def one_block(block_start):
        own_ids = block_start + jnp.arange(block_size, dtype=jnp.int32)
        listed = lax.dynamic_slice_in_dim(partners, block_start, block_size, 0)
        partner_ids = jnp.concatenate([(own_ids + halo_tiles)[:, None], listed], 1)
        own_rows = jnp.take(tile_view, own_ids + halo_tiles, axis=1)
        others = jnp.take(tile_view, partner_ids, axis=1)
        gap_sq = jnp.zeros((block_size, partner_ids.shape[1], 128, 128), jnp.float32)
        for component in range(3):
            gap = own_rows[component][:, None, :, None] - others[component][:, :, None, :]
            gap_sq = gap_sq + gap * gap
        weight = jnp.square(jnp.maximum(1.0 - gap_sq / cutoff_sq, 0.0))
        row_total = jnp.sum(weight, axis=(1, 3))
        pulled = jnp.einsum("bpij,cbpj->cbi", weight, others, precision=lax.Precision.HIGHEST)
        return strength * (own_rows * row_total[None] - pulled)

    starts = first_tile + block_size * jnp.arange(tile_count // block_size, dtype=jnp.int32)
    blocks_out = lax.map(one_block, starts)
    return jnp.moveaxis(blocks_out, 1, 0).reshape(3, tile_count * 128)


def extend(positions):
    return extended_2(positions, (("domain", 1),), HALO)


def on_device(configuration, velocities, pairs, cv_atoms):
    members = lax.axis_size("swarm")
    atoms_here = velocities.shape[4] * members
    tile_count = atoms_here // 128
    partners = pairs[0]
    start_all = lax.all_gather(configuration, "swarm", axis=3, tiled=True)
    vel_all = lax.all_to_all(velocities, "swarm", split_axis=3, concat_axis=4, tiled=True)
    start_pos = start_all.reshape(3, atoms_here)
    start_vel = vel_all.reshape(3, atoms_here)
    first_push = tile_forces(extend(start_pos), partners, 0, tile_count)
    velocity = start_vel + time_step * first_push
    middle = start_pos + time_step * velocity
    velocity = velocity + time_step * tile_forces(extend(middle), partners, 0, tile_count)
    end_pos = middle + time_step * velocity
    final_positions = end_pos.reshape(1, 1, 3, 1, atoms_here)
    local_ids = cv_atoms - lax.axis_index("domain") * atoms_here
    inside = (local_ids >= 0) & (local_ids < atoms_here)
    clipped = jnp.clip(local_ids, 0, atoms_here - 1)
    moved_part = jnp.sum(
        jnp.where(inside[None], jnp.take(end_pos - start_pos, clipped, axis=1), 0.0), axis=-1
    )
    placed = jnp.sum(jnp.where(inside[None], jnp.take(start_pos, clipped, axis=1), 0.0), axis=-1)
    moved_sum, placed_sum = lax.psum((moved_part, placed), ("swarm", "domain"))
    updated = placed_sum / (members * GSIZE) + moved_sum / (members * GSIZE)
    earlier = from_behind(updated, "image", 1)
    later_string = from_behind(updated, "image", -1)
    position = lax.axis_index("image")
    neighbours = (position > 0).astype(jnp.float32) + (
        position < lax.axis_size("image") - 1
    ).astype(jnp.float32)
    new_string = (updated + smoothing * (earlier + later_string - neighbours * updated))[None]
    return (final_positions, new_string)


def solution(mesh):
    in_specs = (
        P("image", None, "domain", "swarm"),
        P("image", None, "domain", None, "swarm"),
        P("domain", None, None),
        P(),
    )
    out_specs = (P("image", "swarm", None, "domain", None), P("image", None, None))
    return jax.shard_map(
        on_device, mesh=mesh, in_specs=in_specs, out_specs=out_specs, check_vma=False
    )
```

profile of v0, /device:TPU:1, one launch (start us, length us, event | category | flops | bytes accessed | tf_op | source)
XLA Modules:
  0.0 787.0 jit_solution(8993984627931020864)
XLA Ops:
  1.6 201.8 %all_gather.3 = f32[1,3,1,16384]{1,3,2,0:T(8,128)S(1)} all-gather(f32[1,3,1,1024]{1,3,2,0:T(8,128)S(1)} %copy.117), channel_id=1, replica_groups=mesh['image'=4,'swarm'=16,'domain'=4] {'swarm'}, dimensions={3}, use_global_device_ids=true | all-gather | bytes 208896 | tf_op jit(solution)/shard_map/all_gather | solution.py:71
  205.1 2.1 copy-done
  207.3 2.2 copy.121
  209.5 3.2 collective-permute-start.1
  213.3 5.2 collective-permute-start
  219.4 8.3 %all-to-all-start = ((f32[1,3,1,16,1024]{4,1,2,0,3:T(4,128)}), f32[1,3,1,16,1024]{4,1,2,0,3:T(4,128)S(1)}, u32[]{:S(2)}, u32[]{:S(2)}) async-start(f32[1,3,1,16,1024]{4,1,2,0,3:T(4,128)} %copy.118), calls=%async_computation | async-start | bytes 524288 | tf_op jit(solution)/shard_map/all_to_all | solution.py:72
  227.8 5.5 copy.122
  233.6 104.4 %while.20 = (s32[]{:T(128)}, f32[8,3,16,128]{3,1,2,0:T(4,128)S(1)}, s32[8]{0:T(128)S(1)}, f32[3,192,128]{2,0,1:T(4,128)S(1)}, s32[128,2]{0,1:T(2,128)S(1)}, /*index=5*/s32[]{:T(128)}, s32[]{:T(128)}, s32[]{:T(128)}) while((s32[]{:T(128)}, f32[8,3,16,128]{3,1,2,0:T(4,128)S(1)}, s32[8]{0:T(128)S(1)}, f32[3,192,128]{2,0,1:T(4,128)S(1)}, ...), condition=%wide.region_2.5_spmd, body=%wide.region_0.4_spmd.sunk | while | flops 48016132 | bytes 1002047 | solution.py:58
  241.9 4.7 fusion.66
  253.0 1.9 fusion.65
  254.9 4.7 fusion.66
  268.0 4.7 fusion.66
  279.1 1.9 fusion.65
  281.0 4.7 fusion.66
  292.2 1.9 fusion.65
  294.1 4.7 fusion.66
  307.1 4.7 fusion.66
  320.2 4.7 fusion.66
  331.3 1.9 fusion.65
  333.2 4.7 fusion.66
  338.1 4.6 copy.124
  342.7 4.7 copy.119
  347.4 8.8 %multiply_add_fusion = f32[3,16384]{0,1:T(8,128)S(1)} fusion(f32[3,8,16,128]{0,3,2,1:T(8,128)} %copy.124, f32[1,3,1,16,1024]{1,4,3,2,0:T(8,128)} %copy.119, f32[1,3,1,16384]{1,3,2,0:T(8,128)} %copy-done), kind=kLoop, calls=%fused_computation.84 | loop fusion | flops 147456 | bytes 786432 | tf_op jit(solution)/shard_map/add | solution.py:77
  358.1 2.0 copy-done.1
  360.1 2.2 copy.128
  362.3 1.9 collective-permute-start.3
  364.8 3.8 collective-permute-start.2
  368.9 8.8 %gather_fusion.4 = f32[2048,3]{1,0:T(8,128)S(1)} fusion(f32[3,16384]{0,1:T(8,128)} %bitcast.164, s32[2048]{0:T(1024)S(1)} %broadcast_clamp_fusion), kind=kCustom, calls=%fused_computation.2.clone | custom fusion | bytes 57344 | tf_op jit(solution)/shard_map/jit(_take)/gather | solution.py:87
  377.8 5.5 copy.129
  383.4 104.4 %while.21 = (s32[]{:T(128)}, f32[8,3,16,128]{3,1,2,0:T(4,128)S(1)}, s32[8]{0:T(128)S(1)}, f32[3,192,128]{2,0,1:T(4,128)S(1)}, s32[128,2]{0,1:T(2,128)S(1)}, /*index=5*/s32[]{:T(128)}, s32[]{:T(128)}, s32[]{:T(128)}) while((s32[]{:T(128)}, f32[8,3,16,128]{3,1,2,0:T(4,128)S(1)}, s32[8]{0:T(128)S(1)}, f32[3,192,128]{2,0,1:T(4,128)S(1)}, ...), condition=%wide.region_5.8_spmd, body=%wide.region_3.7_spmd.sunk | while | flops 48016132 | bytes 1002047 | solution.py:58
  389.8 1.9 fusion.70
  391.7 4.7 fusion.71
  404.8 4.7 fusion.71
  415.9 1.9 fusion.70
  417.8 4.7 fusion.71
  428.9 1.9 fusion.70
  430.9 4.7 fusion.71
  443.9 4.7 fusion.71
  457.0 4.7 fusion.71
  470.0 4.7 fusion.71
  483.1 4.7 fusion.71
  487.9 4.6 copy.131
  492.5 15.0 %fusion.44 = f32[3,16384]{0,1:T(8,128)} fusion(f32[3,8,16,128]{0,3,2,1:T(8,128)} %copy.131, f32[3,8,16,128]{0,3,2,1:T(8,128)} %copy.124, f32[1,3,1,16,1024]{1,4,3,2,0:T(8,128)} %copy.119, f32[1,3,1,16384]{1,3,2,0:T(8,128)} %copy-done), kind=kLoop, calls=%fused_computation.79 | loop fusion | flops 344064 | bytes 983040 | tf_op jit(solution)/shard_map/sub | solution.py:85
  507.6 8.8 %gather_fusion.5 = f32[2048,3]{1,0:T(8,128)S(1)} fusion(f32[3,16384]{0,1:T(8,128)} %fusion.44, s32[2048]{0:T(1024)S(1)} %broadcast_clamp_fusion), kind=kCustom, calls=%fused_computation.5.clone | custom fusion | bytes 57344 | tf_op jit(solution)/shard_map/jit(_take)/gather | solution.py:85
  517.5 243.6 %psum.16 = f32[3,128]{0,1:T(8,128)S(1)} all-reduce(f32[3,128]{0,1:T(8,128)S(1)} %div.10), channel_id=1, replica_groups=mesh['image'=4,'swarm'=16,'domain'=4] {'swarm','domain'}, use_global_device_ids=true, to_apply=%region_7.11 | all-reduce | flops 384 | bytes 3072 | tf_op jit(solution)/shard_map/psum | solution.py:88
  761.1 3.2 collective-permute-start.4
  765.6 14.9 %fusion.45 = f32[1,1,3,1,16384]{2,4,3,1,0:T(8,128)} fusion(f32[1,3,1,16384]{1,3,2,0:T(8,128)} %copy-done, f32[1,1,3,1,16384]{2,4,3,1,0:T(8,128)} %bitcast.166, f32[1,1,3,1,16384]{2,4,3,1,0:T(8,128)} %bitcast.165, f32[1,3,1,16,1024]{1,4,3,2,0:T(8,128)} %copy.119), kind=kLoop, calls=%fused_computation.83 | loop fusion | flops 294912 | bytes 983040 | tf_op jit(solution)/shard_map/add | solution.py:79
  780.5 5.9 copy.138
  (337 shorter events, 97.6 us)
Async XLA Ops:
  203.3 3.9 copy-start
  207.3 11.3 %copy-start.2 = (f32[1,3,1,16,1024]{4,3,2,1,0:T(8,128)S(1)}, f32[1,3,1,16,1024]{4,3,2,1,0:T(8,128)}, u32[]{:S(2)}) copy-start(f32[1,3,1,16,1024]{4,3,2,1,0:T(8,128)} %param.15) | copy-start | bytes 589828
  207.3 20.5 %copy-start.4 = (s32[128,16]{0,1:T(8,128)S(1)}, s32[128,16]{0,1:T(8,128)}, u32[]{:S(2)}) copy-start(s32[128,16]{0,1:T(8,128)} %param.17) | copy-start | bytes 24580
  209.5 23.9 %collective-permute-start.1 = (f32[3,4096]{1,0:T(4,128)S(1)}, f32[3,4096]{1,0:T(4,128)S(1)}, u32[]{:S(2)}, u32[]{:S(2)}) collective-permute-start(f32[3,4096]{1,0:T(4,128)S(1)} %copy.121), channel_id=1, source_target_pairs={{1,0},{2,1},{3,2},{5,4},{6,5},{7,6},{9,8},{10,9},{11,10},{13,12},{... | collective-permute-start | bytes 147464 | tf_op jit(solution)/shard_map/ppermute | solution.py:26
  213.3 20.1 %collective-permute-start = (f32[3,4096]{1,0:T(4,128)S(1)}, f32[3,4096]{1,0:T(4,128)S(1)}, u32[]{:S(2)}, u32[]{:S(2)}) collective-permute-start(f32[3,4096]{1,0:T(4,128)S(1)} %copy.120), channel_id=1, source_target_pairs={{0,1},{1,2},{2,3},{4,5},{5,6},{6,7},{8,9},{9,10},{10,11},{12,13},{... | collective-permute-start | bytes 147464 | tf_op jit(solution)/shard_map/ppermute | solution.py:23
  219.4 123.3 %all-to-all-start = ((f32[1,3,1,16,1024]{4,1,2,0,3:T(4,128)}), f32[1,3,1,16,1024]{4,1,2,0,3:T(4,128)S(1)}, u32[]{:S(2)}, u32[]{:S(2)}) async-start(f32[1,3,1,16,1024]{4,1,2,0,3:T(4,128)} %copy.118), calls=%async_computation | async-start | bytes 524288 | tf_op jit(solution)/shard_map/all_to_all | solution.py:72
  227.8 5.8 copy-start.3
  356.2 3.8 copy-start.1
  362.3 21.0 %collective-permute-start.3 = (f32[3,4096]{1,0:T(4,128)S(1)}, f32[3,4096]{1,0:T(4,128)S(1)}, u32[]{:S(2)}, u32[]{:S(2)}) collective-permute-start(f32[3,4096]{1,0:T(4,128)S(1)} %copy.128), channel_id=1, source_target_pairs={{1,0},{2,1},{3,2},{5,4},{6,5},{7,6},{9,8},{10,9},{11,10},{13,12},{... | collective-permute-start | bytes 147464 | tf_op jit(solution)/shard_map/ppermute | solution.py:26
  364.8 18.4 %collective-permute-start.2 = (f32[3,4096]{1,0:T(4,128)S(1)}, f32[3,4096]{1,0:T(4,128)S(1)}, u32[]{:S(2)}, u32[]{:S(2)}) collective-permute-start(f32[3,4096]{1,0:T(4,128)S(1)} %copy.127), channel_id=1, source_target_pairs={{0,1},{1,2},{2,3},{4,5},{5,6},{6,7},{8,9},{9,10},{10,11},{12,13},{... | collective-permute-start | bytes 147464 | tf_op jit(solution)/shard_map/ppermute | solution.py:23
  761.1 25.3 %collective-permute-start.4 = (f32[3,128]{0,1:T(8,128)S(1)}, f32[3,128]{0,1:T(8,128)S(1)}, u32[]{:S(2)}, u32[]{:S(2)}) collective-permute-start(f32[3,128]{0,1:T(8,128)S(1)} %broadcast_multiply_fusion), channel_id=1, source_target_pairs={{0,64},{64,128},{128,192},{1,65},{65,129},{129,193},{2,66},{66,130... | collective-permute-start | bytes 4616 | tf_op jit(solution)/shard_map/ppermute | solution.py:34
  764.3 22.1 %collective-permute-start.5 = (f32[3,128]{0,1:T(8,128)S(1)}, f32[3,128]{0,1:T(8,128)S(1)}, u32[]{:S(2)}, u32[]{:S(2)}) collective-permute-start(f32[3,128]{0,1:T(8,128)S(1)} %broadcast_multiply_fusion), channel_id=1, source_target_pairs={{64,0},{128,64},{192,128},{65,1},{129,65},{193,129},{66,2},{130,66... | collective-permute-start | bytes 4616 | tf_op jit(solution)/shard_map/ppermute | solution.py:34
where the time goes:
time: 794 us; the launch traced here: 787 us
  blocking collectives  445 us (56%)
  other arithmetic  105 us (13%)
  local copies, waits for them, and re-layouts  100 us (13%)
  matrix products  75.8 us (10%)
  loops' own time  32.6 us (4%)
  starting transfers between devices  26.9 us (3%)
    psum x1, blocking collectives, on_device(): moved_sum, placed_sum = lax.psum((moved_part, placed), ('swarm', 'domain'))  244 us
    all_gather x1, blocking collectives, on_device(): start_all = lax.all_gather(configuration, 'swarm', axis=3, tiled=True)  202 us
    dot_general x16, matrix products, one_block(): jnp.einsum('bpij,cbpj->cbi', weight, others, precision=lax.Precision.HIGH...  75.8 us
    another operation x2, loops' own time, tile_forces(): blocks_out = lax.map(one_block, starts)  32.6 us
    reduce_sum x16, other arithmetic, one_block(): row_total = jnp.sum(weight, axis=(1, 3))  30.6 us
  transfers between devices with their start and end apart: 7, of which 0 were waited for; matrix products, arithmetic and copies ran while one was open for 17% of the time, Pallas kernels for 0%

commit v1 on v0

v1 whole, which is shorter than its diff:
```python
import functools

import jax
import jax.numpy as jnp
from jax import lax
from jax.experimental import pallas as pl
from jax.experimental.pallas import tpu as pltpu
from jax.sharding import PartitionSpec as P

HALO = 4096
GSIZE = 16
LANES = 128
ROWS = 8

time_step = 0.25
strength = 0.1
smoothing = 0.25

F32 = jnp.float32
BF16 = jnp.bfloat16


def three_parts(value):
    high = value.astype(BF16).astype(F32)
    rest = value - high
    middle = rest.astype(BF16).astype(F32)
    return high, middle, rest - middle


def put_rows(ref, rows):
    for place, row in enumerate(rows):
        ref[place * ROWS:(place + 1) * ROWS, :] = row


def build_group(field, rows_q, rows_v, columns, values, first):
    one, zero = jnp.ones((ROWS, LANES), F32), jnp.zeros((ROWS, LANES), F32)
    parts = [three_parts(x) for x in field]
    norm = three_parts(0.5 - 0.5 * (field[0] * field[0] + field[1] * field[1] + field[2] * field[2]))
    of_q = []
    for h, m, l in parts:
        of_q += [h, m, h, m, l, h]
    put_rows(rows_q, of_q + [one] * 3 + list(norm) + [zero] * 8)
    put_rows(
        rows_v,
        [p[0] for p in parts] + [one] + [p[2] for p in parts] + [zero]
        + [p[1] for p in parts] + [zero] * 5,
    )
    for t in range(ROWS):
        table = rows_q[pl.ds(t, 32, stride=ROWS), :]
        columns[first + t] = table.T.astype(BF16)
        values[first + t] = rows_v[pl.ds(t, 16, stride=ROWS), :].astype(BF16)


def own_rows(field, rows_p):
    one, zero = jnp.ones((ROWS, LANES), F32), jnp.zeros((ROWS, LANES), F32)
    norm = three_parts(0.5 - 0.5 * (field[0] * field[0] + field[1] * field[1] + field[2] * field[2]))
    of_p = []
    for x in field:
        h, m, l = three_parts(x)
        of_p += [h, h, m, m, h, l]
    put_rows(rows_p, of_p + list(norm) + [one] * 3 + [zero] * 8)


def group_forces(field, tile0, shift, pairs, rows_p, sums, columns, values):
    own_rows(field, rows_p)
    halo_tiles = HALO // LANES
    for t in range(ROWS):
        tile = tile0 + t
        others = [tile + halo_tiles, pairs[tile, 0], pairs[tile, 1]]
        others = [e - shift for e in others]
        p_side = rows_p[pl.ds(t, 32, stride=ROWS), :].astype(BF16)
        q_side = jnp.concatenate([columns[e] for e in others], axis=0)
        overlap = jnp.maximum(jnp.dot(q_side, p_side, preferred_element_type=F32), 0.0)
        weight = overlap * overlap
        high = weight.astype(BF16)
        low = (weight - high.astype(F32)).astype(BF16)
        q_values = jnp.concatenate([values[e] for e in others], axis=1)
        sums[t * 16:(t + 1) * 16, :] = jnp.dot(
            q_values, high, preferred_element_type=F32
        ) + jnp.dot(q_values, low, preferred_element_type=F32)
    row = lambda r: sums[pl.ds(r, ROWS, stride=16), :]
    total = row(3)
    return [
        strength * (field[c] * total - (row(c) + row(8 + c) + row(4 + c))) for c in range(3)
    ]


def inner_kernel(pairs, field_ref, out_ref, rows_q, rows_v, rows_p, sums, columns, values):
    @pl.loop(0, 16)
    def _(s):
        build_group([field_ref[s, c] for c in range(3)], rows_q, rows_v, columns, values, s * ROWS)

    @pl.loop(0, 8)
    def _(s):
        field = [field_ref[s + 4, c] for c in range(3)]
        force = group_forces(
            field, (s + 4) * ROWS, HALO // LANES, pairs, rows_p, sums, columns, values
        )
        for c in range(3):
            out_ref[s, c] = force[c]


def rim_forces(pairs, field_ref, low_ref, high_ref, rows_q, rows_v, rows_p, sums, columns, values, emit):
    for ref, first, count in ((low_ref, 0, 4), (field_ref, 4, 16), (high_ref, 20, 4)):

        @pl.loop(0, count)
        def _(s):
            build_group(
                [ref[s, c] for c in range(3)], rows_q, rows_v, columns, values, (first + s) * ROWS
            )

    @pl.loop(0, 8)
    def _(step):
        s = jnp.where(step < 4, step, step + 8)
        field = [field_ref[s, c] for c in range(3)]
        force = group_forces(field, s * ROWS, 0, pairs, rows_p, sums, columns, values)
        for c in range(3):
            emit(s, c, force[c])


def first_rim_kernel(
    pairs, field_ref, low_ref, high_ref, inner_ref, vel_ref,
    middle_ref, base_ref, rim_low_ref, rim_high_ref,
    rows_q, rows_v, rows_p, sums, columns, values,
):
    def step(s, c, force):
        velocity = vel_ref[s, c] + time_step * force
        middle = field_ref[s, c] + time_step * velocity
        middle_ref[s, c] = middle
        base_ref[s, c] = middle + time_step * velocity

    rim_forces(
        pairs, field_ref, low_ref, high_ref, rows_q, rows_v, rows_p, sums, columns, values, step
    )

    @pl.loop(0, 8)
    def _(s):
        for c in range(3):
            step(s + 4, c, inner_ref[s, c])

    rim_low_ref[...] = middle_ref[0:4]
    rim_high_ref[...] = middle_ref[12:16]


def second_rim_kernel(
    pairs, domain_ref, groups_ref, field_ref, low_ref, high_ref, inner_ref, base_ref,
    final_ref, part_ref,
    rows_q, rows_v, rows_p, sums, columns, values,
):
    def step(s, c, force):
        final_ref[c, pl.ds(pl.multiple_of(s * ROWS, ROWS), ROWS), :] = (
            base_ref[s, c] + (time_step * time_step) * force
        )

    rim_forces(
        pairs, field_ref, low_ref, high_ref, rows_q, rows_v, rows_p, sums, columns, values, step
    )

    @pl.loop(0, 8)
    def _(s):
        for c in range(3):
            step(s + 4, c, inner_ref[s, c])

    local = groups_ref[...] - domain_ref[0] * (LANES * LANES)
    tile_of, lane_of = local >> 7, local & 127
    columns_of = []
    for c in range(3):
        columns_of.append(
            jnp.concatenate([p.astype(BF16) for p in three_parts(final_ref[c].T)], axis=1)
        )
    moving = jnp.concatenate(columns_of, axis=0)
    down = lax.broadcasted_iota(jnp.int32, (LANES, LANES), 0)
    total = jnp.zeros((3 * LANES, LANES), F32)
    for g in range(GSIZE):
        chosen = (down == tile_of[g:g + 1, :]).astype(F32).astype(BF16)
        here = (down == lane_of[g:g + 1, :]).astype(F32)
        found = jnp.dot(
            moving, jnp.concatenate([chosen] * 3, axis=0), preferred_element_type=F32
        )
        total = total + found * jnp.concatenate([here] * 3, axis=0)
    zero = jnp.zeros((1, LANES), F32)
    part_ref[...] = jnp.concatenate(
        [jnp.sum(total[c * LANES:(c + 1) * LANES], axis=0, keepdims=True) for c in range(3)]
        + [zero] * 5,
        axis=0,
    )


def pack_kernel(vel_ref, conf_ref, out_ref):
    for c in range(3):
        for j in range(ROWS):
            for half in range(2):
                out_ref[pl.ds(half * 8 * 48 + c * ROWS + j, ROWS, stride=48), :] = vel_ref[
                    c, half * 8:half * 8 + 8, j * LANES:(j + 1) * LANES
                ]
        for m in range(16):
            out_ref[m * 48 + 24 + c * ROWS:m * 48 + 32 + c * ROWS, :] = conf_ref[c]


VMEM = pl.BlockSpec(memory_space=pltpu.VMEM)
SMEM = pl.BlockSpec(memory_space=pltpu.SMEM)


def scratch(tiles):
    return [
        pltpu.VMEM((32 * ROWS, LANES), F32),
        pltpu.VMEM((16 * ROWS, LANES), F32),
        pltpu.VMEM((32 * ROWS, LANES), F32),
        pltpu.VMEM((16 * ROWS, LANES), F32),
        pltpu.VMEM((tiles, LANES, 32), BF16),
        pltpu.VMEM((tiles, 16, LANES), BF16),
    ]


def call(kernel, name, out, specs, scratches, flops, moved):
    return pl.pallas_call(
        kernel,
        out_shape=out,
        in_specs=specs,
        out_specs=jax.tree.map(lambda _: VMEM, out),
        scratch_shapes=scratches,
        compiler_params=pltpu.CompilerParams(vmem_limit_bytes=40 * 1024 * 1024),
        cost_estimate=pl.CostEstimate(flops=flops, bytes_accessed=moved, transcendentals=0),
        name=name,
    )


WORK = 8_000_000_000


def shape(*dims):
    return jax.ShapeDtypeStruct(dims, F32)


def rims(low, high):
    count = lax.axis_size("domain")
    forward = [(i, i + 1) for i in range(count - 1)]
    backward = [(i + 1, i) for i in range(count - 1)]
    return lax.ppermute(high, "domain", forward), lax.ppermute(low, "domain", backward)


def on_device(configuration, velocities, pairs, cv_atoms):
    partners = pairs[0]
    groups = cv_atoms.T
    domain = lax.axis_index("domain").astype(jnp.int32).reshape(1)
    packed = call(pack_kernel, "pack", shape(16 * 48, LANES), [VMEM, VMEM], [], 0, 600_000)(
        velocities.reshape(3, 16, 1024), configuration.reshape(3, ROWS, LANES)
    )
    got = lax.all_to_all(
        packed.reshape(16, 6, ROWS, LANES), "swarm", split_axis=0, concat_axis=0, tiled=True
    )
    start_vel, start_pos = got[:, :3], got[:, 3:]

    inner = call(inner_kernel, "inner", shape(8, 3, ROWS, LANES), [SMEM, VMEM], scratch(128), WORK, 0)
    low, high = rims(start_pos[0:4], start_pos[12:16])
    inside = inner(partners, start_pos)
    whole, rim = shape(16, 3, ROWS, LANES), shape(4, 3, ROWS, LANES)
    middle, base, rim_low, rim_high = call(
        first_rim_kernel, "first_rim", (whole, whole, rim, rim), [SMEM] + [VMEM] * 5,
        scratch(192), WORK, 0,
    )(partners, start_pos, low, high, inside, start_vel)

    low, high = rims(rim_low, rim_high)
    inside = inner(partners, middle)
    final, part = call(
        second_rim_kernel, "second_rim", (shape(3, LANES, LANES), shape(ROWS, LANES)),
        [SMEM, SMEM] + [VMEM] * 6, scratch(192), WORK, 0,
    )(partners, domain, groups, middle, low, high, inside, base)
    final_positions = final.reshape(1, 1, 3, 1, LANES * LANES)

    here = part
    for offset in range(1, 4):
        here = here + lax.ppermute(part, "domain", [(i, i ^ offset) for i in range(4)])
    images, members = lax.axis_size("image"), lax.axis_size("swarm")
    everyone = lax.all_to_all(
        jnp.broadcast_to(here[None], (images * members, ROWS, LANES)),
        ("image", "swarm"), split_axis=0, concat_axis=0, tiled=True,
    )
    updated = jnp.sum(everyone.reshape(images, members, ROWS, LANES), axis=1) / (members * GSIZE)
    place = lax.axis_index("image")
    ids = jnp.arange(images)
    neighbours = (place > 0).astype(F32) + (place < images - 1).astype(F32)
    share = jnp.where(jnp.abs(ids - place) == 1, smoothing, 0.0) + jnp.where(
        ids == place, 1.0 - smoothing * neighbours, 0.0
    )
    new_string = jnp.sum(share[:, None, None] * updated, axis=0)[None, :3]
    return (final_positions, new_string)


def solution(mesh):
    in_specs = (
        P("image", None, "domain", "swarm"),
        P("image", None, "domain", None, "swarm"),
        P("domain", None, None),
        P(),
    )
    out_specs = (P("image", "swarm", None, "domain", None), P("image", None, None))
    return jax.shard_map(
        on_device, mesh=mesh, in_specs=in_specs, out_specs=out_specs, check_vma=False
    )
```

time: 794 us -> 134 us (0.17)
  blocking collectives: 445 us -> 0 us
  other arithmetic: 105 us -> 0.11 us
  local copies, waits for them, and re-layouts: 100 us -> 3.74 us
  matrix products: 75.8 us -> 0 us
  Pallas kernels: 0 us -> 66.1 us
  loops' own time: 32.6 us -> 0 us
  waiting for transfers between devices: 0.02 us -> 27.8 us
  starting transfers between devices: 26.9 us -> 35.3 us
    psum x1 -> x0, blocking collectives: 244 us -> none  [on_device(): moved_sum, placed_sum = lax.psum((moved_part, placed), ('swarm', 'domain'))]
    all_gather x1 -> x0, blocking collectives: 202 us -> none  [on_device(): start_all = lax.all_gather(configuration, 'swarm', axis=3, tiled=True)]
    dot_general x16 -> x0, matrix products: 75.8 us -> none  [one_block(): jnp.einsum('bpij,cbpj->cbi', weight, others, precision=lax.Precision.HIGH...]
    pallas_call x0 -> x5, Pallas kernels: none -> 66.1 us  [the longest x1 18.1 us: on_device(): call(second_rim_kernel, 'second_rim', (shape(3, LANES, LANES), shape(ROWS...]
    gather x34 -> x0, local copies, waits for them, and re-layouts: 37.2 us -> none  [the longest x16 10.1 us: one_block(): others = jnp.take(tile_view, partner_ids, axis=1)]
    add x19 -> x1, other arithmetic: 34.2 us -> 0.01 us  [on_device(): here + lax.ppermute(part, 'domain', [(i, i ^ offset) for i in range(4)])]
    another operation x2 -> x0, loops' own time: 32.6 us -> none  [tile_forces(): blocks_out = lax.map(one_block, starts)]
    reduce_sum x17 -> x2, other arithmetic: 31.6 us -> 0.09 us  [the longest x1 0.08 us: on_device(): new_string = jnp.sum(share[:, None, None] * updated, axis=0)[None, :3]]
  transfers between devices with their start and end apart: 7 -> 9, of which waited for: 0 -> 4; matrix products, arithmetic and copies ran while one was open for 17% -> 0% of each run, Pallas kernels for 0% -> 23%
where the time goes in v1:
time: 134 us
  Pallas kernels  66.1 us (49%)
  starting transfers between devices  35.3 us (26%)
  waiting for transfers between devices  27.8 us (21%)
  local copies, waits for them, and re-layouts  3.74 us (3%)
    pallas_call x1, Pallas kernels, on_device(): call(second_rim_kernel, 'second_rim', (shape(3, LANES, LANES), shape(ROWS...  18.1 us
    pallas_call x1, Pallas kernels, on_device(): call(first_rim_kernel, 'first_rim', (whole, whole, rim, rim), [SMEM] + [V...  16.7 us
    pallas_call x1, Pallas kernels, on_device(): inside = inner(partners, start_pos)  15.2 us
    pallas_call x1, Pallas kernels, on_device(): inside = inner(partners, middle)  15.2 us
    all_to_all x1, waiting for transfers between devices, on_device(): lax.all_to_all(jnp.broadcast_to(here[None], (images * members, ROWS, LANE...  13.7 us
    all_to_all x1, starting transfers between devices, on_device(): lax.all_to_all(packed.reshape(16, 6, ROWS, LANES), 'swarm', split_axis=0,...  11.6 us
    all_to_all x1, waiting for transfers between devices, on_device(): lax.all_to_all(packed.reshape(16, 6, ROWS, LANES), 'swarm', split_axis=0,...  11.3 us
    ppermute x2, starting transfers between devices, rims(): lax.ppermute(high, 'domain', forward)  9.72 us
  transfers between devices with their start and end apart: 9, of which 4 were waited for; matrix products, arithmetic and copies ran while one was open for 0% of the time, Pallas kernels for 23%

profile of v1, /device:TPU:1, one launch (start us, length us, event | category | flops | bytes accessed | tf_op | source)
XLA Modules:
  0.0 133.8 jit_solution(4253383327525509635)
XLA Ops:
  0.6 0.0 copy-start
  0.6 0.9 copy-done
  1.6 0.0 copy-start.1
  1.6 0.7 copy-done.1
  2.3 0.8 pack.1
  3.1 11.6 %all-to-all-start = ((f32[16,6,8,128]{3,2,1,0:T(8,128)}), f32[16,6,8,128]{3,2,1,0:T(8,128)S(1)}, u32[]{:S(2)}, u32[]{:S(2)}) async-start(f32[16,6,8,128]{3,2,1,0:T(8,128)} %bitcast.5), calls=%async_computation | async-start | bytes 786432 | tf_op jit(solution)/shard_map/all_to_all | solution.py:249
  14.7 0.0 copy-start.3
  14.7 0.7 copy-done.3
  15.4 0.1 copy.10
  15.5 11.3 %all-to-all-done = f32[16,6,8,128]{3,2,1,0:T(8,128)S(1)} async-done(((f32[16,6,8,128]{3,2,1,0:T(8,128)}), f32[16,6,8,128]{3,2,1,0:T(8,128)S(1)}, u32[]{:S(2)}, u32[]{:S(2)}) %all-to-all-start) | async-done | bytes 393248 | tf_op jit(solution)/shard_map/all_to_all | solution.py:249
  26.8 6.1 %collective-permute-start = (f32[4,3,8,128]{3,2,1,0:T(8,128)S(1)}, f32[4,3,8,128]{3,2,1,0:T(8,128)S(1)}, u32[]{:S(2)}, u32[]{:S(2)}) collective-permute-start(f32[4,3,8,128]{3,2,1,0:T(8,128)S(1)} %get-tuple-element.23), channel_id=1, source_target_pairs={{0,1},{1,2},{2,3},{4,5},{5,6},{6,7},{8,9},{9,10},{10,11},{12,13},{... | collective-permute-start | bytes 147464 | tf_op jit(solution)/shard_map/ppermute | solution.py:239
  32.9 1.9 %collective-permute-start.1 = (f32[4,3,8,128]{3,2,1,0:T(8,128)S(1)}, f32[4,3,8,128]{3,2,1,0:T(8,128)S(1)}, u32[]{:S(2)}, u32[]{:S(2)}) collective-permute-start(f32[4,3,8,128]{3,2,1,0:T(8,128)S(1)} %get-tuple-element.22), channel_id=1, source_target_pairs={{1,0},{2,1},{3,2},{5,4},{6,5},{7,6},{9,8},{10,9},{11,10},{13,12},{... | collective-permute-start | bytes 147464 | tf_op jit(solution)/shard_map/ppermute | solution.py:239
  34.9 15.2 %inner.2.inner_ref = f32[8,3,8,128]{3,2,1,0:T(8,128)S(1)} custom-call(s32[128,2]{1,0:T(8,128)S(1)} %bitcast.12, f32[16,3,8,128]{3,2,1,0:T(8,128)S(1)} %get-tuple-element.21.field_ref), custom_call_target="tpu_custom_call" | custom-call | flops 8000000000 | tf_op jit(solution)/shard_map/inner/pallas_call | solution.py:256
  50.1 0.0 collective-permute-done.low_ref
  50.1 0.0 collective-permute-done.1.high_ref
  50.1 16.7 %first_rim.1 = (f32[16,3,8,128]{3,2,1,0:T(8,128)S(1)}, f32[16,3,8,128]{3,2,1,0:T(8,128)S(1)}, f32[4,3,8,128]{3,2,1,0:T(8,128)S(1)}, f32[4,3,8,128]{3,2,1,0:T(8,128)S(1)}) custom-call(s32[128,2]{1,0:T(8,128)S(1)} %bitcast.13, f32[16,3,8,128]{3,2,1,0:T(8,128)S(1)} %get-tuple-element.21.field_ref, f32[4,3,8,128]{3,2,1,0:T(8,128)S(1)} %collective-permute-done.low_ref, ...), custom_call_target="tpu_custom_call" | custom-call | flops 8000000000 | tf_op jit(solution)/shard_map/first_rim/pallas_call | solution.py:258
  66.8 3.6 %collective-permute-start.2 = (f32[4,3,8,128]{3,2,1,0:T(8,128)S(1)}, f32[4,3,8,128]{3,2,1,0:T(8,128)S(1)}, u32[]{:S(2)}, u32[]{:S(2)}) collective-permute-start(f32[4,3,8,128]{3,2,1,0:T(8,128)S(1)} %get-tuple-element.9), channel_id=1, source_target_pairs={{0,1},{1,2},{2,3},{4,5},{5,6},{6,7},{8,9},{9,10},{10,11},{12,13},{... | collective-permute-start | bytes 147464 | tf_op jit(solution)/shard_map/ppermute | solution.py:239
  70.5 1.9 %collective-permute-start.3 = (f32[4,3,8,128]{3,2,1,0:T(8,128)S(1)}, f32[4,3,8,128]{3,2,1,0:T(8,128)S(1)}, u32[]{:S(2)}, u32[]{:S(2)}) collective-permute-start(f32[4,3,8,128]{3,2,1,0:T(8,128)S(1)} %get-tuple-element.10), channel_id=1, source_target_pairs={{1,0},{2,1},{3,2},{5,4},{6,5},{7,6},{9,8},{10,9},{11,10},{13,12},{... | collective-permute-start | bytes 147464 | tf_op jit(solution)/shard_map/ppermute | solution.py:239
  72.4 0.0 copy-start.2
  72.4 15.2 %inner.3.inner_ref = f32[8,3,8,128]{3,2,1,0:T(8,128)S(1)} custom-call(s32[128,2]{1,0:T(8,128)S(1)} %bitcast.14, f32[16,3,8,128]{3,2,1,0:T(8,128)S(1)} %get-tuple-element.8.field_ref), custom_call_target="tpu_custom_call" | custom-call | flops 8000000000 | tf_op jit(solution)/shard_map/inner/pallas_call | solution.py:264
  87.7 0.0 collective-permute-done.2.low_ref
  87.7 0.0 collective-permute-done.3.high_ref
  87.7 0.0 copy-done.2
  87.7 18.1 %second_rim.1 = (f32[3,128,128]{2,1,0:T(8,128)}, f32[8,128]{1,0:T(8,128)S(1)}) custom-call(s32[128,2]{1,0:T(8,128)S(1)} %bitcast.15, s32[1]{0:T(128)} %bitcast.1.domain_ref, s32[16,128]{1,0:T(8,128)S(1)} %bitcast.17, f32[16,3,8,128]{3,2,1,0:T(8,128)S(1)} %get-tuple-element.8.field_ref, f32[4,3,8,128]{3,2,1,0:T(8,128)S(1)} %collective-permute-done.2.low_ref, ...), custom_call_target="tpu_custom_call" | custom-call | flops 8000000000 | tf_op jit(solution)/shard_map/second_rim/pallas_call | solution.py:265
  105.8 0.1 collective-permute-start.4
  105.9 1.9 %collective-permute-start.5 = (f32[8,128]{1,0:T(8,128)S(1)}, f32[8,128]{1,0:T(8,128)S(1)}, u32[]{:S(2)}, u32[]{:S(2)}) collective-permute-start(f32[8,128]{1,0:T(8,128)S(1)} %get-tuple-element.13), channel_id=1, source_target_pairs={{0,2},{1,3},{2,0},{3,1},{4,6},{5,7},{6,4},{7,5},{8,10},{9,11},{10,... | collective-permute-start | bytes 12296 | tf_op jit(solution)/shard_map/ppermute | solution.py:273
  107.8 0.3 collective-permute-start.6
  108.0 0.0 collective-permute-done.4
  108.0 0.7 collective-permute-done.5
  108.7 2.1 %collective-permute-done.6 = f32[8,128]{1,0:T(8,128)S(1)} collective-permute-done((f32[8,128]{1,0:T(8,128)S(1)}, f32[8,128]{1,0:T(8,128)S(1)}, u32[]{:S(2)}, u32[]{:S(2)}) %collective-permute-start.6) | collective-permute-done | bytes 4128 | tf_op jit(solution)/shard_map/ppermute | solution.py:273
  110.8 0.7 broadcast_in_dim.24
  111.5 7.9 %all-to-all-start.1 = ((f32[64,8,128]{2,1,0:T(8,128)}), f32[64,8,128]{2,1,0:T(8,128)S(1)}, u32[]{:S(2)}, u32[]{:S(2)}) async-start(f32[64,8,128]{2,1,0:T(8,128)} %broadcast_in_dim.24), calls=%async_computation.1 | async-start | bytes 524288 | tf_op jit(solution)/shard_map/all_to_all | solution.py:275
  119.5 13.7 %all-to-all-done.1 = f32[64,8,128]{2,1,0:T(8,128)S(1)} async-done(((f32[64,8,128]{2,1,0:T(8,128)}), f32[64,8,128]{2,1,0:T(8,128)S(1)}, u32[]{:S(2)}, u32[]{:S(2)}) %all-to-all-start.1) | async-done | bytes 262176 | tf_op jit(solution)/shard_map/all_to_all | solution.py:275
  133.2 0.1 multiply_reduce_fusion
  133.3 0.6 copy.12
  (6 shorter events, 0.1 us)
Async XLA Ops:
  0.6 0.9 copy-start
  1.6 0.7 copy-start.1
  3.1 23.7 %all-to-all-start = ((f32[16,6,8,128]{3,2,1,0:T(8,128)}), f32[16,6,8,128]{3,2,1,0:T(8,128)S(1)}, u32[]{:S(2)}, u32[]{:S(2)}) async-start(f32[16,6,8,128]{3,2,1,0:T(8,128)} %bitcast.5), calls=%async_computation | async-start | bytes 786432 | tf_op jit(solution)/shard_map/all_to_all | solution.py:249
  14.7 0.7 copy-start.3
  26.8 23.3 %collective-permute-start = (f32[4,3,8,128]{3,2,1,0:T(8,128)S(1)}, f32[4,3,8,128]{3,2,1,0:T(8,128)S(1)}, u32[]{:S(2)}, u32[]{:S(2)}) collective-permute-start(f32[4,3,8,128]{3,2,1,0:T(8,128)S(1)} %get-tuple-element.23), channel_id=1, source_target_pairs={{0,1},{1,2},{2,3},{4,5},{5,6},{6,7},{8,9},{9,10},{10,11},{12,13},{... | collective-permute-start | bytes 147464 | tf_op jit(solution)/shard_map/ppermute | solution.py:239
  32.9 17.2 %collective-permute-start.1 = (f32[4,3,8,128]{3,2,1,0:T(8,128)S(1)}, f32[4,3,8,128]{3,2,1,0:T(8,128)S(1)}, u32[]{:S(2)}, u32[]{:S(2)}) collective-permute-start(f32[4,3,8,128]{3,2,1,0:T(8,128)S(1)} %get-tuple-element.22), channel_id=1, source_target_pairs={{1,0},{2,1},{3,2},{5,4},{6,5},{7,6},{9,8},{10,9},{11,10},{13,12},{... | collective-permute-start | bytes 147464 | tf_op jit(solution)/shard_map/ppermute | solution.py:239
  66.8 20.8 %collective-permute-start.2 = (f32[4,3,8,128]{3,2,1,0:T(8,128)S(1)}, f32[4,3,8,128]{3,2,1,0:T(8,128)S(1)}, u32[]{:S(2)}, u32[]{:S(2)}) collective-permute-start(f32[4,3,8,128]{3,2,1,0:T(8,128)S(1)} %get-tuple-element.9), channel_id=1, source_target_pairs={{0,1},{1,2},{2,3},{4,5},{5,6},{6,7},{8,9},{9,10},{10,11},{12,13},{... | collective-permute-start | bytes 147464 | tf_op jit(solution)/shard_map/ppermute | solution.py:239
  70.5 17.2 %collective-permute-start.3 = (f32[4,3,8,128]{3,2,1,0:T(8,128)S(1)}, f32[4,3,8,128]{3,2,1,0:T(8,128)S(1)}, u32[]{:S(2)}, u32[]{:S(2)}) collective-permute-start(f32[4,3,8,128]{3,2,1,0:T(8,128)S(1)} %get-tuple-element.10), channel_id=1, source_target_pairs={{1,0},{2,1},{3,2},{5,4},{6,5},{7,6},{9,8},{10,9},{11,10},{13,12},{... | collective-permute-start | bytes 147464 | tf_op jit(solution)/shard_map/ppermute | solution.py:239
  72.4 15.3 %copy-start.2 = (s32[128,16]{0,1:T(8,128)S(1)}, s32[128,16]{0,1:T(8,128)}, u32[]{:S(2)}) copy-start(s32[128,16]{0,1:T(8,128)} %param.7) | copy-start | bytes 24580
  105.8 2.2 %collective-permute-start.4 = (f32[8,128]{1,0:T(8,128)S(1)}, f32[8,128]{1,0:T(8,128)S(1)}, u32[]{:S(2)}, u32[]{:S(2)}) collective-permute-start(f32[8,128]{1,0:T(8,128)S(1)} %get-tuple-element.13), channel_id=1, source_target_pairs={{0,1},{1,0},{2,3},{3,2},{4,5},{5,4},{6,7},{7,6},{8,9},{9,8},{10,11... | collective-permute-start | bytes 12296 | tf_op jit(solution)/shard_map/ppermute | solution.py:273
  105.9 2.8 %collective-permute-start.5 = (f32[8,128]{1,0:T(8,128)S(1)}, f32[8,128]{1,0:T(8,128)S(1)}, u32[]{:S(2)}, u32[]{:S(2)}) collective-permute-start(f32[8,128]{1,0:T(8,128)S(1)} %get-tuple-element.13), channel_id=1, source_target_pairs={{0,2},{1,3},{2,0},{3,1},{4,6},{5,7},{6,4},{7,5},{8,10},{9,11},{10,... | collective-permute-start | bytes 12296 | tf_op jit(solution)/shard_map/ppermute | solution.py:273
  107.8 3.0 %collective-permute-start.6 = (f32[8,128]{1,0:T(8,128)S(1)}, f32[8,128]{1,0:T(8,128)S(1)}, u32[]{:S(2)}, u32[]{:S(2)}) collective-permute-start(f32[8,128]{1,0:T(8,128)S(1)} %get-tuple-element.13), channel_id=1, source_target_pairs={{0,3},{1,2},{2,1},{3,0},{4,7},{5,6},{6,5},{7,4},{8,11},{9,10},{10,... | collective-permute-start | bytes 12296 | tf_op jit(solution)/shard_map/ppermute | solution.py:273
  111.5 21.6 %all-to-all-start.1 = ((f32[64,8,128]{2,1,0:T(8,128)}), f32[64,8,128]{2,1,0:T(8,128)S(1)}, u32[]{:S(2)}, u32[]{:S(2)}) async-start(f32[64,8,128]{2,1,0:T(8,128)} %broadcast_in_dim.24), calls=%async_computation.1 | async-start | bytes 524288 | tf_op jit(solution)/shard_map/all_to_all | solution.py:275

commit v2 on v1

--- a/solution.py
+++ b/solution.py
@@ -46,8 +46,7 @@
         + [p[1] for p in parts] + [zero] * 5,
     )
     for t in range(ROWS):
-        table = rows_q[pl.ds(t, 32, stride=ROWS), :]
-        columns[first + t] = table.T.astype(BF16)
+        columns[first + t] = rows_q[pl.ds(t, 32, stride=ROWS), :].astype(BF16)
         values[first + t] = rows_v[pl.ds(t, 16, stride=ROWS), :].astype(BF16)
 
 
@@ -69,15 +68,22 @@
         others = [tile + halo_tiles, pairs[tile, 0], pairs[tile, 1]]
         others = [e - shift for e in others]
         p_side = rows_p[pl.ds(t, 32, stride=ROWS), :].astype(BF16)
-        q_side = jnp.concatenate([columns[e] for e in others], axis=0)
-        overlap = jnp.maximum(jnp.dot(q_side, p_side, preferred_element_type=F32), 0.0)
+        q_side = jnp.concatenate([columns[e] for e in others], axis=1)
+        overlap = jnp.maximum(
+            lax.dot_general(
+                q_side, p_side, (((0,), (0,)), ((), ())), preferred_element_type=F32
+            ),
+            0.0,
+        )
         weight = overlap * overlap
         high = weight.astype(BF16)
         low = (weight - high.astype(F32)).astype(BF16)
         q_values = jnp.concatenate([values[e] for e in others], axis=1)
         sums[t * 16:(t + 1) * 16, :] = jnp.dot(
-            q_values, high, preferred_element_type=F32
-        ) + jnp.dot(q_values, low, preferred_element_type=F32)
+            jnp.concatenate([q_values] * 2, axis=1),
+            jnp.concatenate([high, low], axis=0),
+            preferred_element_type=F32,
+        )
     row = lambda r: sums[pl.ds(r, ROWS, stride=16), :]
     total = row(3)
     return [
@@ -90,8 +96,7 @@
     def _(s):
         build_group([field_ref[s, c] for c in range(3)], rows_q, rows_v, columns, values, s * ROWS)
 
-    @pl.loop(0, 8)
-    def _(s):
+    for s in range(8):
         field = [field_ref[s + 4, c] for c in range(3)]
         force = group_forces(
             field, (s + 4) * ROWS, HALO // LANES, pairs, rows_p, sums, columns, values
@@ -109,9 +114,7 @@
                 [ref[s, c] for c in range(3)], rows_q, rows_v, columns, values, (first + s) * ROWS
             )
 
-    @pl.loop(0, 8)
-    def _(step):
-        s = jnp.where(step < 4, step, step + 8)
+    for s in (0, 1, 2, 3, 12, 13, 14, 15):
         field = [field_ref[s, c] for c in range(3)]
         force = group_forces(field, s * ROWS, 0, pairs, rows_p, sums, columns, values)
         for c in range(3):
@@ -133,8 +136,7 @@
         pairs, field_ref, low_ref, high_ref, rows_q, rows_v, rows_p, sums, columns, values, step
     )
 
-    @pl.loop(0, 8)
-    def _(s):
+    for s in range(8):
         for c in range(3):
             step(s + 4, c, inner_ref[s, c])
 
@@ -148,7 +150,7 @@
     rows_q, rows_v, rows_p, sums, columns, values,
 ):
     def step(s, c, force):
-        final_ref[c, pl.ds(pl.multiple_of(s * ROWS, ROWS), ROWS), :] = (
+        final_ref[c, pl.ds(s * ROWS, ROWS), :] = (
             base_ref[s, c] + (time_step * time_step) * force
         )
 
@@ -156,8 +158,7 @@
         pairs, field_ref, low_ref, high_ref, rows_q, rows_v, rows_p, sums, columns, values, step
     )
 
-    @pl.loop(0, 8)
-    def _(s):
+    for s in range(8):
         for c in range(3):
             step(s + 4, c, inner_ref[s, c])
 
@@ -178,12 +179,10 @@
             moving, jnp.concatenate([chosen] * 3, axis=0), preferred_element_type=F32
         )
         total = total + found * jnp.concatenate([here] * 3, axis=0)
-    zero = jnp.zeros((1, LANES), F32)
-    part_ref[...] = jnp.concatenate(
-        [jnp.sum(total[c * LANES:(c + 1) * LANES], axis=0, keepdims=True) for c in range(3)]
-        + [zero] * 5,
-        axis=0,
-    )
+    for c in range(3):
+        part_ref[:, c * LANES:(c + 1) * LANES] = jnp.sum(
+            total[c * LANES:(c + 1) * LANES], axis=0, keepdims=True
+        )
 
 
 def pack_kernel(vel_ref, conf_ref, out_ref):
@@ -207,7 +206,7 @@
         pltpu.VMEM((16 * ROWS, LANES), F32),
         pltpu.VMEM((32 * ROWS, LANES), F32),
         pltpu.VMEM((16 * ROWS, LANES), F32),
-        pltpu.VMEM((tiles, LANES, 32), BF16),
+        pltpu.VMEM((tiles, 32, LANES), BF16),
         pltpu.VMEM((tiles, 16, LANES), BF16),
     ]
 
@@ -263,7 +262,7 @@
     low, high = rims(rim_low, rim_high)
     inside = inner(partners, middle)
     final, part = call(
-        second_rim_kernel, "second_rim", (shape(3, LANES, LANES), shape(ROWS, LANES)),
+        second_rim_kernel, "second_rim", (shape(3, LANES, LANES), shape(1, 3 * LANES)),
         [SMEM, SMEM] + [VMEM] * 6, scratch(192), WORK, 0,
     )(partners, domain, groups, middle, low, high, inside, base)
     final_positions = final.reshape(1, 1, 3, 1, LANES * LANES)
@@ -273,17 +272,17 @@
         here = here + lax.ppermute(part, "domain", [(i, i ^ offset) for i in range(4)])
     images, members = lax.axis_size("image"), lax.axis_size("swarm")
     everyone = lax.all_to_all(
-        jnp.broadcast_to(here[None], (images * members, ROWS, LANES)),
+        jnp.broadcast_to(here[None], (images * members, 1, 3 * LANES)),
         ("image", "swarm"), split_axis=0, concat_axis=0, tiled=True,
     )
-    updated = jnp.sum(everyone.reshape(images, members, ROWS, LANES), axis=1) / (members * GSIZE)
+    updated = jnp.sum(everyone.reshape(images, members, 3 * LANES), axis=1) / (members * GSIZE)
     place = lax.axis_index("image")
     ids = jnp.arange(images)
     neighbours = (place > 0).astype(F32) + (place < images - 1).astype(F32)
     share = jnp.where(jnp.abs(ids - place) == 1, smoothing, 0.0) + jnp.where(
         ids == place, 1.0 - smoothing * neighbours, 0.0
     )
-    new_string = jnp.sum(share[:, None, None] * updated, axis=0)[None, :3]
+    new_string = jnp.sum(share[:, None] * updated, axis=0).reshape(1, 3, LANES)
     return (final_positions, new_string)
 
 

time: 134 us -> 94.1 us (0.70)
  Pallas kernels: 66.1 us -> 27.6 us
  waiting for transfers between devices: 27.8 us -> 25.8 us
    pallas_call x1, Pallas kernels: 16.7 us -> 6.46 us  [on_device(): call(first_rim_kernel, 'first_rim', (whole, whole, rim, rim), [SMEM] + [V...]
    pallas_call x1, Pallas kernels: 18.1 us -> 8.26 us  [on_device(): call(second_rim_kernel, 'second_rim', (shape(3, LANES, LANES), shape(1, 3...]
    pallas_call x1, Pallas kernels: 15.2 us -> 6.04 us  [on_device(): inside = inner(partners, start_pos)]
    pallas_call x1, Pallas kernels: 15.2 us -> 6.04 us  [on_device(): inside = inner(partners, middle)]
    all_to_all x1, waiting for transfers between devices: 13.7 us -> 11.8 us  [on_device(): lax.all_to_all(jnp.broadcast_to(here[None], (images * members, 1, 3 * LAN...]
  transfers between devices with their start and end apart: 9 -> 9, of which waited for: 4 -> 4; matrix products, arithmetic and copies ran while one was open for 0% -> 0% of each run, Pallas kernels for 23% -> 13%
where the time goes in v2:
time: 94.1 us; the launch traced here: 93.6 us
  starting transfers between devices  35.5 us (38%)
  Pallas kernels  27.6 us (29%)
  waiting for transfers between devices  25.8 us (27%)
  local copies, waits for them, and re-layouts  3.73 us (4%)
    all_to_all x1, waiting for transfers between devices, on_device(): lax.all_to_all(jnp.broadcast_to(here[None], (images * members, 1, 3 * LAN...  11.8 us
    all_to_all x1, starting transfers between devices, on_device(): lax.all_to_all(packed.reshape(16, 6, ROWS, LANES), 'swarm', split_axis=0,...  11.6 us
    all_to_all x1, waiting for transfers between devices, on_device(): lax.all_to_all(packed.reshape(16, 6, ROWS, LANES), 'swarm', split_axis=0,...  11.3 us
    ppermute x2, starting transfers between devices, rims(): lax.ppermute(high, 'domain', forward)  9.73 us
    pallas_call x1, Pallas kernels, on_device(): call(second_rim_kernel, 'second_rim', (shape(3, LANES, LANES), shape(1, 3...  8.26 us
    all_to_all x1, starting transfers between devices, on_device(): lax.all_to_all(jnp.broadcast_to(here[None], (images * members, 1, 3 * LAN...  7.92 us
    pallas_call x1, Pallas kernels, on_device(): call(first_rim_kernel, 'first_rim', (whole, whole, rim, rim), [SMEM] + [V...  6.46 us
    pallas_call x1, Pallas kernels, on_device(): inside = inner(partners, middle)  6.04 us
  transfers between devices with their start and end apart: 9, of which 4 were waited for; matrix products, arithmetic and copies ran while one was open for 0% of the time, Pallas kernels for 13%

profile of v2, /device:TPU:1, one launch (start us, length us, event | category | flops | bytes accessed | tf_op | source)
XLA Modules:
  0.0 93.6 jit_solution(14418745332866989251)
XLA Ops:
  0.6 0.0 copy-start
  0.6 0.9 copy-done
  1.6 0.0 copy-start.1
  1.6 0.7 copy-done.1
  2.3 0.8 pack.1
  3.1 11.6 %all-to-all-start = ((f32[16,6,8,128]{3,2,1,0:T(8,128)}), f32[16,6,8,128]{3,2,1,0:T(8,128)S(1)}, u32[]{:S(2)}, u32[]{:S(2)}) async-start(f32[16,6,8,128]{3,2,1,0:T(8,128)} %bitcast.5), calls=%async_computation | async-start | bytes 786432 | tf_op jit(solution)/shard_map/all_to_all | solution.py:248
  14.7 0.0 copy-start.3
  14.7 0.7 copy-done.3
  15.4 0.1 copy.12
  15.5 11.3 %all-to-all-done = f32[16,6,8,128]{3,2,1,0:T(8,128)S(1)} async-done(((f32[16,6,8,128]{3,2,1,0:T(8,128)}), f32[16,6,8,128]{3,2,1,0:T(8,128)S(1)}, u32[]{:S(2)}, u32[]{:S(2)}) %all-to-all-start) | async-done | bytes 393248 | tf_op jit(solution)/shard_map/all_to_all | solution.py:248
  26.8 6.1 %collective-permute-start = (f32[4,3,8,128]{3,2,1,0:T(8,128)S(1)}, f32[4,3,8,128]{3,2,1,0:T(8,128)S(1)}, u32[]{:S(2)}, u32[]{:S(2)}) collective-permute-start(f32[4,3,8,128]{3,2,1,0:T(8,128)S(1)} %get-tuple-element.25), channel_id=1, source_target_pairs={{0,1},{1,2},{2,3},{4,5},{5,6},{6,7},{8,9},{9,10},{10,11},{12,13},{... | collective-permute-start | bytes 147464 | tf_op jit(solution)/shard_map/ppermute | solution.py:238
  32.9 1.9 %collective-permute-start.1 = (f32[4,3,8,128]{3,2,1,0:T(8,128)S(1)}, f32[4,3,8,128]{3,2,1,0:T(8,128)S(1)}, u32[]{:S(2)}, u32[]{:S(2)}) collective-permute-start(f32[4,3,8,128]{3,2,1,0:T(8,128)S(1)} %get-tuple-element.24), channel_id=1, source_target_pairs={{1,0},{2,1},{3,2},{5,4},{6,5},{7,6},{9,8},{10,9},{11,10},{13,12},{... | collective-permute-start | bytes 147464 | tf_op jit(solution)/shard_map/ppermute | solution.py:238
  34.9 6.0 %inner.2.inner_ref = f32[8,3,8,128]{3,2,1,0:T(8,128)S(1)} custom-call(s32[128,2]{1,0:T(8,128)S(1)} %bitcast.9, f32[16,3,8,128]{3,2,1,0:T(8,128)S(1)} %get-tuple-element.23.field_ref), custom_call_target="tpu_custom_call" | custom-call | flops 8000000000 | tf_op jit(solution)/shard_map/inner/pallas_call | solution.py:255
  40.9 0.0 collective-permute-done.low_ref
  40.9 0.0 collective-permute-done.1.high_ref
  40.9 6.5 %first_rim.1 = (f32[16,3,8,128]{3,2,1,0:T(8,128)S(1)}, f32[16,3,8,128]{3,2,1,0:T(8,128)S(1)}, f32[4,3,8,128]{3,2,1,0:T(8,128)S(1)}, f32[4,3,8,128]{3,2,1,0:T(8,128)S(1)}) custom-call(s32[128,2]{1,0:T(8,128)S(1)} %bitcast.10, f32[16,3,8,128]{3,2,1,0:T(8,128)S(1)} %get-tuple-element.23.field_ref, f32[4,3,8,128]{3,2,1,0:T(8,128)S(1)} %collective-permute-done.low_ref, ...), custom_call_target="tpu_custom_call" | custom-call | flops 8000000000 | tf_op jit(solution)/shard_map/first_rim/pallas_call | solution.py:257
  47.4 3.6 %collective-permute-start.2 = (f32[4,3,8,128]{3,2,1,0:T(8,128)S(1)}, f32[4,3,8,128]{3,2,1,0:T(8,128)S(1)}, u32[]{:S(2)}, u32[]{:S(2)}) collective-permute-start(f32[4,3,8,128]{3,2,1,0:T(8,128)S(1)} %get-tuple-element.9), channel_id=1, source_target_pairs={{0,1},{1,2},{2,3},{4,5},{5,6},{6,7},{8,9},{9,10},{10,11},{12,13},{... | collective-permute-start | bytes 147464 | tf_op jit(solution)/shard_map/ppermute | solution.py:238
  51.1 2.1 %collective-permute-start.3 = (f32[4,3,8,128]{3,2,1,0:T(8,128)S(1)}, f32[4,3,8,128]{3,2,1,0:T(8,128)S(1)}, u32[]{:S(2)}, u32[]{:S(2)}) collective-permute-start(f32[4,3,8,128]{3,2,1,0:T(8,128)S(1)} %get-tuple-element.10), channel_id=1, source_target_pairs={{1,0},{2,1},{3,2},{5,4},{6,5},{7,6},{9,8},{10,9},{11,10},{13,12},{... | collective-permute-start | bytes 147464 | tf_op jit(solution)/shard_map/ppermute | solution.py:238
  53.2 0.0 copy-start.2
  53.2 6.0 %inner.3.inner_ref = f32[8,3,8,128]{3,2,1,0:T(8,128)S(1)} custom-call(s32[128,2]{1,0:T(8,128)S(1)} %bitcast.11, f32[16,3,8,128]{3,2,1,0:T(8,128)S(1)} %get-tuple-element.8.field_ref), custom_call_target="tpu_custom_call" | custom-call | flops 8000000000 | tf_op jit(solution)/shard_map/inner/pallas_call | solution.py:263
  59.2 0.0 collective-permute-done.2.low_ref
  59.2 0.0 collective-permute-done.3.high_ref
  59.3 0.0 copy-done.2
  59.3 8.3 %second_rim.1 = (f32[3,128,128]{2,1,0:T(8,128)}, f32[1,384]{1,0:T(1,128)S(1)}) custom-call(s32[128,2]{1,0:T(8,128)S(1)} %bitcast.12, s32[1]{0:T(128)} %bitcast.1.domain_ref, s32[16,128]{1,0:T(8,128)S(1)} %bitcast.14, f32[16,3,8,128]{3,2,1,0:T(8,128)S(1)} %get-tuple-element.8.field_ref, f32[4,3,8,128]{3,2,1,0:T(8,128)S(1)} %collective-permute-done.2.low_ref, ...), custom_call_target="tpu_custom_call" | custom-call | flops 8000000000 | tf_op jit(solution)/shard_map/second_rim/pallas_call | solution.py:264
  67.5 0.1 collective-permute-start.4
  67.6 1.9 %collective-permute-start.5 = (f32[1,384]{1,0:T(1,128)S(1)}, f32[1,384]{1,0:T(1,128)S(1)}, u32[]{:S(2)}, u32[]{:S(2)}) collective-permute-start(f32[1,384]{1,0:T(1,128)S(1)} %get-tuple-element.13), channel_id=1, source_target_pairs={{0,2},{1,3},{2,0},{3,1},{4,6},{5,7},{6,4},{7,5},{8,10},{9,11},{10,... | collective-permute-start | bytes 4616 | tf_op jit(solution)/shard_map/ppermute | solution.py:272
  69.5 0.3 collective-permute-start.6
  69.8 0.0 collective-permute-done.4
  69.8 0.7 collective-permute-done.5
  70.4 2.1 %collective-permute-done.6 = f32[1,384]{1,0:T(1,128)S(1)} collective-permute-done((f32[1,384]{1,0:T(1,128)S(1)}, f32[1,384]{1,0:T(1,128)S(1)}, u32[]{:S(2)}, u32[]{:S(2)}) %collective-permute-start.6) | collective-permute-done | bytes 1568 | tf_op jit(solution)/shard_map/ppermute | solution.py:272
  72.5 0.7 broadcast_in_dim.24
  73.2 7.9 %all-to-all-start.1 = ((f32[64,1,384]{2,1,0:T(1,128)}), f32[64,1,384]{2,1,0:T(1,128)S(1)}, u32[]{:S(2)}, u32[]{:S(2)}) async-start(f32[64,1,384]{2,1,0:T(1,128)} %broadcast_in_dim.24), calls=%async_computation.1 | async-start | bytes 196608 | tf_op jit(solution)/shard_map/all_to_all | solution.py:274
  81.2 11.8 %all-to-all-done.1 = f32[64,1,384]{2,1,0:T(1,128)S(1)} async-done(((f32[64,1,384]{2,1,0:T(1,128)}), f32[64,1,384]{2,1,0:T(1,128)S(1)}, u32[]{:S(2)}, u32[]{:S(2)}) %all-to-all-start.1) | async-done | bytes 98336 | tf_op jit(solution)/shard_map/all_to_all | solution.py:274
  93.0 0.1 multiply_reduce_fusion
  93.0 0.6 reshape.45
  (6 shorter events, 0.1 us)
Async XLA Ops:
  0.6 0.9 copy-start
  1.6 0.7 copy-start.1
  3.1 23.7 %all-to-all-start = ((f32[16,6,8,128]{3,2,1,0:T(8,128)}), f32[16,6,8,128]{3,2,1,0:T(8,128)S(1)}, u32[]{:S(2)}, u32[]{:S(2)}) async-start(f32[16,6,8,128]{3,2,1,0:T(8,128)} %bitcast.5), calls=%async_computation | async-start | bytes 786432 | tf_op jit(solution)/shard_map/all_to_all | solution.py:248
  14.7 0.7 copy-start.3
  26.8 14.1 %collective-permute-start = (f32[4,3,8,128]{3,2,1,0:T(8,128)S(1)}, f32[4,3,8,128]{3,2,1,0:T(8,128)S(1)}, u32[]{:S(2)}, u32[]{:S(2)}) collective-permute-start(f32[4,3,8,128]{3,2,1,0:T(8,128)S(1)} %get-tuple-element.25), channel_id=1, source_target_pairs={{0,1},{1,2},{2,3},{4,5},{5,6},{6,7},{8,9},{9,10},{10,11},{12,13},{... | collective-permute-start | bytes 147464 | tf_op jit(solution)/shard_map/ppermute | solution.py:238
  32.9 8.0 %collective-permute-start.1 = (f32[4,3,8,128]{3,2,1,0:T(8,128)S(1)}, f32[4,3,8,128]{3,2,1,0:T(8,128)S(1)}, u32[]{:S(2)}, u32[]{:S(2)}) collective-permute-start(f32[4,3,8,128]{3,2,1,0:T(8,128)S(1)} %get-tuple-element.24), channel_id=1, source_target_pairs={{1,0},{2,1},{3,2},{5,4},{6,5},{7,6},{9,8},{10,9},{11,10},{13,12},{... | collective-permute-start | bytes 147464 | tf_op jit(solution)/shard_map/ppermute | solution.py:238
  47.4 11.8 %collective-permute-start.2 = (f32[4,3,8,128]{3,2,1,0:T(8,128)S(1)}, f32[4,3,8,128]{3,2,1,0:T(8,128)S(1)}, u32[]{:S(2)}, u32[]{:S(2)}) collective-permute-start(f32[4,3,8,128]{3,2,1,0:T(8,128)S(1)} %get-tuple-element.9), channel_id=1, source_target_pairs={{0,1},{1,2},{2,3},{4,5},{5,6},{6,7},{8,9},{9,10},{10,11},{12,13},{... | collective-permute-start | bytes 147464 | tf_op jit(solution)/shard_map/ppermute | solution.py:238
  51.1 8.2 %collective-permute-start.3 = (f32[4,3,8,128]{3,2,1,0:T(8,128)S(1)}, f32[4,3,8,128]{3,2,1,0:T(8,128)S(1)}, u32[]{:S(2)}, u32[]{:S(2)}) collective-permute-start(f32[4,3,8,128]{3,2,1,0:T(8,128)S(1)} %get-tuple-element.10), channel_id=1, source_target_pairs={{1,0},{2,1},{3,2},{5,4},{6,5},{7,6},{9,8},{10,9},{11,10},{13,12},{... | collective-permute-start | bytes 147464 | tf_op jit(solution)/shard_map/ppermute | solution.py:238
  53.2 6.1 %copy-start.2 = (s32[128,16]{0,1:T(8,128)S(1)}, s32[128,16]{0,1:T(8,128)}, u32[]{:S(2)}) copy-start(s32[128,16]{0,1:T(8,128)} %param.7) | copy-start | bytes 24580
  67.5 2.2 %collective-permute-start.4 = (f32[1,384]{1,0:T(1,128)S(1)}, f32[1,384]{1,0:T(1,128)S(1)}, u32[]{:S(2)}, u32[]{:S(2)}) collective-permute-start(f32[1,384]{1,0:T(1,128)S(1)} %get-tuple-element.13), channel_id=1, source_target_pairs={{0,1},{1,0},{2,3},{3,2},{4,5},{5,4},{6,7},{7,6},{8,9},{9,8},{10,11... | collective-permute-start | bytes 4616 | tf_op jit(solution)/shard_map/ppermute | solution.py:272
  67.6 2.8 %collective-permute-start.5 = (f32[1,384]{1,0:T(1,128)S(1)}, f32[1,384]{1,0:T(1,128)S(1)}, u32[]{:S(2)}, u32[]{:S(2)}) collective-permute-start(f32[1,384]{1,0:T(1,128)S(1)} %get-tuple-element.13), channel_id=1, source_target_pairs={{0,2},{1,3},{2,0},{3,1},{4,6},{5,7},{6,4},{7,5},{8,10},{9,11},{10,... | collective-permute-start | bytes 4616 | tf_op jit(solution)/shard_map/ppermute | solution.py:272
  69.5 3.0 %collective-permute-start.6 = (f32[1,384]{1,0:T(1,128)S(1)}, f32[1,384]{1,0:T(1,128)S(1)}, u32[]{:S(2)}, u32[]{:S(2)}) collective-permute-start(f32[1,384]{1,0:T(1,128)S(1)} %get-tuple-element.13), channel_id=1, source_target_pairs={{0,3},{1,2},{2,1},{3,0},{4,7},{5,6},{6,5},{7,4},{8,11},{9,10},{10,... | collective-permute-start | bytes 4616 | tf_op jit(solution)/shard_map/ppermute | solution.py:272
  73.2 19.7 %all-to-all-start.1 = ((f32[64,1,384]{2,1,0:T(1,128)}), f32[64,1,384]{2,1,0:T(1,128)S(1)}, u32[]{:S(2)}, u32[]{:S(2)}) async-start(f32[64,1,384]{2,1,0:T(1,128)} %broadcast_in_dim.24), calls=%async_computation.1 | async-start | bytes 196608 | tf_op jit(solution)/shard_map/all_to_all | solution.py:274

commit v3 on v2

v3 whole, which is shorter than its diff:
```python
import functools

import jax
import jax.numpy as jnp
from jax import lax
from jax.experimental import pallas as pl
from jax.experimental.pallas import tpu as pltpu
from jax.sharding import PartitionSpec as P

HALO = 4096
GSIZE = 16
LANES = 128
ROWS = 8

time_step = 0.25
strength = 0.1
smoothing = 0.25

F32 = jnp.float32
BF16 = jnp.bfloat16


def three_parts(value):
    high = value.astype(BF16).astype(F32)
    rest = value - high
    middle = rest.astype(BF16).astype(F32)
    return high, middle, rest - middle


def two_parts(value):
    high = value.astype(BF16)
    return high, (value - high.astype(F32)).astype(BF16)


def put_rows(ref, rows):
    for place, row in enumerate(rows):
        ref[place * ROWS:(place + 1) * ROWS, :] = row


def build_group(field, rows_q, rows_v, columns, values, first):
    one, zero = jnp.ones((ROWS, LANES), F32), jnp.zeros((ROWS, LANES), F32)
    parts = [three_parts(x) for x in field]
    norm = three_parts(0.5 - 0.5 * (field[0] * field[0] + field[1] * field[1] + field[2] * field[2]))
    of_q = []
    for h, m, l in parts:
        of_q += [h, m, h, m, l, h]
    put_rows(rows_q, of_q + [one] * 3 + list(norm) + [zero] * 8)
    put_rows(
        rows_v,
        [p[0] for p in parts] + [one] + [p[2] for p in parts] + [zero]
        + [p[1] for p in parts] + [zero] * 5,
    )
    for t in range(ROWS):
        columns[first + t] = rows_q[pl.ds(t, 32, stride=ROWS), :].astype(BF16)
        values[first + t] = rows_v[pl.ds(t, 16, stride=ROWS), :].astype(BF16)


def own_rows(field, rows_p):
    one, zero = jnp.ones((ROWS, LANES), F32), jnp.zeros((ROWS, LANES), F32)
    norm = three_parts(0.5 - 0.5 * (field[0] * field[0] + field[1] * field[1] + field[2] * field[2]))
    of_p = []
    for x in field:
        h, m, l = three_parts(x)
        of_p += [h, h, m, m, h, l]
    put_rows(rows_p, of_p + list(norm) + [one] * 3 + [zero] * 8)


def group_forces(field, tile0, shift, pairs, rows_p, sums, columns, values):
    own_rows(field, rows_p)
    halo_tiles = HALO // LANES
    for t in range(ROWS):
        tile = tile0 + t
        others = [tile + halo_tiles, pairs[tile, 0], pairs[tile, 1]]
        others = [e - shift for e in others]
        p_side = rows_p[pl.ds(t, 32, stride=ROWS), :].astype(BF16)
        q_side = jnp.concatenate([columns[e] for e in others], axis=1)
        overlap = jnp.maximum(
            lax.dot_general(
                q_side, p_side, (((0,), (0,)), ((), ())), preferred_element_type=F32
            ),
            0.0,
        )
        weight = overlap * overlap
        high, low = two_parts(weight)
        q_values = jnp.concatenate([values[e] for e in others], axis=1)
        sums[t * 16:(t + 1) * 16, :] = jnp.dot(
            jnp.concatenate([q_values] * 2, axis=1),
            jnp.concatenate([high, low], axis=0),
            preferred_element_type=F32,
        )
    row = lambda r: sums[pl.ds(r, ROWS, stride=16), :]
    total = row(3)
    return [
        strength * (field[c] * total - (row(c) + row(8 + c) + row(4 + c))) for c in range(3)
    ]


def inner_kernel(pairs, field_ref, out_ref, columns, values, rows_q, rows_v, rows_p, sums):
    @pl.loop(0, 16)
    def _(s):
        build_group([field_ref[s, c] for c in range(3)], rows_q, rows_v, columns, values, s * ROWS)

    for s in range(8):
        field = [field_ref[s + 4, c] for c in range(3)]
        force = group_forces(
            field, (s + 4) * ROWS, HALO // LANES, pairs, rows_p, sums, columns, values
        )
        for c in range(3):
            out_ref[s, c] = force[c]


def rim_forces(
    pairs, place, field_ref, rim_refs, own_tables, rows_q, rows_v, rows_p, sums, columns, values, emit
):
    @pl.loop(0, 16)
    def _(s):
        for whole, own in ((columns, own_tables[0]), (values, own_tables[1])):
            whole[pl.ds(HALO // LANES + s * ROWS, ROWS)] = own[pl.ds(s * ROWS, ROWS)]

    odd = place[1]
    for ref, first in ((rim_refs[0], 20 * (1 - odd)), (rim_refs[1], 20 * odd)):

        @pl.loop(0, 4)
        def _(s):
            build_group(
                [ref[s, c] for c in range(3)], rows_q, rows_v, columns, values, (first + s) * ROWS
            )

    for s in (0, 1, 2, 3, 12, 13, 14, 15):
        field = [field_ref[s, c] for c in range(3)]
        force = group_forces(field, s * ROWS, 0, pairs, rows_p, sums, columns, values)
        for c in range(3):
            emit(s, c, force[c])


def first_rim_kernel(
    pairs, place, field_ref, rim1_ref, rim2_ref, inner_ref, columns_ref, values_ref, vel_ref,
    middle_ref, base_ref, send1_ref, send2_ref,
    rows_q, rows_v, rows_p, sums, columns, values,
):
    def step(s, c, force):
        velocity = vel_ref[s, c] + time_step * force
        middle = field_ref[s, c] + time_step * velocity
        middle_ref[s, c] = middle
        base_ref[s, c] = middle + time_step * velocity

    rim_forces(
        pairs, place, field_ref, (rim1_ref, rim2_ref), (columns_ref, values_ref),
        rows_q, rows_v, rows_p, sums, columns, values, step,
    )
    for s in range(8):
        for c in range(3):
            step(s + 4, c, inner_ref[s, c])

    odd = place[1]
    send1_ref[...] = middle_ref[pl.ds(12 * (1 - odd), 4)]
    send2_ref[...] = middle_ref[pl.ds(12 * odd, 4)]


def second_rim_kernel(
    pairs, place, groups_ref, field_ref, rim1_ref, rim2_ref, inner_ref, columns_ref, values_ref,
    base_ref, final_ref, part_ref,
    rows_q, rows_v, rows_p, sums, columns, values,
):
    def step(s, c, force):
        final_ref[c, pl.ds(s * ROWS, ROWS), :] = (
            base_ref[s, c] + (time_step * time_step) * force
        )

    rim_forces(
        pairs, place, field_ref, (rim1_ref, rim2_ref), (columns_ref, values_ref),
        rows_q, rows_v, rows_p, sums, columns, values, step,
    )
    for s in range(8):
        for c in range(3):
            step(s + 4, c, inner_ref[s, c])

    local = groups_ref[...] - place[0] * (LANES * LANES)
    tile_of, lane_of = local >> 7, local & 127
    moving = jnp.concatenate(
        [jnp.concatenate(two_parts(final_ref[c].T), axis=1) for c in range(3)], axis=0
    )
    down = lax.broadcasted_iota(jnp.int32, (LANES, LANES), 0)
    total = jnp.zeros((3, ROWS, 2 * LANES), F32)
    for g in range(0, GSIZE, 2):
        pair = lambda rows: jnp.concatenate([down == rows[g + i:g + i + 1, :] for i in (0, 1)], axis=1)
        chosen = pair(tile_of).astype(F32).astype(BF16)
        here = pair(lane_of)
        found = jnp.dot(
            moving, jnp.concatenate([chosen] * 2, axis=0), preferred_element_type=F32
        )
        kept = jnp.where(jnp.concatenate([here] * 3, axis=0), found, 0.0)
        total = total + jnp.sum(kept.reshape(3, LANES // ROWS, ROWS, 2 * LANES), axis=1)
    for c in range(3):
        both = total[c, :, :LANES] + total[c, :, LANES:]
        part_ref[:, c * LANES:(c + 1) * LANES] = jnp.sum(both, axis=0, keepdims=True)


def pack_kernel(vel_hbm, conf_hbm, out_ref, vel_ref, conf_ref, arrived):
    vel_copy = pltpu.make_async_copy(vel_hbm, vel_ref, arrived.at[0])
    conf_copy = pltpu.make_async_copy(conf_hbm, conf_ref, arrived.at[1])
    vel_copy.start()
    conf_copy.start()
    conf_copy.wait()
    for c in range(3):
        for m in range(16):
            out_ref[m * 48 + 24 + c * ROWS:m * 48 + 32 + c * ROWS, :] = conf_ref[c]
    vel_copy.wait()
    for c in range(3):
        for j in range(ROWS):
            for half in range(2):
                out_ref[pl.ds(half * 8 * 48 + c * ROWS + j, ROWS, stride=48), :] = vel_ref[
                    c, half * 8:half * 8 + 8, j * LANES:(j + 1) * LANES
                ]


VMEM = pl.BlockSpec(memory_space=pltpu.VMEM)
SMEM = pl.BlockSpec(memory_space=pltpu.SMEM)
ANY = pl.BlockSpec(memory_space=pl.ANY)


ROW_SCRATCH = [
    pltpu.VMEM((32 * ROWS, LANES), F32),
    pltpu.VMEM((16 * ROWS, LANES), F32),
    pltpu.VMEM((32 * ROWS, LANES), F32),
    pltpu.VMEM((16 * ROWS, LANES), F32),
]
TABLES = [pltpu.VMEM((192, 32, LANES), BF16), pltpu.VMEM((192, 16, LANES), BF16)]


def call(kernel, name, out, specs, scratches, flops, moved, vmem=40 * 1024 * 1024):
    return pl.pallas_call(
        kernel,
        out_shape=out,
        in_specs=specs,
        out_specs=jax.tree.map(lambda _: VMEM, out),
        scratch_shapes=scratches,
        compiler_params=pltpu.CompilerParams(vmem_limit_bytes=vmem),
        cost_estimate=pl.CostEstimate(flops=flops, bytes_accessed=moved, transcendentals=0),
        name=name,
    )


WORK = 8_000_000_000


def shape(*dims):
    return jax.ShapeDtypeStruct(dims, F32)


def swap_rims(first, second):
    count = lax.axis_size("domain")
    inside = [(i, i ^ 1) for i in range(count)]
    across = [(i, j) for i in range(count) for j in [i + 1 if i % 2 else i - 1] if 0 <= j < count]
    return lax.ppermute(first, "domain", inside), lax.ppermute(second, "domain", across)


def string_shares():
    images, place = lax.axis_size("image"), lax.axis_index("image")
    ids = jnp.arange(images)
    neighbours = (place > 0).astype(F32) + (place < images - 1).astype(F32)
    return jnp.where(jnp.abs(ids - place) == 1, smoothing, 0.0) + jnp.where(
        ids == place, 1.0 - smoothing * neighbours, 0.0
    )


def on_device(configuration, velocities, pairs, cv_atoms):
    partners = pairs[0]
    groups = cv_atoms.T
    domain = lax.axis_index("domain").astype(jnp.int32)
    odd = domain % 2
    place = jnp.stack([domain, odd])
    packed = call(
        pack_kernel, "pack", shape(16 * 48, LANES), [ANY, ANY],
        [
            pltpu.VMEM((3, 16, 1024), F32),
            pltpu.VMEM((3, ROWS, LANES), F32),
            pltpu.SemaphoreType.DMA((2,)),
        ],
        0, 600_000, 62_900_000,
    )(velocities.reshape(3, 16, 1024), configuration.reshape(3, ROWS, LANES))
    got = lax.all_to_all(
        packed.reshape(16, 6, ROWS, LANES), "swarm", split_axis=0, concat_axis=0, tiled=True
    )
    start_vel, start_pos = got[:, :3], got[:, 3:]

    whole, rim = shape(16, 3, ROWS, LANES), shape(4, 3, ROWS, LANES)
    tables = (
        jax.ShapeDtypeStruct((128, 32, LANES), BF16), jax.ShapeDtypeStruct((128, 16, LANES), BF16)
    )
    inner = call(
        inner_kernel, "inner", (shape(8, 3, ROWS, LANES),) + tables, [SMEM, VMEM], ROW_SCRATCH, WORK, 0
    )
    rim1, rim2 = swap_rims(
        lax.dynamic_slice_in_dim(start_pos, 12 * (1 - odd), 4, 0),
        lax.dynamic_slice_in_dim(start_pos, 12 * odd, 4, 0),
    )
    inside = inner(partners, start_pos)
    middle, base, send1, send2 = call(
        first_rim_kernel, "first_rim", (whole, whole, rim, rim), [SMEM, SMEM] + [VMEM] * 7,
        ROW_SCRATCH + TABLES, WORK, 0,
    )(partners, place, start_pos, rim1, rim2, *inside, start_vel)

    rim1, rim2 = swap_rims(send1, send2)
    inside = inner(partners, middle)
    final, part = call(
        second_rim_kernel, "second_rim", (shape(3, LANES, LANES), shape(1, 3 * LANES)),
        [SMEM, SMEM] + [VMEM] * 8, ROW_SCRATCH + TABLES, WORK, 0,
    )(partners, place, groups, middle, rim1, rim2, *inside, base)
    part, share = lax.optimization_barrier((part, string_shares()))
    final_positions = final.reshape(1, 1, 3, 1, LANES * LANES)

    here = part
    for offset in range(1, 4):
        here = here + lax.ppermute(part, "domain", [(i, i ^ offset) for i in range(4)])
    images, members = lax.axis_size("image"), lax.axis_size("swarm")
    everyone = lax.all_to_all(
        jnp.broadcast_to(here[None], (images * members, 1, 3 * LANES)),
        ("image", "swarm"), split_axis=0, concat_axis=0, tiled=True,
    )
    updated = jnp.sum(everyone.reshape(images, members, 3 * LANES), axis=1) / (members * GSIZE)
    new_string = jnp.sum(share[:, None] * updated, axis=0).reshape(1, 3, LANES)
    return (final_positions, new_string)


def solution(mesh):
    in_specs = (
        P("image", None, "domain", "swarm"),
        P("image", None, "domain", None, "swarm"),
        P("domain", None, None),
        P(),
    )
    out_specs = (P("image", "swarm", None, "domain", None), P("image", None, None))
    return jax.shard_map(
        on_device, mesh=mesh, in_specs=in_specs, out_specs=out_specs, check_vma=False
    )
```

time: 94.1 us -> 86.3 us (0.917)
  starting transfers between devices: 35.5 us -> 30.7 us
  Pallas kernels: 27.6 us -> 26.6 us
  waiting for transfers between devices: 25.8 us -> 24.8 us
  local copies, waits for them, and re-layouts: 3.73 us -> 2.78 us
    ppermute x4, starting transfers between devices: 13.8 us -> 8.86 us  [the longest x2 8.18 us: swap_rims(): lax.ppermute(second, 'domain', across)]
    pallas_call x1, Pallas kernels: 8.26 us -> 6.99 us  [on_device(): call(second_rim_kernel, 'second_rim', (shape(3, LANES, LANES), shape(1, 3...]
    unnamed x10 -> x6, local copies, waits for them, and re-layouts: 2.42 us -> 1.47 us
  transfers between devices with their start and end apart: 9 -> 9, of which waited for: 4 -> 4; matrix products, arithmetic and copies ran while one was open for 0% -> 0% of each run, Pallas kernels for 13% -> 14%
where the time goes in v3:
time: 86.3 us; the launch traced here: 85.9 us
  starting transfers between devices  30.7 us (36%)
  Pallas kernels  26.6 us (31%)
  waiting for transfers between devices  24.8 us (29%)
  local copies, waits for them, and re-layouts  2.78 us (3%)
    all_to_all x1, waiting for transfers between devices, on_device(): lax.all_to_all(jnp.broadcast_to(here[None], (images * members, 1, 3 * LAN...  11.6 us
    all_to_all x1, starting transfers between devices, on_device(): lax.all_to_all(packed.reshape(16, 6, ROWS, LANES), 'swarm', split_axis=0,...  11.6 us
    all_to_all x1, waiting for transfers between devices, on_device(): lax.all_to_all(packed.reshape(16, 6, ROWS, LANES), 'swarm', split_axis=0,...  11.2 us
    ppermute x2, starting transfers between devices, swap_rims(): lax.ppermute(second, 'domain', across)  8.18 us
    all_to_all x1, starting transfers between devices, on_device(): lax.all_to_all(jnp.broadcast_to(here[None], (images * members, 1, 3 * LAN...  7.93 us
    pallas_call x1, Pallas kernels, on_device(): call(second_rim_kernel, 'second_rim', (shape(3, LANES, LANES), shape(1, 3...  6.99 us
    pallas_call x1, Pallas kernels, on_device(): inside = inner(partners, middle)  6.04 us
    pallas_call x1, Pallas kernels, on_device(): inside = inner(partners, start_pos)  6.04 us
  transfers between devices with their start and end apart: 9, of which 4 were waited for; matrix products, arithmetic and copies ran while one was open for 0% of the time, Pallas kernels for 14%

profile of v3, /device:TPU:1, one launch (start us, length us, event | category | flops | bytes accessed | tf_op | source)
XLA Modules:
  0.0 85.9 jit_solution(2549445244120620899)
XLA Ops:
  0.6 1.8 %pack.1 = f32[768,128]{1,0:T(8,128)} custom-call(f32[3,16,1024]{2,1,0:T(8,128)} %bitcast.16, f32[3,8,128]{2,1,0:T(8,128)} %bitcast.17), custom_call_target="tpu_custom_call" | custom-call | bytes 600000 | tf_op jit(solution)/shard_map/pack/pallas_call | solution.py:273
  2.4 11.6 %all-to-all-start = ((f32[16,6,8,128]{3,2,1,0:T(8,128)}), f32[16,6,8,128]{3,2,1,0:T(8,128)S(1)}, u32[]{:S(2)}, u32[]{:S(2)}) async-start(f32[16,6,8,128]{3,2,1,0:T(8,128)} %bitcast.14), calls=%async_computation | async-start | bytes 786432 | tf_op jit(solution)/shard_map/all_to_all | solution.py:282
  14.0 0.0 copy-start.1
  14.0 0.7 copy-done.1
  14.7 0.1 copy.12
  14.8 0.1 pad_add_fusion.place
  14.9 11.2 %all-to-all-done = f32[16,6,8,128]{3,2,1,0:T(8,128)S(1)} async-done(((f32[16,6,8,128]{3,2,1,0:T(8,128)}), f32[16,6,8,128]{3,2,1,0:T(8,128)S(1)}, u32[]{:S(2)}, u32[]{:S(2)}) %all-to-all-start) | async-done | bytes 393248 | tf_op jit(solution)/shard_map/all_to_all | solution.py:282
  26.2 6.1 %collective-permute-start.1 = (f32[4,3,8,128]{3,2,1,0:T(8,128)S(1)}, f32[4,3,8,128]{3,2,1,0:T(8,128)S(1)}, u32[]{:S(2)}, u32[]{:S(2)}) collective-permute-start(f32[4,3,8,128]{3,2,1,0:T(8,128)S(1)} %get-tuple-element.40), channel_id=1, source_target_pairs={{1,2},{2,1},{5,6},{6,5},{9,10},{10,9},{13,14},{14,13},{17,18},{18,... | collective-permute-start | bytes 147464 | tf_op jit(solution)/shard_map/ppermute | solution.py:255
  32.3 0.1 collective-permute-start
  32.4 6.0 %inner.2 = (f32[8,3,8,128]{3,2,1,0:T(8,128)S(1)}, bf16[128,32,128]{2,1,0:T(8,128)(2,1)S(1)}, bf16[128,16,128]{2,1,0:T(8,128)(2,1)S(1)}) custom-call(s32[128,2]{1,0:T(8,128)S(1)} %bitcast.9, f32[16,3,8,128]{3,2,1,0:T(8,128)S(1)} %get-tuple-element.39.field_ref), custom_call_target="tpu_custom_call" | custom-call | flops 8000000000 | tf_op jit(solution)/shard_map/inner/pallas_call | solution.py:298
  38.4 0.0 collective-permute-done.1.rim2_ref
  38.4 0.0 collective-permute-done.rim1_ref
  38.4 5.8 %first_rim.1 = (f32[16,3,8,128]{3,2,1,0:T(8,128)S(1)}, f32[16,3,8,128]{3,2,1,0:T(8,128)S(1)}, f32[4,3,8,128]{3,2,1,0:T(8,128)S(1)}, f32[4,3,8,128]{3,2,1,0:T(8,128)S(1)}) custom-call(s32[128,2]{1,0:T(8,128)S(1)} %bitcast.10, s32[2]{0:T(128)S(1)} %pad_add_fusion.place, f32[16,3,8,128]{3,2,1,0:T(8,128)S(1)} %get-tuple-element.39.field_ref, ...), custom_call_target="tpu_custom_call" | custom-call | flops 8000000000 | tf_op jit(solution)/shard_map/first_rim/pallas_call | solution.py:299
  44.2 0.6 collective-permute-start.2
  44.8 2.1 %collective-permute-start.3 = (f32[4,3,8,128]{3,2,1,0:T(8,128)S(1)}, f32[4,3,8,128]{3,2,1,0:T(8,128)S(1)}, u32[]{:S(2)}, u32[]{:S(2)}) collective-permute-start(f32[4,3,8,128]{3,2,1,0:T(8,128)S(1)} %get-tuple-element.21), channel_id=1, source_target_pairs={{1,2},{2,1},{5,6},{6,5},{9,10},{10,9},{13,14},{14,13},{17,18},{18,... | collective-permute-start | bytes 147464 | tf_op jit(solution)/shard_map/ppermute | solution.py:255
  46.9 6.0 %inner.3 = (f32[8,3,8,128]{3,2,1,0:T(8,128)S(1)}, bf16[128,32,128]{2,1,0:T(8,128)(2,1)S(1)}, bf16[128,16,128]{2,1,0:T(8,128)(2,1)S(1)}) custom-call(s32[128,2]{1,0:T(8,128)S(1)} %bitcast.11, f32[16,3,8,128]{3,2,1,0:T(8,128)S(1)} %get-tuple-element.19.field_ref), custom_call_target="tpu_custom_call" | custom-call | flops 8000000000 | tf_op jit(solution)/shard_map/inner/pallas_call | solution.py:305
  53.0 0.0 copy-start
  53.0 0.0 collective-permute-done.2.rim1_ref
  53.0 0.0 collective-permute-done.3.rim2_ref
  53.0 0.7 copy-done
  53.7 7.0 %second_rim.1 = (f32[3,128,128]{2,1,0:T(8,128)}, f32[1,384]{1,0:T(1,128)S(1)}) custom-call(s32[128,2]{1,0:T(8,128)S(1)} %bitcast.12, s32[2]{0:T(128)S(1)} %pad_add_fusion.place, s32[16,128]{1,0:T(8,128)S(1)} %bitcast.13, f32[16,3,8,128]{3,2,1,0:T(8,128)S(1)} %get-tuple-element.19.field_ref, f32[4,3,8,128]{3,2,1,0:T(8,128)S(1)} %collective-permute-done.2.rim1_ref, ...), custom_call_target="tpu_custom_call" | custom-call | flops 8000000000 | tf_op jit(solution)/shard_map/second_rim/pallas_call | solution.py:306
  60.7 1.8 %collective-permute-start.6 = (f32[1,384]{1,0:T(1,128)S(1)}, f32[1,384]{1,0:T(1,128)S(1)}, u32[]{:S(2)}, u32[]{:S(2)}) collective-permute-start(f32[1,384]{1,0:T(1,128)S(1)} %get-tuple-element.28), channel_id=1, source_target_pairs={{0,3},{1,2},{2,1},{3,0},{4,7},{5,6},{6,5},{7,4},{8,11},{9,10},{10,... | collective-permute-start | bytes 4616 | tf_op jit(solution)/shard_map/ppermute | solution.py:315
  62.5 0.0 collective-permute-start.5
  62.5 0.5 collective-permute-start.4
  63.0 0.8 collective-permute-done.6
  63.8 1.2 %collective-permute-done.5 = f32[1,384]{1,0:T(1,128)S(1)} collective-permute-done((f32[1,384]{1,0:T(1,128)S(1)}, f32[1,384]{1,0:T(1,128)S(1)}, u32[]{:S(2)}, u32[]{:S(2)}) %collective-permute-start.5) | collective-permute-done | bytes 1568 | tf_op jit(solution)/shard_map/ppermute | solution.py:315
  64.9 0.0 collective-permute-done.4
  64.9 0.7 broadcast_in_dim.27
  65.6 7.9 %all-to-all-start.1 = ((f32[64,1,384]{2,1,0:T(1,128)}), f32[64,1,384]{2,1,0:T(1,128)S(1)}, u32[]{:S(2)}, u32[]{:S(2)}) async-start(f32[64,1,384]{2,1,0:T(1,128)} %broadcast_in_dim.27), calls=%async_computation.1 | async-start | bytes 196608 | tf_op jit(solution)/shard_map/all_to_all | solution.py:317
  73.6 11.6 %all-to-all-done.1 = f32[64,1,384]{2,1,0:T(1,128)S(1)} async-done(((f32[64,1,384]{2,1,0:T(1,128)}), f32[64,1,384]{2,1,0:T(1,128)S(1)}, u32[]{:S(2)}, u32[]{:S(2)}) %all-to-all-start.1) | async-done | bytes 98336 | tf_op jit(solution)/shard_map/all_to_all | solution.py:317
  85.3 0.1 multiply_reduce_fusion
  85.3 0.6 reshape.31
  (7 shorter events, 0.1 us)
Async XLA Ops:
  2.4 23.7 %all-to-all-start = ((f32[16,6,8,128]{3,2,1,0:T(8,128)}), f32[16,6,8,128]{3,2,1,0:T(8,128)S(1)}, u32[]{:S(2)}, u32[]{:S(2)}) async-start(f32[16,6,8,128]{3,2,1,0:T(8,128)} %bitcast.14), calls=%async_computation | async-start | bytes 786432 | tf_op jit(solution)/shard_map/all_to_all | solution.py:282
  14.0 0.7 copy-start.1
  26.2 12.2 %collective-permute-start.1 = (f32[4,3,8,128]{3,2,1,0:T(8,128)S(1)}, f32[4,3,8,128]{3,2,1,0:T(8,128)S(1)}, u32[]{:S(2)}, u32[]{:S(2)}) collective-permute-start(f32[4,3,8,128]{3,2,1,0:T(8,128)S(1)} %get-tuple-element.40), channel_id=1, source_target_pairs={{1,2},{2,1},{5,6},{6,5},{9,10},{10,9},{13,14},{14,13},{17,18},{18,... | collective-permute-start | bytes 147464 | tf_op jit(solution)/shard_map/ppermute | solution.py:255
  32.3 6.2 %collective-permute-start = (f32[4,3,8,128]{3,2,1,0:T(8,128)S(1)}, f32[4,3,8,128]{3,2,1,0:T(8,128)S(1)}, u32[]{:S(2)}, u32[]{:S(2)}) collective-permute-start(f32[4,3,8,128]{3,2,1,0:T(8,128)S(1)} %get-tuple-element.41), channel_id=1, source_target_pairs={{0,1},{1,0},{2,3},{3,2},{4,5},{5,4},{6,7},{7,6},{8,9},{9,8},{10,11... | collective-permute-start | bytes 147464 | tf_op jit(solution)/shard_map/ppermute | solution.py:255
  44.2 8.7 %collective-permute-start.2 = (f32[4,3,8,128]{3,2,1,0:T(8,128)S(1)}, f32[4,3,8,128]{3,2,1,0:T(8,128)S(1)}, u32[]{:S(2)}, u32[]{:S(2)}) collective-permute-start(f32[4,3,8,128]{3,2,1,0:T(8,128)S(1)} %get-tuple-element.20), channel_id=1, source_target_pairs={{0,1},{1,0},{2,3},{3,2},{4,5},{5,4},{6,7},{7,6},{8,9},{9,8},{10,11... | collective-permute-start | bytes 147464 | tf_op jit(solution)/shard_map/ppermute | solution.py:255
  44.8 8.2 %collective-permute-start.3 = (f32[4,3,8,128]{3,2,1,0:T(8,128)S(1)}, f32[4,3,8,128]{3,2,1,0:T(8,128)S(1)}, u32[]{:S(2)}, u32[]{:S(2)}) collective-permute-start(f32[4,3,8,128]{3,2,1,0:T(8,128)S(1)} %get-tuple-element.21), channel_id=1, source_target_pairs={{1,2},{2,1},{5,6},{6,5},{9,10},{10,9},{13,14},{14,13},{17,18},{18,... | collective-permute-start | bytes 147464 | tf_op jit(solution)/shard_map/ppermute | solution.py:255
  53.0 0.7 copy-start
  60.7 3.1 %collective-permute-start.6 = (f32[1,384]{1,0:T(1,128)S(1)}, f32[1,384]{1,0:T(1,128)S(1)}, u32[]{:S(2)}, u32[]{:S(2)}) collective-permute-start(f32[1,384]{1,0:T(1,128)S(1)} %get-tuple-element.28), channel_id=1, source_target_pairs={{0,3},{1,2},{2,1},{3,0},{4,7},{5,6},{6,5},{7,4},{8,11},{9,10},{10,... | collective-permute-start | bytes 4616 | tf_op jit(solution)/shard_map/ppermute | solution.py:315
  62.5 2.4 %collective-permute-start.5 = (f32[1,384]{1,0:T(1,128)S(1)}, f32[1,384]{1,0:T(1,128)S(1)}, u32[]{:S(2)}, u32[]{:S(2)}) collective-permute-start(f32[1,384]{1,0:T(1,128)S(1)} %get-tuple-element.28), channel_id=1, source_target_pairs={{0,2},{1,3},{2,0},{3,1},{4,6},{5,7},{6,4},{7,5},{8,10},{9,11},{10,... | collective-permute-start | bytes 4616 | tf_op jit(solution)/shard_map/ppermute | solution.py:315
  62.5 2.4 %collective-permute-start.4 = (f32[1,384]{1,0:T(1,128)S(1)}, f32[1,384]{1,0:T(1,128)S(1)}, u32[]{:S(2)}, u32[]{:S(2)}) collective-permute-start(f32[1,384]{1,0:T(1,128)S(1)} %get-tuple-element.28), channel_id=1, source_target_pairs={{0,1},{1,0},{2,3},{3,2},{4,5},{5,4},{6,7},{7,6},{8,9},{9,8},{10,11... | collective-permute-start | bytes 4616 | tf_op jit(solution)/shard_map/ppermute | solution.py:315
  65.6 19.6 %all-to-all-start.1 = ((f32[64,1,384]{2,1,0:T(1,128)}), f32[64,1,384]{2,1,0:T(1,128)S(1)}, u32[]{:S(2)}, u32[]{:S(2)}) async-start(f32[64,1,384]{2,1,0:T(1,128)} %broadcast_in_dim.27), calls=%async_computation.1 | async-start | bytes 196608 | tf_op jit(solution)/shard_map/all_to_all | solution.py:317

commit v4 on v3

--- a/solution.py
+++ b/solution.py
@@ -11,6 +11,8 @@
 GSIZE = 16
 LANES = 128
 ROWS = 8
+LAG = 5
+SLOTS = 16
 
 time_step = 0.25
 strength = 0.1
@@ -55,24 +57,28 @@
         values[first + t] = rows_v[pl.ds(t, 16, stride=ROWS), :].astype(BF16)
 
 
-def own_rows(field, rows_p):
+def put_own_rows(field, rows_p, first):
     one, zero = jnp.ones((ROWS, LANES), F32), jnp.zeros((ROWS, LANES), F32)
     norm = three_parts(0.5 - 0.5 * (field[0] * field[0] + field[1] * field[1] + field[2] * field[2]))
     of_p = []
     for x in field:
         h, m, l = three_parts(x)
         of_p += [h, h, m, m, h, l]
-    put_rows(rows_p, of_p + list(norm) + [one] * 3 + [zero] * 8)
-
-
-def group_forces(field, tile0, shift, pairs, rows_p, sums, columns, values):
-    own_rows(field, rows_p)
-    halo_tiles = HALO // LANES
-    for t in range(ROWS):
-        tile = tile0 + t
-        others = [tile + halo_tiles, pairs[tile, 0], pairs[tile, 1]]
-        others = [e - shift for e in others]
-        p_side = rows_p[pl.ds(t, 32, stride=ROWS), :].astype(BF16)
+    put_rows(rows_p.at[pl.ds(first, 32 * ROWS)], of_p + list(norm) + [one] * 3 + [zero] * 8)
+
+
+def forces(groups, field_ref, shift, pairs, rows_p, sums, weights, columns, values, emit):
+    def place_of(n):
+        group, t = divmod(n, ROWS)
+        tile = groups[group] * ROWS + t
+        others = [tile + HALO // LANES, pairs[0, tile], pairs[1, tile]]
+        return group, t, [e - shift for e in others]
+
+    def make_weights(n):
+        group, t, others = place_of(n)
+        if t == 0:
+            put_own_rows([field_ref[groups[group], c] for c in range(3)], rows_p, group * 32 * ROWS)
+        p_side = rows_p[pl.ds(group * 32 * ROWS + t, 32, stride=ROWS), :].astype(BF16)
         q_side = jnp.concatenate([columns[e] for e in others], axis=1)
         overlap = jnp.maximum(
             lax.dot_general(
@@ -80,37 +86,47 @@
             ),
             0.0,
         )
-        weight = overlap * overlap
-        high, low = two_parts(weight)
+        high, low = two_parts(overlap * overlap)
+        weights[n % SLOTS, :3 * LANES] = high
+        weights[n % SLOTS, 3 * LANES:] = low
+
+    def use_weights(n):
+        group, t, others = place_of(n)
         q_values = jnp.concatenate([values[e] for e in others], axis=1)
-        sums[t * 16:(t + 1) * 16, :] = jnp.dot(
-            jnp.concatenate([q_values] * 2, axis=1),
-            jnp.concatenate([high, low], axis=0),
-            preferred_element_type=F32,
+        base = group * 16 * ROWS
+        sums[base + t * 16:base + (t + 1) * 16, :] = jnp.dot(
+            jnp.concatenate([q_values] * 2, axis=1), weights[n % SLOTS], preferred_element_type=F32
         )
-    row = lambda r: sums[pl.ds(r, ROWS, stride=16), :]
-    total = row(3)
-    return [
-        strength * (field[c] * total - (row(c) + row(8 + c) + row(4 + c))) for c in range(3)
-    ]
-
-
-def inner_kernel(pairs, field_ref, out_ref, columns, values, rows_q, rows_v, rows_p, sums):
+        if t == ROWS - 1:
+            row = lambda r: sums[pl.ds(base + r, ROWS, stride=16), :]
+            total = row(3)
+            for c in range(3):
+                pulled = row(c) + row(8 + c) + row(4 + c)
+                emit(groups[group], c, strength * (field_ref[groups[group], c] * total - pulled))
+
+    count = len(groups) * ROWS
+    for n in range(count + LAG):
+        if n < count:
+            make_weights(n)
+        if n >= LAG:
+            use_weights(n - LAG)
+
+
+def inner_kernel(pairs, field_ref, out_ref, columns, values, rows_q, rows_v, rows_p, sums, weights):
     @pl.loop(0, 16)
     def _(s):
         build_group([field_ref[s, c] for c in range(3)], rows_q, rows_v, columns, values, s * ROWS)
 
-    for s in range(8):
-        field = [field_ref[s + 4, c] for c in range(3)]
-        force = group_forces(
-            field, (s + 4) * ROWS, HALO // LANES, pairs, rows_p, sums, columns, values
-        )
-        for c in range(3):
-            out_ref[s, c] = force[c]
+    def emit(s, c, force):
+        out_ref[s - 4, c] = force
+
+    forces(
+        range(4, 12), field_ref, HALO // LANES, pairs, rows_p, sums, weights, columns, values, emit
+    )
 
 
 def rim_forces(
-    pairs, place, field_ref, rim_refs, own_tables, rows_q, rows_v, rows_p, sums, columns, values, emit
+    pairs, place, field_ref, rim_refs, own_tables, rows_q, rows_v, rows_p, sums, weights, columns, values, emit
 ):
     @pl.loop(0, 16)
     def _(s):
@@ -126,17 +142,15 @@
                 [ref[s, c] for c in range(3)], rows_q, rows_v, columns, values, (first + s) * ROWS
             )
 
-    for s in (0, 1, 2, 3, 12, 13, 14, 15):
-        field = [field_ref[s, c] for c in range(3)]
-        force = group_forces(field, s * ROWS, 0, pairs, rows_p, sums, columns, values)
-        for c in range(3):
-            emit(s, c, force[c])
+    forces(
+        (0, 1, 2, 3, 12, 13, 14, 15), field_ref, 0, pairs, rows_p, sums, weights, columns, values, emit
+    )
 
 
 def first_rim_kernel(
     pairs, place, field_ref, rim1_ref, rim2_ref, inner_ref, columns_ref, values_ref, vel_ref,
     middle_ref, base_ref, send1_ref, send2_ref,
-    rows_q, rows_v, rows_p, sums, columns, values,
+    rows_q, rows_v, rows_p, sums, weights, columns, values,
 ):
     def step(s, c, force):
         velocity = vel_ref[s, c] + time_step * force
@@ -146,7 +160,7 @@
 
     rim_forces(
         pairs, place, field_ref, (rim1_ref, rim2_ref), (columns_ref, values_ref),
-        rows_q, rows_v, rows_p, sums, columns, values, step,
+        rows_q, rows_v, rows_p, sums, weights, columns, values, step,
     )
     for s in range(8):
         for c in range(3):
@@ -160,7 +174,7 @@
 def second_rim_kernel(
     pairs, place, groups_ref, field_ref, rim1_ref, rim2_ref, inner_ref, columns_ref, values_ref,
     base_ref, final_ref, part_ref,
-    rows_q, rows_v, rows_p, sums, columns, values,
+    rows_q, rows_v, rows_p, sums, weights, columns, values,
 ):
     def step(s, c, force):
         final_ref[c, pl.ds(s * ROWS, ROWS), :] = (
@@ -169,7 +183,7 @@
 
     rim_forces(
         pairs, place, field_ref, (rim1_ref, rim2_ref), (columns_ref, values_ref),
-        rows_q, rows_v, rows_p, sums, columns, values, step,
+        rows_q, rows_v, rows_p, sums, weights, columns, values, step,
     )
     for s in range(8):
         for c in range(3):
@@ -222,8 +236,9 @@
 ROW_SCRATCH = [
     pltpu.VMEM((32 * ROWS, LANES), F32),
     pltpu.VMEM((16 * ROWS, LANES), F32),
-    pltpu.VMEM((32 * ROWS, LANES), F32),
-    pltpu.VMEM((16 * ROWS, LANES), F32),
+    pltpu.VMEM((8 * 32 * ROWS, LANES), F32),
+    pltpu.VMEM((8 * 16 * ROWS, LANES), F32),
+    pltpu.VMEM((SLOTS, 6 * LANES, LANES), BF16),
 ]
 TABLES = [pltpu.VMEM((192, 32, LANES), BF16), pltpu.VMEM((192, 16, LANES), BF16)]
 
@@ -255,8 +270,8 @@
     return lax.ppermute(first, "domain", inside), lax.ppermute(second, "domain", across)
 
 
-def string_shares():
-    images, place = lax.axis_size("image"), lax.axis_index("image")
+def string_shares(place):
+    images = lax.axis_size("image")
     ids = jnp.arange(images)
     neighbours = (place > 0).astype(F32) + (place < images - 1).astype(F32)
     return jnp.where(jnp.abs(ids - place) == 1, smoothing, 0.0) + jnp.where(
@@ -265,11 +280,11 @@
 
 
 def on_device(configuration, velocities, pairs, cv_atoms):
-    partners = pairs[0]
+    partners = pairs[0].T
     groups = cv_atoms.T
-    domain = lax.axis_index("domain").astype(jnp.int32)
-    odd = domain % 2
-    place = jnp.stack([domain, odd])
+    configuration, velocities, domain, image = lax.optimization_barrier(
+        (configuration, velocities, lax.axis_index("domain"), lax.axis_index("image"))
+    )
     packed = call(
         pack_kernel, "pack", shape(16 * 48, LANES), [ANY, ANY],
         [
@@ -282,7 +297,10 @@
     got = lax.all_to_all(
         packed.reshape(16, 6, ROWS, LANES), "swarm", split_axis=0, concat_axis=0, tiled=True
     )
+    got, domain, image = lax.optimization_barrier((got, domain, image))
     start_vel, start_pos = got[:, :3], got[:, 3:]
+    odd = domain % 2
+    place = jnp.stack([domain, odd])
 
     whole, rim = shape(16, 3, ROWS, LANES), shape(4, 3, ROWS, LANES)
     tables = (
@@ -307,19 +325,22 @@
         second_rim_kernel, "second_rim", (shape(3, LANES, LANES), shape(1, 3 * LANES)),
         [SMEM, SMEM] + [VMEM] * 8, ROW_SCRATCH + TABLES, WORK, 0,
     )(partners, place, groups, middle, rim1, rim2, *inside, base)
-    part, share = lax.optimization_barrier((part, string_shares()))
+    images, members = lax.axis_size("image"), lax.axis_size("swarm")
+    shares = jnp.broadcast_to(
+        (string_shares(image) / (members * GSIZE))[:, None], (images, 3 * LANES)
+    )
+    part, shares = lax.optimization_barrier((part, shares))
     final_positions = final.reshape(1, 1, 3, 1, LANES * LANES)
 
     here = part
     for offset in range(1, 4):
         here = here + lax.ppermute(part, "domain", [(i, i ^ offset) for i in range(4)])
-    images, members = lax.axis_size("image"), lax.axis_size("swarm")
     everyone = lax.all_to_all(
         jnp.broadcast_to(here[None], (images * members, 1, 3 * LANES)),
         ("image", "swarm"), split_axis=0, concat_axis=0, tiled=True,
     )
-    updated = jnp.sum(everyone.reshape(images, members, 3 * LANES), axis=1) / (members * GSIZE)
-    new_string = jnp.sum(share[:, None] * updated, axis=0).reshape(1, 3, LANES)
+    mixed = everyone.reshape(images, members, 3 * LANES) * shares[:, None]
+    new_string = jnp.sum(mixed, axis=(0, 1)).reshape(1, 3, LANES)
     return (final_positions, new_string)
 
 

time: 86.3 us -> 80 us (0.927)
  blocking collectives: 0 us -> 23.7 us
  waiting for transfers between devices: 24.8 us -> 12.7 us
  starting transfers between devices: 30.7 us -> 19.6 us
  Pallas kernels: 26.6 us -> 20.3 us
    all_to_all x0 -> x1, blocking collectives: none -> 23.7 us  [on_device(): lax.all_to_all(packed.reshape(16, 6, ROWS, LANES), 'swarm', split_axis=0,...]
    all_to_all x1 -> x0, starting transfers between devices: 11.6 us -> none  [on_device(): lax.all_to_all(packed.reshape(16, 6, ROWS, LANES), 'swarm', split_axis=0,...]
    all_to_all x1 -> x0, waiting for transfers between devices: 11.2 us -> none  [on_device(): lax.all_to_all(packed.reshape(16, 6, ROWS, LANES), 'swarm', split_axis=0,...]
    ppermute x2, starting transfers between devices: 0.67 us -> 3.67 us  [swap_rims(): lax.ppermute(first, 'domain', inside)]
    ppermute x2, starting transfers between devices: 8.18 us -> 5.86 us  [swap_rims(): lax.ppermute(second, 'domain', across)]
    pallas_call x1, Pallas kernels: 6.99 us -> 5.11 us  [on_device(): call(second_rim_kernel, 'second_rim', (shape(3, LANES, LANES), shape(1, 3...]
    pallas_call x1, Pallas kernels: 5.8 us -> 4.32 us  [on_device(): call(first_rim_kernel, 'first_rim', (whole, whole, rim, rim), [SMEM, SMEM...]
    pallas_call x1, Pallas kernels: 6.04 us -> 4.56 us  [on_device(): inside = inner(partners, start_pos)]
  transfers between devices with their start and end apart: 9 -> 8, of which waited for: 4 -> 3; matrix products, arithmetic and copies ran while one was open for 0% -> 0% of each run, Pallas kernels for 14% -> 11%
where the time goes in v4:
time: 80 us; the launch traced here: 79.5 us
  blocking collectives  23.7 us (30%)
  Pallas kernels  20.3 us (25%)
  starting transfers between devices  19.6 us (25%)
  waiting for transfers between devices  12.7 us (16%)
  local copies, waits for them, and re-layouts  2.15 us (3%)
  between operations  0.81 us (1%)
    all_to_all x1, blocking collectives, on_device(): lax.all_to_all(packed.reshape(16, 6, ROWS, LANES), 'swarm', split_axis=0,...  23.7 us
    all_to_all x1, waiting for transfers between devices, on_device(): lax.all_to_all(jnp.broadcast_to(here[None], (images * members, 1, 3 * LAN...  11.1 us
    all_to_all x1, starting transfers between devices, on_device(): lax.all_to_all(jnp.broadcast_to(here[None], (images * members, 1, 3 * LAN...  7.92 us
    ppermute x2, starting transfers between devices, swap_rims(): lax.ppermute(second, 'domain', across)  5.86 us
    pallas_call x1, Pallas kernels, on_device(): call(second_rim_kernel, 'second_rim', (shape(3, LANES, LANES), shape(1, 3...  5.11 us
    pallas_call x1, Pallas kernels, on_device(): inside = inner(partners, middle)  4.57 us
    pallas_call x1, Pallas kernels, on_device(): inside = inner(partners, start_pos)  4.56 us
    pallas_call x1, Pallas kernels, on_device(): call(first_rim_kernel, 'first_rim', (whole, whole, rim, rim), [SMEM, SMEM...  4.32 us
  transfers between devices with their start and end apart: 8, of which 3 were waited for; matrix products, arithmetic and copies ran while one was open for 0% of the time, Pallas kernels for 11%

profile of v4, /device:TPU:1, one launch (start us, length us, event | category | flops | bytes accessed | tf_op | source)
XLA Modules:
  0.0 79.5 jit_solution(9563764590603503003)
XLA Ops:
  0.6 1.7 %pack.1 = f32[768,128]{1,0:T(8,128)} custom-call(f32[3,16,1024]{2,1,0:T(8,128)} %bitcast.16, f32[3,8,128]{2,1,0:T(8,128)} %bitcast.17), custom_call_target="tpu_custom_call" | custom-call | bytes 600000 | tf_op jit(solution)/shard_map/pack/pallas_call | solution.py:288
  2.4 23.7 %all_to_all.10 = f32[16,6,8,128]{3,2,1,0:T(8,128)S(1)} all-to-all(f32[16,6,8,128]{3,2,1,0:T(8,128)} %bitcast.15), channel_id=1, replica_groups=mesh['image'=4,'swarm'=16,'domain'=4] {'swarm'}, dimensions={0} | all-to-all | bytes 786432 | tf_op jit(solution)/shard_map/all_to_all | solution.py:297
  26.2 3.6 %collective-permute-start = (f32[4,3,8,128]{3,2,1,0:T(8,128)S(1)}, f32[4,3,8,128]{3,2,1,0:T(8,128)S(1)}, u32[]{:S(2)}, u32[]{:S(2)}) collective-permute-start(f32[4,3,8,128]{3,2,1,0:T(8,128)S(1)} %get-tuple-element.55), channel_id=1, source_target_pairs={{0,1},{1,0},{2,3},{3,2},{4,5},{5,4},{6,7},{7,6},{8,9},{9,8},{10,11... | collective-permute-start | bytes 147464 | tf_op jit(solution)/shard_map/ppermute | solution.py:270
  29.7 0.0 copy-start.1
  29.7 2.6 %collective-permute-start.1 = (f32[4,3,8,128]{3,2,1,0:T(8,128)S(1)}, f32[4,3,8,128]{3,2,1,0:T(8,128)S(1)}, u32[]{:S(2)}, u32[]{:S(2)}) collective-permute-start(f32[4,3,8,128]{3,2,1,0:T(8,128)S(1)} %get-tuple-element.54), channel_id=1, source_target_pairs={{1,2},{2,1},{5,6},{6,5},{9,10},{10,9},{13,14},{14,13},{17,18},{18,... | collective-permute-start | bytes 147464 | tf_op jit(solution)/shard_map/ppermute | solution.py:270
  32.4 0.0 copy-done.1
  32.4 4.6 %inner.2 = (f32[8,3,8,128]{3,2,1,0:T(8,128)S(1)}, bf16[128,32,128]{2,1,0:T(8,128)(2,1)S(1)}, bf16[128,16,128]{2,1,0:T(8,128)(2,1)S(1)}) custom-call(s32[2,128]{1,0:T(2,128)S(1)} %bitcast.11, f32[16,3,8,128]{3,2,1,0:T(8,128)S(1)} %get-tuple-element.53.field_ref), custom_call_target="tpu_custom_call" | custom-call | flops 8000000000 | tf_op jit(solution)/shard_map/inner/pallas_call | solution.py:316
  37.0 0.1 pad_add_fusion.place
  37.1 0.0 collective-permute-done.rim1_ref
  37.1 0.0 collective-permute-done.1.rim2_ref
  37.1 4.3 %first_rim.1 = (f32[16,3,8,128]{3,2,1,0:T(8,128)S(1)}, f32[16,3,8,128]{3,2,1,0:T(8,128)S(1)}, f32[4,3,8,128]{3,2,1,0:T(8,128)S(1)}, f32[4,3,8,128]{3,2,1,0:T(8,128)S(1)}) custom-call(s32[2,128]{1,0:T(2,128)S(1)} %bitcast.12, s32[2]{0:T(128)S(1)} %pad_add_fusion.place, f32[16,3,8,128]{3,2,1,0:T(8,128)S(1)} %get-tuple-element.53.field_ref, ...), custom_call_target="tpu_custom_call" | custom-call | flops 8000000000 | tf_op jit(solution)/shard_map/first_rim/pallas_call | solution.py:317
  41.4 0.1 collective-permute-start.2
  41.5 3.2 %collective-permute-start.3 = (f32[4,3,8,128]{3,2,1,0:T(8,128)S(1)}, f32[4,3,8,128]{3,2,1,0:T(8,128)S(1)}, u32[]{:S(2)}, u32[]{:S(2)}) collective-permute-start(f32[4,3,8,128]{3,2,1,0:T(8,128)S(1)} %get-tuple-element.34), channel_id=1, source_target_pairs={{1,2},{2,1},{5,6},{6,5},{9,10},{10,9},{13,14},{14,13},{17,18},{18,... | collective-permute-start | bytes 147464 | tf_op jit(solution)/shard_map/ppermute | solution.py:270
  44.7 4.6 %inner.3 = (f32[8,3,8,128]{3,2,1,0:T(8,128)S(1)}, bf16[128,32,128]{2,1,0:T(8,128)(2,1)S(1)}, bf16[128,16,128]{2,1,0:T(8,128)(2,1)S(1)}) custom-call(s32[2,128]{1,0:T(2,128)S(1)} %bitcast.13, f32[16,3,8,128]{3,2,1,0:T(8,128)S(1)} %get-tuple-element.32.field_ref), custom_call_target="tpu_custom_call" | custom-call | flops 8000000000 | tf_op jit(solution)/shard_map/inner/pallas_call | solution.py:323
  49.3 0.0 copy-start
  49.3 0.0 collective-permute-done.2.rim1_ref
  49.3 0.0 collective-permute-done.3.rim2_ref
  49.3 0.7 copy-done
  50.0 5.1 %second_rim.1 = (f32[3,128,128]{2,1,0:T(8,128)}, f32[1,384]{1,0:T(1,128)S(1)}) custom-call(s32[2,128]{1,0:T(2,128)S(1)} %bitcast.14, s32[2]{0:T(128)S(1)} %pad_add_fusion.place, s32[16,128]{1,0:T(8,128)S(1)} %bitcast.10, f32[16,3,8,128]{3,2,1,0:T(8,128)S(1)} %get-tuple-element.32.field_ref, f32[4,3,8,128]{3,2,1,0:T(8,128)S(1)} %collective-permute-done.2.rim1_ref, ...), custom_call_target="tpu_custom_call" | custom-call | flops 8000000000 | tf_op jit(solution)/shard_map/second_rim/pallas_call | solution.py:324
  55.1 0.1 broadcast_in_dim.32
  55.2 0.0 collective-permute-start.4
  55.2 0.7 collective-permute-start.5
  55.9 1.4 %collective-permute-start.6 = (f32[1,384]{1,0:T(1,128)S(1)}, f32[1,384]{1,0:T(1,128)S(1)}, u32[]{:S(2)}, u32[]{:S(2)}) collective-permute-start(f32[1,384]{1,0:T(1,128)S(1)} %get-tuple-element.42), channel_id=1, source_target_pairs={{0,3},{1,2},{2,1},{3,0},{4,7},{5,6},{6,5},{7,4},{8,11},{9,10},{10,... | collective-permute-start | bytes 4616 | tf_op jit(solution)/shard_map/ppermute | solution.py:337
  57.4 0.0 collective-permute-done.4
  57.4 0.4 collective-permute-done.5
  57.8 1.2 %collective-permute-done.6 = f32[1,384]{1,0:T(1,128)S(1)} collective-permute-done((f32[1,384]{1,0:T(1,128)S(1)}, f32[1,384]{1,0:T(1,128)S(1)}, u32[]{:S(2)}, u32[]{:S(2)}) %collective-permute-start.6) | collective-permute-done | bytes 1568 | tf_op jit(solution)/shard_map/ppermute | solution.py:337
  59.0 0.7 broadcast_in_dim.34
  59.7 7.9 %all-to-all-start.1 = ((f32[64,1,384]{2,1,0:T(1,128)}), f32[64,1,384]{2,1,0:T(1,128)S(1)}, u32[]{:S(2)}, u32[]{:S(2)}) async-start(f32[64,1,384]{2,1,0:T(1,128)} %broadcast_in_dim.34), calls=%async_computation.1 | async-start | bytes 196608 | tf_op jit(solution)/shard_map/all_to_all | solution.py:338
  67.6 0.1 mul.24
  67.7 11.1 %all-to-all-done.1 = f32[64,1,384]{2,1,0:T(1,128)S(1)} async-done(((f32[64,1,384]{2,1,0:T(1,128)}), f32[64,1,384]{2,1,0:T(1,128)S(1)}, u32[]{:S(2)}, u32[]{:S(2)}) %all-to-all-start.1) | async-done | bytes 98336 | tf_op jit(solution)/shard_map/all_to_all | solution.py:338
  78.8 0.1 multiply_reduce_fusion
  78.9 0.6 reshape.43
  (5 shorter events, 0.1 us)
Async XLA Ops:
  26.2 10.9 %collective-permute-start = (f32[4,3,8,128]{3,2,1,0:T(8,128)S(1)}, f32[4,3,8,128]{3,2,1,0:T(8,128)S(1)}, u32[]{:S(2)}, u32[]{:S(2)}) collective-permute-start(f32[4,3,8,128]{3,2,1,0:T(8,128)S(1)} %get-tuple-element.55), channel_id=1, source_target_pairs={{0,1},{1,0},{2,3},{3,2},{4,5},{5,4},{6,7},{7,6},{8,9},{9,8},{10,11... | collective-permute-start | bytes 147464 | tf_op jit(solution)/shard_map/ppermute | solution.py:270
  29.7 2.6 %copy-start.1 = (s32[1,128,2]{1,2,0:T(2,128)S(1)}, s32[1,128,2]{1,2,0:T(2,128)}, u32[]{:S(2)}) copy-start(s32[1,128,2]{1,2,0:T(2,128)} %param.6) | copy-start | bytes 3076
  29.7 7.3 %collective-permute-start.1 = (f32[4,3,8,128]{3,2,1,0:T(8,128)S(1)}, f32[4,3,8,128]{3,2,1,0:T(8,128)S(1)}, u32[]{:S(2)}, u32[]{:S(2)}) collective-permute-start(f32[4,3,8,128]{3,2,1,0:T(8,128)S(1)} %get-tuple-element.54), channel_id=1, source_target_pairs={{1,2},{2,1},{5,6},{6,5},{9,10},{10,9},{13,14},{14,13},{17,18},{18,... | collective-permute-start | bytes 147464 | tf_op jit(solution)/shard_map/ppermute | solution.py:270
  41.4 7.9 %collective-permute-start.2 = (f32[4,3,8,128]{3,2,1,0:T(8,128)S(1)}, f32[4,3,8,128]{3,2,1,0:T(8,128)S(1)}, u32[]{:S(2)}, u32[]{:S(2)}) collective-permute-start(f32[4,3,8,128]{3,2,1,0:T(8,128)S(1)} %get-tuple-element.33), channel_id=1, source_target_pairs={{0,1},{1,0},{2,3},{3,2},{4,5},{5,4},{6,7},{7,6},{8,9},{9,8},{10,11... | collective-permute-start | bytes 147464 | tf_op jit(solution)/shard_map/ppermute | solution.py:270
  41.5 7.8 %collective-permute-start.3 = (f32[4,3,8,128]{3,2,1,0:T(8,128)S(1)}, f32[4,3,8,128]{3,2,1,0:T(8,128)S(1)}, u32[]{:S(2)}, u32[]{:S(2)}) collective-permute-start(f32[4,3,8,128]{3,2,1,0:T(8,128)S(1)} %get-tuple-element.34), channel_id=1, source_target_pairs={{1,2},{2,1},{5,6},{6,5},{9,10},{10,9},{13,14},{14,13},{17,18},{18,... | collective-permute-start | bytes 147464 | tf_op jit(solution)/shard_map/ppermute | solution.py:270
  49.3 0.7 copy-start
  55.2 2.2 %collective-permute-start.4 = (f32[1,384]{1,0:T(1,128)S(1)}, f32[1,384]{1,0:T(1,128)S(1)}, u32[]{:S(2)}, u32[]{:S(2)}) collective-permute-start(f32[1,384]{1,0:T(1,128)S(1)} %get-tuple-element.42), channel_id=1, source_target_pairs={{0,1},{1,0},{2,3},{3,2},{4,5},{5,4},{6,7},{7,6},{8,9},{9,8},{10,11... | collective-permute-start | bytes 4616 | tf_op jit(solution)/shard_map/ppermute | solution.py:337
  55.2 2.5 %collective-permute-start.5 = (f32[1,384]{1,0:T(1,128)S(1)}, f32[1,384]{1,0:T(1,128)S(1)}, u32[]{:S(2)}, u32[]{:S(2)}) collective-permute-start(f32[1,384]{1,0:T(1,128)S(1)} %get-tuple-element.42), channel_id=1, source_target_pairs={{0,2},{1,3},{2,0},{3,1},{4,6},{5,7},{6,4},{7,5},{8,10},{9,11},{10,... | collective-permute-start | bytes 4616 | tf_op jit(solution)/shard_map/ppermute | solution.py:337
  55.9 3.0 %collective-permute-start.6 = (f32[1,384]{1,0:T(1,128)S(1)}, f32[1,384]{1,0:T(1,128)S(1)}, u32[]{:S(2)}, u32[]{:S(2)}) collective-permute-start(f32[1,384]{1,0:T(1,128)S(1)} %get-tuple-element.42), channel_id=1, source_target_pairs={{0,3},{1,2},{2,1},{3,0},{4,7},{5,6},{6,5},{7,4},{8,11},{9,10},{10,... | collective-permute-start | bytes 4616 | tf_op jit(solution)/shard_map/ppermute | solution.py:337
  59.7 19.1 %all-to-all-start.1 = ((f32[64,1,384]{2,1,0:T(1,128)}), f32[64,1,384]{2,1,0:T(1,128)S(1)}, u32[]{:S(2)}, u32[]{:S(2)}) async-start(f32[64,1,384]{2,1,0:T(1,128)} %broadcast_in_dim.34), calls=%async_computation.1 | async-start | bytes 196608 | tf_op jit(solution)/shard_map/all_to_all | solution.py:338

commit v5 on v4

--- a/solution.py
+++ b/solution.py
@@ -112,7 +112,7 @@
             use_weights(n - LAG)
 
 
-def inner_kernel(pairs, field_ref, out_ref, columns, values, rows_q, rows_v, rows_p, sums, weights):
+def inner_kernel(pairs, field_ref, groups_ref, out_ref, columns, values, rows_q, rows_v, rows_p, sums, weights):
     @pl.loop(0, 16)
     def _(s):
         build_group([field_ref[s, c] for c in range(3)], rows_q, rows_v, columns, values, s * ROWS)
@@ -208,6 +208,25 @@
     for c in range(3):
         both = total[c, :, :LANES] + total[c, :, LANES:]
         part_ref[:, c * LANES:(c + 1) * LANES] = jnp.sum(both, axis=0, keepdims=True)
+
+
+def spread_kernel(own_ref, *refs):
+    others, out_ref = refs[:-1], refs[-1]
+    total = own_ref[...]
+    for ref in others:
+        total = total + ref[...]
+    out_ref[...] = jnp.broadcast_to(total[None], out_ref.shape)
+
+
+def string_kernel(shares, everyone_ref, out_ref):
+    images = shares.shape[0]
+    members = everyone_ref.shape[0] // images
+    total = jnp.zeros((1, 3 * LANES), F32)
+    for i in range(images):
+        updated = jnp.sum(everyone_ref[i * members:(i + 1) * members], axis=0)
+        total = total + shares[i] * updated
+    for c in range(3):
+        out_ref[c] = total[:, c * LANES:(c + 1) * LANES]
 
 
 def pack_kernel(vel_hbm, conf_hbm, out_ref, vel_ref, conf_ref, arrived):
@@ -307,40 +326,40 @@
         jax.ShapeDtypeStruct((128, 32, LANES), BF16), jax.ShapeDtypeStruct((128, 16, LANES), BF16)
     )
     inner = call(
-        inner_kernel, "inner", (shape(8, 3, ROWS, LANES),) + tables, [SMEM, VMEM], ROW_SCRATCH, WORK, 0
+        inner_kernel, "inner", (shape(8, 3, ROWS, LANES),) + tables, [SMEM, VMEM, VMEM], ROW_SCRATCH, WORK, 0
     )
     rim1, rim2 = swap_rims(
         lax.dynamic_slice_in_dim(start_pos, 12 * (1 - odd), 4, 0),
         lax.dynamic_slice_in_dim(start_pos, 12 * odd, 4, 0),
     )
-    inside = inner(partners, start_pos)
+    inside = inner(partners, start_pos, groups)
     middle, base, send1, send2 = call(
         first_rim_kernel, "first_rim", (whole, whole, rim, rim), [SMEM, SMEM] + [VMEM] * 7,
         ROW_SCRATCH + TABLES, WORK, 0,
     )(partners, place, start_pos, rim1, rim2, *inside, start_vel)
 
     rim1, rim2 = swap_rims(send1, send2)
-    inside = inner(partners, middle)
+    inside = inner(partners, middle, groups)
     final, part = call(
         second_rim_kernel, "second_rim", (shape(3, LANES, LANES), shape(1, 3 * LANES)),
         [SMEM, SMEM] + [VMEM] * 8, ROW_SCRATCH + TABLES, WORK, 0,
     )(partners, place, groups, middle, rim1, rim2, *inside, base)
     images, members = lax.axis_size("image"), lax.axis_size("swarm")
-    shares = jnp.broadcast_to(
-        (string_shares(image) / (members * GSIZE))[:, None], (images, 3 * LANES)
-    )
+    shares = string_shares(image) / (members * GSIZE)
     part, shares = lax.optimization_barrier((part, shares))
     final_positions = final.reshape(1, 1, 3, 1, LANES * LANES)
 
-    here = part
-    for offset in range(1, 4):
-        here = here + lax.ppermute(part, "domain", [(i, i ^ offset) for i in range(4)])
-    everyone = lax.all_to_all(
-        jnp.broadcast_to(here[None], (images * members, 1, 3 * LANES)),
-        ("image", "swarm"), split_axis=0, concat_axis=0, tiled=True,
-    )
-    mixed = everyone.reshape(images, members, 3 * LANES) * shares[:, None]
-    new_string = jnp.sum(mixed, axis=(0, 1)).reshape(1, 3, LANES)
+    parts = [part] + [
+        lax.ppermute(part, "domain", [(i, i ^ offset) for i in range(4)]) for offset in (1, 2, 3)
+    ]
+    copies = call(
+        spread_kernel, "spread", shape(images * members, 1, 3 * LANES), [VMEM] * 4, [], 0, 100_000
+    )(*parts)
+    everyone = lax.all_to_all(copies, ("image", "swarm"), split_axis=0, concat_axis=0, tiled=True)
+    new_string = call(
+        string_kernel, "string", shape(3, 1, LANES), [SMEM, VMEM], [], 0, 100_000
+    )(shares, everyone)
+    new_string = new_string.transpose(1, 0, 2)
     return (final_positions, new_string)
 
 

time: 80 us -> 79.5 us (level)
  blocking collectives: 23.7 us -> 43.1 us
  waiting for transfers between devices: 12.7 us -> 1.95 us
  starting transfers between devices: 19.6 us -> 11.2 us
  local copies, waits for them, and re-layouts: 2.15 us -> 0.71 us
  Pallas kernels: 20.3 us -> 21.5 us
    all_to_all x0 -> x1, blocking collectives: none -> 19.4 us  [on_device(): lax.all_to_all(copies, ('image', 'swarm'), split_axis=0, concat_axis=0, t...]
    all_to_all x1 -> x0, waiting for transfers between devices: 11.1 us -> none  [on_device(): lax.all_to_all(jnp.broadcast_to(here[None], (images * members, 1, 3 * LAN...]
    all_to_all x1 -> x0, starting transfers between devices: 7.92 us -> none  [on_device(): lax.all_to_all(jnp.broadcast_to(here[None], (images * members, 1, 3 * LAN...]
    ppermute x2, starting transfers between devices: 3.67 us -> 0.68 us  [swap_rims(): lax.ppermute(first, 'domain', inside)]
    ppermute x2, starting transfers between devices: 5.86 us -> 8.18 us  [swap_rims(): lax.ppermute(second, 'domain', across)]
    pallas_call x2 -> x4, Pallas kernels: 9.12 us -> 10.3 us  [the longest x1 4.56 us: on_device(): inside = inner(partners, middle, groups)]
  transfers between devices with their start and end apart: 8 -> 7, of which waited for: 3 -> 2; matrix products, arithmetic and copies ran while one was open for 0% -> 0% of each run, Pallas kernels for 11% -> 12%
where the time goes in v5:
time: 79.5 us; the launch traced here: 79.2 us
  blocking collectives  43.1 us (54%)
  Pallas kernels  21.5 us (27%)
  starting transfers between devices  11.2 us (14%)
  waiting for transfers between devices  1.95 us (2%)
    all_to_all x1, blocking collectives, on_device(): lax.all_to_all(packed.reshape(16, 6, ROWS, LANES), 'swarm', split_axis=0,...  23.7 us
    all_to_all x1, blocking collectives, on_device(): lax.all_to_all(copies, ('image', 'swarm'), split_axis=0, concat_axis=0, t...  19.4 us
    ppermute x2, starting transfers between devices, swap_rims(): lax.ppermute(second, 'domain', across)  8.18 us
    pallas_call x1, Pallas kernels, on_device(): call(second_rim_kernel, 'second_rim', (shape(3, LANES, LANES), shape(1, 3...  5.1 us
    pallas_call x1, Pallas kernels, on_device(): inside = inner(partners, middle, groups)  4.56 us
    pallas_call x1, Pallas kernels, on_device(): inside = inner(partners, start_pos, groups)  4.56 us
    pallas_call x1, Pallas kernels, on_device(): call(first_rim_kernel, 'first_rim', (whole, whole, rim, rim), [SMEM, SMEM...  4.31 us
    ppermute x3, starting transfers between devices, on_device(): lax.ppermute(part, 'domain', [(i, i ^ offset) for i in range(4)])  2.3 us
  transfers between devices with their start and end apart: 7, of which 2 were waited for; matrix products, arithmetic and copies ran while one was open for 0% of the time, Pallas kernels for 12%

profile of v5, /device:TPU:1, one launch (start us, length us, event | category | flops | bytes accessed | tf_op | source)
XLA Modules:
  0.0 79.2 jit_solution(13986015770665646104)
XLA Ops:
  0.6 1.7 %pack.1 = f32[768,128]{1,0:T(8,128)} custom-call(f32[3,16,1024]{2,1,0:T(8,128)} %bitcast.19, f32[3,8,128]{2,1,0:T(8,128)} %bitcast.20), custom_call_target="tpu_custom_call" | custom-call | bytes 600000 | tf_op jit(solution)/shard_map/pack/pallas_call | solution.py:307
  2.4 23.7 %all_to_all.10 = f32[16,6,8,128]{3,2,1,0:T(8,128)S(1)} all-to-all(f32[16,6,8,128]{3,2,1,0:T(8,128)} %bitcast.18), channel_id=1, replica_groups=mesh['image'=4,'swarm'=16,'domain'=4] {'swarm'}, dimensions={0} | all-to-all | bytes 786432 | tf_op jit(solution)/shard_map/all_to_all | solution.py:316
  26.2 0.0 copy-start
  26.2 6.1 %collective-permute-start.1 = (f32[4,3,8,128]{3,2,1,0:T(8,128)S(1)}, f32[4,3,8,128]{3,2,1,0:T(8,128)S(1)}, u32[]{:S(2)}, u32[]{:S(2)}) collective-permute-start(f32[4,3,8,128]{3,2,1,0:T(8,128)S(1)} %get-tuple-element.50), channel_id=1, source_target_pairs={{1,2},{2,1},{5,6},{6,5},{9,10},{10,9},{13,14},{14,13},{17,18},{18,... | collective-permute-start | bytes 147464 | tf_op jit(solution)/shard_map/ppermute | solution.py:289
  32.3 0.1 collective-permute-start
  32.4 0.0 copy-start.1
  32.4 0.0 copy-done
  32.4 0.7 copy-done.1
  33.1 4.6 %inner.2 = (f32[8,3,8,128]{3,2,1,0:T(8,128)S(1)}, bf16[128,32,128]{2,1,0:T(8,128)(2,1)S(1)}, bf16[128,16,128]{2,1,0:T(8,128)(2,1)S(1)}) custom-call(s32[2,128]{1,0:T(2,128)S(1)} %bitcast.14, f32[16,3,8,128]{3,2,1,0:T(8,128)S(1)} %get-tuple-element.49.field_ref, s32[16,128]{1,0:T(8,128)S(1)} %bitcast.11), custom_call_target="tpu_custom_call" | custom-call | flops 8000000000 | tf_op jit(solution)/shard_map/inner/pallas_call | solution.py:335
  37.6 0.1 pad_add_fusion.place
  37.7 0.0 collective-permute-done.1.rim2_ref
  37.7 0.0 collective-permute-done.rim1_ref
  37.7 4.3 %first_rim.1 = (f32[16,3,8,128]{3,2,1,0:T(8,128)S(1)}, f32[16,3,8,128]{3,2,1,0:T(8,128)S(1)}, f32[4,3,8,128]{3,2,1,0:T(8,128)S(1)}, f32[4,3,8,128]{3,2,1,0:T(8,128)S(1)}) custom-call(s32[2,128]{1,0:T(2,128)S(1)} %bitcast.15, s32[2]{0:T(128)S(1)} %pad_add_fusion.place, f32[16,3,8,128]{3,2,1,0:T(8,128)S(1)} %get-tuple-element.49.field_ref, ...), custom_call_target="tpu_custom_call" | custom-call | flops 8000000000 | tf_op jit(solution)/shard_map/first_rim/pallas_call | solution.py:336
  42.0 0.6 collective-permute-start.2
  42.6 2.1 %collective-permute-start.3 = (f32[4,3,8,128]{3,2,1,0:T(8,128)S(1)}, f32[4,3,8,128]{3,2,1,0:T(8,128)S(1)}, u32[]{:S(2)}, u32[]{:S(2)}) collective-permute-start(f32[4,3,8,128]{3,2,1,0:T(8,128)S(1)} %get-tuple-element.34), channel_id=1, source_target_pairs={{1,2},{2,1},{5,6},{6,5},{9,10},{10,9},{13,14},{14,13},{17,18},{18,... | collective-permute-start | bytes 147464 | tf_op jit(solution)/shard_map/ppermute | solution.py:289
  44.7 4.6 %inner.3 = (f32[8,3,8,128]{3,2,1,0:T(8,128)S(1)}, bf16[128,32,128]{2,1,0:T(8,128)(2,1)S(1)}, bf16[128,16,128]{2,1,0:T(8,128)(2,1)S(1)}) custom-call(s32[2,128]{1,0:T(2,128)S(1)} %bitcast.16, f32[16,3,8,128]{3,2,1,0:T(8,128)S(1)} %get-tuple-element.32.field_ref, s32[16,128]{1,0:T(8,128)S(1)} %bitcast.12), custom_call_target="tpu_custom_call" | custom-call | flops 8000000000 | tf_op jit(solution)/shard_map/inner/pallas_call | solution.py:342
  49.3 0.0 collective-permute-done.2.rim1_ref
  49.3 0.0 collective-permute-done.3.rim2_ref
  49.3 5.1 %second_rim.1 = (f32[3,128,128]{2,1,0:T(8,128)}, f32[1,384]{1,0:T(1,128)S(1)}) custom-call(s32[2,128]{1,0:T(2,128)S(1)} %bitcast.17, s32[2]{0:T(128)S(1)} %pad_add_fusion.place, s32[16,128]{1,0:T(8,128)S(1)} %bitcast.13, f32[16,3,8,128]{3,2,1,0:T(8,128)S(1)} %get-tuple-element.32.field_ref, f32[4,3,8,128]{3,2,1,0:T(8,128)S(1)} %collective-permute-done.2.rim1_ref, ...), custom_call_target="tpu_custom_call" | custom-call | flops 8000000000 | tf_op jit(solution)/shard_map/second_rim/pallas_call | solution.py:343
  54.4 1.8 %collective-permute-start.6 = (f32[1,384]{1,0:T(1,128)S(1)}, f32[1,384]{1,0:T(1,128)S(1)}, u32[]{:S(2)}, u32[]{:S(2)}) collective-permute-start(f32[1,384]{1,0:T(1,128)S(1)} %get-tuple-element.43.own_ref), channel_id=1, source_target_pairs={{0,3},{1,2},{2,1},{3,0},{4,7},{5,6},{6,5},{7,4},{8,11},{9,10},{10,... | collective-permute-start | bytes 4616 | tf_op jit(solution)/shard_map/ppermute | solution.py:353
  56.2 0.0 collective-permute-start.5
  56.2 0.5 collective-permute-start.4
  56.7 0.8 collective-permute-done.6.refs_2_
  57.5 1.1 %collective-permute-done.5.refs_1_ = f32[1,384]{1,0:T(1,128)S(1)} collective-permute-done((f32[1,384]{1,0:T(1,128)S(1)}, f32[1,384]{1,0:T(1,128)S(1)}, u32[]{:S(2)}, u32[]{:S(2)}) %collective-permute-start.5) | collective-permute-done | bytes 1568 | tf_op jit(solution)/shard_map/ppermute | solution.py:353
  58.7 0.0 collective-permute-done.4.refs_0_
  58.7 19.4 %all_to_all.11.everyone_ref = f32[64,1,384]{2,1,0:T(1,128)S(1)} all-to-all(f32[64,1,384]{2,1,0:T(1,128)S(1)} %spread.1), channel_id=1, replica_groups=mesh['image'=4,'swarm'=16,'domain'=4] {'image','swarm'}, dimensions={0} | all-to-all | bytes 196608 | tf_op jit(solution)/shard_map/all_to_all | solution.py:358
  78.1 1.2 %string.1 = f32[3,1,128]{2,1,0:T(1,128)} custom-call(f32[4]{0:T(128)S(1)} %fusion.1.shares, f32[64,1,384]{2,1,0:T(1,128)S(1)} %all_to_all.11.everyone_ref), custom_call_target="tpu_custom_call" | custom-call | bytes 100000 | tf_op jit(solution)/shard_map/string/pallas_call | solution.py:359
  (4 shorter events, 0.1 us)
Async XLA Ops:
  26.2 6.2 %copy-start = (s32[128,16]{0,1:T(8,128)S(1)}, s32[128,16]{0,1:T(8,128)}, u32[]{:S(2)}) copy-start(s32[128,16]{0,1:T(8,128)} %param.7) | copy-start | bytes 24580
  26.2 11.5 %collective-permute-start.1 = (f32[4,3,8,128]{3,2,1,0:T(8,128)S(1)}, f32[4,3,8,128]{3,2,1,0:T(8,128)S(1)}, u32[]{:S(2)}, u32[]{:S(2)}) collective-permute-start(f32[4,3,8,128]{3,2,1,0:T(8,128)S(1)} %get-tuple-element.50), channel_id=1, source_target_pairs={{1,2},{2,1},{5,6},{6,5},{9,10},{10,9},{13,14},{14,13},{17,18},{18,... | collective-permute-start | bytes 147464 | tf_op jit(solution)/shard_map/ppermute | solution.py:289
  32.3 5.4 %collective-permute-start = (f32[4,3,8,128]{3,2,1,0:T(8,128)S(1)}, f32[4,3,8,128]{3,2,1,0:T(8,128)S(1)}, u32[]{:S(2)}, u32[]{:S(2)}) collective-permute-start(f32[4,3,8,128]{3,2,1,0:T(8,128)S(1)} %get-tuple-element.51), channel_id=1, source_target_pairs={{0,1},{1,0},{2,3},{3,2},{4,5},{5,4},{6,7},{7,6},{8,9},{9,8},{10,11... | collective-permute-start | bytes 147464 | tf_op jit(solution)/shard_map/ppermute | solution.py:289
  32.4 0.7 copy-start.1
  42.0 7.3 %collective-permute-start.2 = (f32[4,3,8,128]{3,2,1,0:T(8,128)S(1)}, f32[4,3,8,128]{3,2,1,0:T(8,128)S(1)}, u32[]{:S(2)}, u32[]{:S(2)}) collective-permute-start(f32[4,3,8,128]{3,2,1,0:T(8,128)S(1)} %get-tuple-element.33), channel_id=1, source_target_pairs={{0,1},{1,0},{2,3},{3,2},{4,5},{5,4},{6,7},{7,6},{8,9},{9,8},{10,11... | collective-permute-start | bytes 147464 | tf_op jit(solution)/shard_map/ppermute | solution.py:289
  42.6 6.7 %collective-permute-start.3 = (f32[4,3,8,128]{3,2,1,0:T(8,128)S(1)}, f32[4,3,8,128]{3,2,1,0:T(8,128)S(1)}, u32[]{:S(2)}, u32[]{:S(2)}) collective-permute-start(f32[4,3,8,128]{3,2,1,0:T(8,128)S(1)} %get-tuple-element.34), channel_id=1, source_target_pairs={{1,2},{2,1},{5,6},{6,5},{9,10},{10,9},{13,14},{14,13},{17,18},{18,... | collective-permute-start | bytes 147464 | tf_op jit(solution)/shard_map/ppermute | solution.py:289
  54.4 3.1 %collective-permute-start.6 = (f32[1,384]{1,0:T(1,128)S(1)}, f32[1,384]{1,0:T(1,128)S(1)}, u32[]{:S(2)}, u32[]{:S(2)}) collective-permute-start(f32[1,384]{1,0:T(1,128)S(1)} %get-tuple-element.43.own_ref), channel_id=1, source_target_pairs={{0,3},{1,2},{2,1},{3,0},{4,7},{5,6},{6,5},{7,4},{8,11},{9,10},{10,... | collective-permute-start | bytes 4616 | tf_op jit(solution)/shard_map/ppermute | solution.py:353
  56.2 2.4 %collective-permute-start.5 = (f32[1,384]{1,0:T(1,128)S(1)}, f32[1,384]{1,0:T(1,128)S(1)}, u32[]{:S(2)}, u32[]{:S(2)}) collective-permute-start(f32[1,384]{1,0:T(1,128)S(1)} %get-tuple-element.43.own_ref), channel_id=1, source_target_pairs={{0,2},{1,3},{2,0},{3,1},{4,6},{5,7},{6,4},{7,5},{8,10},{9,11},{10,... | collective-permute-start | bytes 4616 | tf_op jit(solution)/shard_map/ppermute | solution.py:353
  56.2 2.4 %collective-permute-start.4 = (f32[1,384]{1,0:T(1,128)S(1)}, f32[1,384]{1,0:T(1,128)S(1)}, u32[]{:S(2)}, u32[]{:S(2)}) collective-permute-start(f32[1,384]{1,0:T(1,128)S(1)} %get-tuple-element.43.own_ref), channel_id=1, source_target_pairs={{0,1},{1,0},{2,3},{3,2},{4,5},{5,4},{6,7},{7,6},{8,9},{9,8},{10,11... | collective-permute-start | bytes 4616 | tf_op jit(solution)/shard_map/ppermute | solution.py:353

commit v6 on v5

--- a/solution.py
+++ b/solution.py
@@ -112,7 +112,7 @@
             use_weights(n - LAG)
 
 
-def inner_kernel(pairs, field_ref, groups_ref, out_ref, columns, values, rows_q, rows_v, rows_p, sums, weights):
+def inner_kernel(pairs, field_ref, out_ref, columns, values, rows_q, rows_v, rows_p, sums, weights):
     @pl.loop(0, 16)
     def _(s):
         build_group([field_ref[s, c] for c in range(3)], rows_q, rows_v, columns, values, s * ROWS)
@@ -210,23 +210,17 @@
         part_ref[:, c * LANES:(c + 1) * LANES] = jnp.sum(both, axis=0, keepdims=True)
 
 
+def fetch_kernel(pairs_ref, groups_ref, pairs_out, groups_out):
+    pairs_out[...] = pairs_ref[...]
+    groups_out[...] = groups_ref[...]
+
+
 def spread_kernel(own_ref, *refs):
     others, out_ref = refs[:-1], refs[-1]
     total = own_ref[...]
     for ref in others:
         total = total + ref[...]
     out_ref[...] = jnp.broadcast_to(total[None], out_ref.shape)
-
-
-def string_kernel(shares, everyone_ref, out_ref):
-    images = shares.shape[0]
-    members = everyone_ref.shape[0] // images
-    total = jnp.zeros((1, 3 * LANES), F32)
-    for i in range(images):
-        updated = jnp.sum(everyone_ref[i * members:(i + 1) * members], axis=0)
-        total = total + shares[i] * updated
-    for c in range(3):
-        out_ref[c] = total[:, c * LANES:(c + 1) * LANES]
 
 
 def pack_kernel(vel_hbm, conf_hbm, out_ref, vel_ref, conf_ref, arrived):
@@ -316,7 +310,14 @@
     got = lax.all_to_all(
         packed.reshape(16, 6, ROWS, LANES), "swarm", split_axis=0, concat_axis=0, tiled=True
     )
-    got, domain, image = lax.optimization_barrier((got, domain, image))
+    partners, groups = call(
+        fetch_kernel, "fetch",
+        (jax.ShapeDtypeStruct((2, LANES), jnp.int32), jax.ShapeDtypeStruct((GSIZE, LANES), jnp.int32)),
+        [VMEM, VMEM], [], 0, 20_000,
+    )(partners, groups)
+    got, domain, image, partners, groups = lax.optimization_barrier(
+        (got, domain, image, partners, groups)
+    )
     start_vel, start_pos = got[:, :3], got[:, 3:]
     odd = domain % 2
     place = jnp.stack([domain, odd])
@@ -326,20 +327,20 @@
         jax.ShapeDtypeStruct((128, 32, LANES), BF16), jax.ShapeDtypeStruct((128, 16, LANES), BF16)
     )
     inner = call(
-        inner_kernel, "inner", (shape(8, 3, ROWS, LANES),) + tables, [SMEM, VMEM, VMEM], ROW_SCRATCH, WORK, 0
+        inner_kernel, "inner", (shape(8, 3, ROWS, LANES),) + tables, [SMEM, VMEM], ROW_SCRATCH, WORK, 0
     )
     rim1, rim2 = swap_rims(
         lax.dynamic_slice_in_dim(start_pos, 12 * (1 - odd), 4, 0),
         lax.dynamic_slice_in_dim(start_pos, 12 * odd, 4, 0),
     )
-    inside = inner(partners, start_pos, groups)
+    inside = inner(partners, start_pos)
     middle, base, send1, send2 = call(
         first_rim_kernel, "first_rim", (whole, whole, rim, rim), [SMEM, SMEM] + [VMEM] * 7,
         ROW_SCRATCH + TABLES, WORK, 0,
     )(partners, place, start_pos, rim1, rim2, *inside, start_vel)
 
     rim1, rim2 = swap_rims(send1, send2)
-    inside = inner(partners, middle, groups)
+    inside = inner(partners, middle)
     final, part = call(
         second_rim_kernel, "second_rim", (shape(3, LANES, LANES), shape(1, 3 * LANES)),
         [SMEM, SMEM] + [VMEM] * 8, ROW_SCRATCH + TABLES, WORK, 0,
@@ -356,10 +357,8 @@
         spread_kernel, "spread", shape(images * members, 1, 3 * LANES), [VMEM] * 4, [], 0, 100_000
     )(*parts)
     everyone = lax.all_to_all(copies, ("image", "swarm"), split_axis=0, concat_axis=0, tiled=True)
-    new_string = call(
-        string_kernel, "string", shape(3, 1, LANES), [SMEM, VMEM], [], 0, 100_000
-    )(shares, everyone)
-    new_string = new_string.transpose(1, 0, 2)
+    updated = jnp.sum(everyone.reshape(images, members, 3 * LANES), axis=1)
+    new_string = jnp.sum(shares[:, None] * updated, axis=0).reshape(1, 3, LANES)
     return (final_positions, new_string)
 
 

time: 79.5 us -> 78.4 us (0.986)
  blocking collectives: 43.1 us -> 19.4 us
  starting transfers between devices: 11.2 us -> 22.8 us
  waiting for transfers between devices: 1.95 us -> 13.4 us
  Pallas kernels: 21.5 us -> 20.3 us
    all_to_all x1 -> x0, blocking collectives: 23.7 us -> none  [on_device(): lax.all_to_all(packed.reshape(16, 6, ROWS, LANES), 'swarm', split_axis=0,...]
    all_to_all x0 -> x1, starting transfers between devices: none -> 11.6 us  [on_device(): lax.all_to_all(packed.reshape(16, 6, ROWS, LANES), 'swarm', split_axis=0,...]
    all_to_all x0 -> x1, waiting for transfers between devices: none -> 11.4 us  [on_device(): lax.all_to_all(packed.reshape(16, 6, ROWS, LANES), 'swarm', split_axis=0,...]
    pallas_call x3, Pallas kernels: 10.3 us -> 9.13 us  [the longest x1 4.57 us: on_device(): inside = inner(partners, middle)]
  transfers between devices with their start and end apart: 7 -> 8, of which waited for: 2 -> 3; matrix products, arithmetic and copies ran while one was open for 0% -> 0% of each run, Pallas kernels for 12% -> 12%
where the time goes in v6:
time: 78.4 us; the launch traced here: 78.1 us
  starting transfers between devices  22.8 us (29%)
  Pallas kernels  20.3 us (26%)
  blocking collectives  19.4 us (25%)
  waiting for transfers between devices  13.4 us (17%)
  local copies, waits for them, and re-layouts  1.3 us (2%)
    all_to_all x1, blocking collectives, on_device(): lax.all_to_all(copies, ('image', 'swarm'), split_axis=0, concat_axis=0, t...  19.4 us
    all_to_all x1, starting transfers between devices, on_device(): lax.all_to_all(packed.reshape(16, 6, ROWS, LANES), 'swarm', split_axis=0,...  11.6 us
    all_to_all x1, waiting for transfers between devices, on_device(): lax.all_to_all(packed.reshape(16, 6, ROWS, LANES), 'swarm', split_axis=0,...  11.4 us
    ppermute x2, starting transfers between devices, swap_rims(): lax.ppermute(second, 'domain', across)  8.19 us
    pallas_call x1, Pallas kernels, on_device(): call(second_rim_kernel, 'second_rim', (shape(3, LANES, LANES), shape(1, 3...  5.11 us
    pallas_call x1, Pallas kernels, on_device(): inside = inner(partners, middle)  4.57 us
    pallas_call x1, Pallas kernels, on_device(): inside = inner(partners, start_pos)  4.56 us
    pallas_call x1, Pallas kernels, on_device(): call(first_rim_kernel, 'first_rim', (whole, whole, rim, rim), [SMEM, SMEM...  4.32 us
  transfers between devices with their start and end apart: 8, of which 3 were waited for; matrix products, arithmetic and copies ran while one was open for 0% of the time, Pallas kernels for 12%

profile of v6, /device:TPU:1, one launch (start us, length us, event | category | flops | bytes accessed | tf_op | source)
XLA Modules:
  0.0 78.1 jit_solution(12158465197036160307)
XLA Ops:
  0.6 1.7 %pack.1 = f32[768,128]{1,0:T(8,128)} custom-call(f32[3,16,1024]{2,1,0:T(8,128)} %bitcast.15, f32[3,8,128]{2,1,0:T(8,128)} %bitcast.16), custom_call_target="tpu_custom_call" | custom-call | bytes 600000 | tf_op jit(solution)/shard_map/pack/pallas_call | solution.py:301
  2.4 0.0 copy-start
  2.4 11.6 %all-to-all-start = ((f32[16,6,8,128]{3,2,1,0:T(8,128)}), f32[16,6,8,128]{3,2,1,0:T(8,128)S(1)}, u32[]{:S(2)}, u32[]{:S(2)}) async-start(f32[16,6,8,128]{3,2,1,0:T(8,128)} %bitcast.13), calls=%async_computation | async-start | bytes 786432 | tf_op jit(solution)/shard_map/all_to_all | solution.py:310
  14.0 0.0 copy-start.1
  14.0 0.0 copy-done
  14.0 0.7 copy-done.1
  14.7 11.4 %all-to-all-done = f32[16,6,8,128]{3,2,1,0:T(8,128)S(1)} async-done(((f32[16,6,8,128]{3,2,1,0:T(8,128)}), f32[16,6,8,128]{3,2,1,0:T(8,128)S(1)}, u32[]{:S(2)}, u32[]{:S(2)}) %all-to-all-start) | async-done | bytes 393248 | tf_op jit(solution)/shard_map/all_to_all | solution.py:310
  26.2 6.1 %collective-permute-start.1 = (f32[4,3,8,128]{3,2,1,0:T(8,128)S(1)}, f32[4,3,8,128]{3,2,1,0:T(8,128)S(1)}, u32[]{:S(2)}, u32[]{:S(2)}) collective-permute-start(f32[4,3,8,128]{3,2,1,0:T(8,128)S(1)} %get-tuple-element.60), channel_id=1, source_target_pairs={{1,2},{2,1},{5,6},{6,5},{9,10},{10,9},{13,14},{14,13},{17,18},{18,... | collective-permute-start | bytes 147464 | tf_op jit(solution)/shard_map/ppermute | solution.py:283
  32.3 0.1 collective-permute-start
  32.4 4.6 %inner.2 = (f32[8,3,8,128]{3,2,1,0:T(8,128)S(1)}, bf16[128,32,128]{2,1,0:T(8,128)(2,1)S(1)}, bf16[128,16,128]{2,1,0:T(8,128)(2,1)S(1)}) custom-call(s32[2,128]{1,0:T(2,128)S(1)} %get-tuple-element.33.pairs, f32[16,3,8,128]{3,2,1,0:T(8,128)S(1)} %get-tuple-element.59.field_ref), custom_call_target="tpu_custom_call" | custom-call | flops 8000000000 | tf_op jit(solution)/shard_map/inner/pallas_call | solution.py:336
  37.0 0.1 pad_add_fusion.place
  37.0 0.0 collective-permute-done.1.rim2_ref
  37.0 0.0 collective-permute-done.rim1_ref
  37.0 4.3 %first_rim.1 = (f32[16,3,8,128]{3,2,1,0:T(8,128)S(1)}, f32[16,3,8,128]{3,2,1,0:T(8,128)S(1)}, f32[4,3,8,128]{3,2,1,0:T(8,128)S(1)}, f32[4,3,8,128]{3,2,1,0:T(8,128)S(1)}) custom-call(s32[2,128]{1,0:T(2,128)S(1)} %get-tuple-element.33.pairs, s32[2]{0:T(128)S(1)} %pad_add_fusion.place, f32[16,3,8,128]{3,2,1,0:T(8,128)S(1)} %get-tuple-element.59.field_ref, ...), custom_call_target="tpu_custom_call" | custom-call | flops 8000000000 | tf_op jit(solution)/shard_map/first_rim/pallas_call | solution.py:337
  41.4 0.6 collective-permute-start.2
  42.0 2.1 %collective-permute-start.3 = (f32[4,3,8,128]{3,2,1,0:T(8,128)S(1)}, f32[4,3,8,128]{3,2,1,0:T(8,128)S(1)}, u32[]{:S(2)}, u32[]{:S(2)}) collective-permute-start(f32[4,3,8,128]{3,2,1,0:T(8,128)S(1)} %get-tuple-element.42), channel_id=1, source_target_pairs={{1,2},{2,1},{5,6},{6,5},{9,10},{10,9},{13,14},{14,13},{17,18},{18,... | collective-permute-start | bytes 147464 | tf_op jit(solution)/shard_map/ppermute | solution.py:283
  44.1 4.6 %inner.3 = (f32[8,3,8,128]{3,2,1,0:T(8,128)S(1)}, bf16[128,32,128]{2,1,0:T(8,128)(2,1)S(1)}, bf16[128,16,128]{2,1,0:T(8,128)(2,1)S(1)}) custom-call(s32[2,128]{1,0:T(2,128)S(1)} %get-tuple-element.33.pairs, f32[16,3,8,128]{3,2,1,0:T(8,128)S(1)} %get-tuple-element.40.field_ref), custom_call_target="tpu_custom_call" | custom-call | flops 8000000000 | tf_op jit(solution)/shard_map/inner/pallas_call | solution.py:343
  48.6 0.0 collective-permute-done.2.rim1_ref
  48.6 0.0 collective-permute-done.3.rim2_ref
  48.7 5.1 %second_rim.1 = (f32[3,128,128]{2,1,0:T(8,128)}, f32[1,384]{1,0:T(1,128)S(1)}) custom-call(s32[2,128]{1,0:T(2,128)S(1)} %get-tuple-element.33.pairs, s32[2]{0:T(128)S(1)} %pad_add_fusion.place, s32[16,128]{1,0:T(8,128)S(1)} %get-tuple-element.35.groups_ref, f32[16,3,8,128]{3,2,1,0:T(8,128)S(1)} %get-tuple-element.40.field_ref, ...), custom_call_target="tpu_custom_call" | custom-call | flops 8000000000 | tf_op jit(solution)/shard_map/second_rim/pallas_call | solution.py:344
  53.8 1.8 %collective-permute-start.6 = (f32[1,384]{1,0:T(1,128)S(1)}, f32[1,384]{1,0:T(1,128)S(1)}, u32[]{:S(2)}, u32[]{:S(2)}) collective-permute-start(f32[1,384]{1,0:T(1,128)S(1)} %get-tuple-element.51.own_ref), channel_id=1, source_target_pairs={{0,3},{1,2},{2,1},{3,0},{4,7},{5,6},{6,5},{7,4},{8,11},{9,10},{10,... | collective-permute-start | bytes 4616 | tf_op jit(solution)/shard_map/ppermute | solution.py:354
  55.6 0.0 collective-permute-start.5
  55.6 0.5 collective-permute-start.4
  56.1 0.8 collective-permute-done.6.refs_2_
  56.9 1.2 %collective-permute-done.5.refs_1_ = f32[1,384]{1,0:T(1,128)S(1)} collective-permute-done((f32[1,384]{1,0:T(1,128)S(1)}, f32[1,384]{1,0:T(1,128)S(1)}, u32[]{:S(2)}, u32[]{:S(2)}) %collective-permute-start.5) | collective-permute-done | bytes 1568 | tf_op jit(solution)/shard_map/ppermute | solution.py:354
  58.0 0.0 collective-permute-done.4.refs_0_
  58.1 19.4 %all_to_all.10 = f32[64,1,384]{2,1,0:T(1,128)S(1)} all-to-all(f32[64,1,384]{2,1,0:T(1,128)S(1)} %spread.1), channel_id=1, replica_groups=mesh['image'=4,'swarm'=16,'domain'=4] {'image','swarm'}, dimensions={0} | all-to-all | bytes 196608 | tf_op jit(solution)/shard_map/all_to_all | solution.py:359
  77.5 0.1 multiply_reduce_fusion
  77.5 0.6 reshape.28
  (7 shorter events, 0.1 us)
Async XLA Ops:
  2.4 11.6 %copy-start = (s32[128,16]{0,1:T(8,128)S(1)}, s32[128,16]{0,1:T(8,128)}, u32[]{:S(2)}) copy-start(s32[128,16]{0,1:T(8,128)} %param.7) | copy-start | bytes 24580
  2.4 23.7 %all-to-all-start = ((f32[16,6,8,128]{3,2,1,0:T(8,128)}), f32[16,6,8,128]{3,2,1,0:T(8,128)S(1)}, u32[]{:S(2)}, u32[]{:S(2)}) async-start(f32[16,6,8,128]{3,2,1,0:T(8,128)} %bitcast.13), calls=%async_computation | async-start | bytes 786432 | tf_op jit(solution)/shard_map/all_to_all | solution.py:310
  14.0 0.7 copy-start.1
  26.2 10.8 %collective-permute-start.1 = (f32[4,3,8,128]{3,2,1,0:T(8,128)S(1)}, f32[4,3,8,128]{3,2,1,0:T(8,128)S(1)}, u32[]{:S(2)}, u32[]{:S(2)}) collective-permute-start(f32[4,3,8,128]{3,2,1,0:T(8,128)S(1)} %get-tuple-element.60), channel_id=1, source_target_pairs={{1,2},{2,1},{5,6},{6,5},{9,10},{10,9},{13,14},{14,13},{17,18},{18,... | collective-permute-start | bytes 147464 | tf_op jit(solution)/shard_map/ppermute | solution.py:283
  32.3 4.8 %collective-permute-start = (f32[4,3,8,128]{3,2,1,0:T(8,128)S(1)}, f32[4,3,8,128]{3,2,1,0:T(8,128)S(1)}, u32[]{:S(2)}, u32[]{:S(2)}) collective-permute-start(f32[4,3,8,128]{3,2,1,0:T(8,128)S(1)} %get-tuple-element.61), channel_id=1, source_target_pairs={{0,1},{1,0},{2,3},{3,2},{4,5},{5,4},{6,7},{7,6},{8,9},{9,8},{10,11... | collective-permute-start | bytes 147464 | tf_op jit(solution)/shard_map/ppermute | solution.py:283
  41.4 7.3 %collective-permute-start.2 = (f32[4,3,8,128]{3,2,1,0:T(8,128)S(1)}, f32[4,3,8,128]{3,2,1,0:T(8,128)S(1)}, u32[]{:S(2)}, u32[]{:S(2)}) collective-permute-start(f32[4,3,8,128]{3,2,1,0:T(8,128)S(1)} %get-tuple-element.41), channel_id=1, source_target_pairs={{0,1},{1,0},{2,3},{3,2},{4,5},{5,4},{6,7},{7,6},{8,9},{9,8},{10,11... | collective-permute-start | bytes 147464 | tf_op jit(solution)/shard_map/ppermute | solution.py:283
  42.0 6.7 %collective-permute-start.3 = (f32[4,3,8,128]{3,2,1,0:T(8,128)S(1)}, f32[4,3,8,128]{3,2,1,0:T(8,128)S(1)}, u32[]{:S(2)}, u32[]{:S(2)}) collective-permute-start(f32[4,3,8,128]{3,2,1,0:T(8,128)S(1)} %get-tuple-element.42), channel_id=1, source_target_pairs={{1,2},{2,1},{5,6},{6,5},{9,10},{10,9},{13,14},{14,13},{17,18},{18,... | collective-permute-start | bytes 147464 | tf_op jit(solution)/shard_map/ppermute | solution.py:283
  53.8 3.1 %collective-permute-start.6 = (f32[1,384]{1,0:T(1,128)S(1)}, f32[1,384]{1,0:T(1,128)S(1)}, u32[]{:S(2)}, u32[]{:S(2)}) collective-permute-start(f32[1,384]{1,0:T(1,128)S(1)} %get-tuple-element.51.own_ref), channel_id=1, source_target_pairs={{0,3},{1,2},{2,1},{3,0},{4,7},{5,6},{6,5},{7,4},{8,11},{9,10},{10,... | collective-permute-start | bytes 4616 | tf_op jit(solution)/shard_map/ppermute | solution.py:354
  55.6 2.4 %collective-permute-start.5 = (f32[1,384]{1,0:T(1,128)S(1)}, f32[1,384]{1,0:T(1,128)S(1)}, u32[]{:S(2)}, u32[]{:S(2)}) collective-permute-start(f32[1,384]{1,0:T(1,128)S(1)} %get-tuple-element.51.own_ref), channel_id=1, source_target_pairs={{0,2},{1,3},{2,0},{3,1},{4,6},{5,7},{6,4},{7,5},{8,10},{9,11},{10,... | collective-permute-start | bytes 4616 | tf_op jit(solution)/shard_map/ppermute | solution.py:354
  55.6 2.4 %collective-permute-start.4 = (f32[1,384]{1,0:T(1,128)S(1)}, f32[1,384]{1,0:T(1,128)S(1)}, u32[]{:S(2)}, u32[]{:S(2)}) collective-permute-start(f32[1,384]{1,0:T(1,128)S(1)} %get-tuple-element.51.own_ref), channel_id=1, source_target_pairs={{0,1},{1,0},{2,3},{3,2},{4,5},{5,4},{6,7},{7,6},{8,9},{9,8},{10,11... | collective-permute-start | bytes 4616 | tf_op jit(solution)/shard_map/ppermute | solution.py:354

commit v7 on v6

--- a/solution.py
+++ b/solution.py
@@ -133,14 +133,15 @@
         for whole, own in ((columns, own_tables[0]), (values, own_tables[1])):
             whole[pl.ds(HALO // LANES + s * ROWS, ROWS)] = own[pl.ds(s * ROWS, ROWS)]
 
-    odd = place[1]
-    for ref, first in ((rim_refs[0], 20 * (1 - odd)), (rim_refs[1], 20 * odd)):
+    odd, second = place[1], place[2] > 0
+    for ref, first, exists in ((rim_refs[0], 20 * (1 - odd), None), (rim_refs[1], 20 * odd, second)):
 
         @pl.loop(0, 4)
         def _(s):
-            build_group(
-                [ref[s, c] for c in range(3)], rows_q, rows_v, columns, values, (first + s) * ROWS
-            )
+            field = [ref[s, c] for c in range(3)]
+            if exists is not None:
+                field = [jnp.where(exists, x, 0.0) for x in field]
+            build_group(field, rows_q, rows_v, columns, values, (first + s) * ROWS)
 
     forces(
         (0, 1, 2, 3, 12, 13, 14, 15), field_ref, 0, pairs, rows_p, sums, weights, columns, values, emit
@@ -279,7 +280,7 @@
 def swap_rims(first, second):
     count = lax.axis_size("domain")
     inside = [(i, i ^ 1) for i in range(count)]
-    across = [(i, j) for i in range(count) for j in [i + 1 if i % 2 else i - 1] if 0 <= j < count]
+    across = [(i, (i + 1 if i % 2 else i - 1) % count) for i in range(count)]
     return lax.ppermute(first, "domain", inside), lax.ppermute(second, "domain", across)
 
 
@@ -320,7 +321,8 @@
     )
     start_vel, start_pos = got[:, :3], got[:, 3:]
     odd = domain % 2
-    place = jnp.stack([domain, odd])
+    inner_domain = (domain > 0) & (domain < lax.axis_size("domain") - 1)
+    place = jnp.stack([domain, odd, inner_domain.astype(domain.dtype)])
 
     whole, rim = shape(16, 3, ROWS, LANES), shape(4, 3, ROWS, LANES)
     tables = (

time: 78.4 us -> 74.4 us (0.949)
  starting transfers between devices: 22.8 us -> 19.5 us
    ppermute x2, starting transfers between devices: 8.19 us -> 5.09 us  [swap_rims(): lax.ppermute(second, 'domain', across)]
where the time goes in v7:
time: 74.4 us; the launch traced here: 73.7 us
  Pallas kernels  20.3 us (27%)
  starting transfers between devices  19.5 us (26%)
  blocking collectives  19 us (26%)
  waiting for transfers between devices  12.7 us (17%)
  local copies, waits for them, and re-layouts  1.3 us (2%)
  between operations  0.76 us (1%)
    all_to_all x1, blocking collectives, on_device(): lax.all_to_all(copies, ('image', 'swarm'), split_axis=0, concat_axis=0, t...  19 us
    all_to_all x1, starting transfers between devices, on_device(): lax.all_to_all(packed.reshape(16, 6, ROWS, LANES), 'swarm', split_axis=0,...  11.6 us
    all_to_all x1, waiting for transfers between devices, on_device(): lax.all_to_all(packed.reshape(16, 6, ROWS, LANES), 'swarm', split_axis=0,...  11.4 us
    pallas_call x1, Pallas kernels, on_device(): call(second_rim_kernel, 'second_rim', (shape(3, LANES, LANES), shape(1, 3...  5.1 us
    ppermute x2, starting transfers between devices, swap_rims(): lax.ppermute(second, 'domain', across)  5.09 us
    pallas_call x1, Pallas kernels, on_device(): inside = inner(partners, middle)  4.57 us
    pallas_call x1, Pallas kernels, on_device(): inside = inner(partners, start_pos)  4.56 us
    pallas_call x1, Pallas kernels, on_device(): call(first_rim_kernel, 'first_rim', (whole, whole, rim, rim), [SMEM, SMEM...  4.33 us
  transfers between devices with their start and end apart: 8, of which 3 were waited for; matrix products, arithmetic and copies ran while one was open for 0% of the time, Pallas kernels for 12%

profile of v7, /device:TPU:1, one launch (start us, length us, event | category | flops | bytes accessed | tf_op | source)
XLA Modules:
  0.0 73.7 jit_solution(11288478293576519589)
XLA Ops:
  0.6 1.7 %pack.1 = f32[768,128]{1,0:T(8,128)} custom-call(f32[3,16,1024]{2,1,0:T(8,128)} %bitcast.16, f32[3,8,128]{2,1,0:T(8,128)} %bitcast.17), custom_call_target="tpu_custom_call" | custom-call | bytes 600000 | tf_op jit(solution)/shard_map/pack/pallas_call | solution.py:302
  2.4 0.0 copy-start
  2.4 11.6 %all-to-all-start = ((f32[16,6,8,128]{3,2,1,0:T(8,128)}), f32[16,6,8,128]{3,2,1,0:T(8,128)S(1)}, u32[]{:S(2)}, u32[]{:S(2)}) async-start(f32[16,6,8,128]{3,2,1,0:T(8,128)} %bitcast.14), calls=%async_computation | async-start | bytes 786432 | tf_op jit(solution)/shard_map/all_to_all | solution.py:311
  14.0 0.0 copy-start.1
  14.0 0.0 copy-done
  14.0 0.7 copy-done.1
  14.7 11.4 %all-to-all-done = f32[16,6,8,128]{3,2,1,0:T(8,128)S(1)} async-done(((f32[16,6,8,128]{3,2,1,0:T(8,128)}), f32[16,6,8,128]{3,2,1,0:T(8,128)S(1)}, u32[]{:S(2)}, u32[]{:S(2)}) %all-to-all-start) | async-done | bytes 393248 | tf_op jit(solution)/shard_map/all_to_all | solution.py:311
  26.2 4.3 %collective-permute-start.1 = (f32[4,3,8,128]{3,2,1,0:T(8,128)S(1)}, f32[4,3,8,128]{3,2,1,0:T(8,128)S(1)}, u32[]{:S(2)}, u32[]{:S(2)}) collective-permute-start(f32[4,3,8,128]{3,2,1,0:T(8,128)S(1)} %get-tuple-element.60), channel_id=1, source_target_pairs={{0,3},{1,2},{2,1},{3,0},{4,7},{5,6},{6,5},{7,4},{8,11},{9,10},{10,... | collective-permute-start | bytes 147464 | tf_op jit(solution)/shard_map/ppermute | solution.py:284
  30.5 0.0 collective-permute-start
  30.5 4.6 %inner.2 = (f32[8,3,8,128]{3,2,1,0:T(8,128)S(1)}, bf16[128,32,128]{2,1,0:T(8,128)(2,1)S(1)}, bf16[128,16,128]{2,1,0:T(8,128)(2,1)S(1)}) custom-call(s32[2,128]{1,0:T(2,128)S(1)} %get-tuple-element.33.pairs, f32[16,3,8,128]{3,2,1,0:T(8,128)S(1)} %get-tuple-element.59.field_ref), custom_call_target="tpu_custom_call" | custom-call | flops 8000000000 | tf_op jit(solution)/shard_map/inner/pallas_call | solution.py:338
  35.0 0.1 pad_add_fusion.place
  35.1 0.0 collective-permute-done.1.rim2_ref
  35.1 0.0 collective-permute-done.rim1_ref
  35.1 4.3 %first_rim.1 = (f32[16,3,8,128]{3,2,1,0:T(8,128)S(1)}, f32[16,3,8,128]{3,2,1,0:T(8,128)S(1)}, f32[4,3,8,128]{3,2,1,0:T(8,128)S(1)}, f32[4,3,8,128]{3,2,1,0:T(8,128)S(1)}) custom-call(s32[2,128]{1,0:T(2,128)S(1)} %get-tuple-element.33.pairs, s32[3]{0:T(128)S(1)} %pad_add_fusion.place, f32[16,3,8,128]{3,2,1,0:T(8,128)S(1)} %get-tuple-element.59.field_ref, ...), custom_call_target="tpu_custom_call" | custom-call | flops 8000000000 | tf_op jit(solution)/shard_map/first_rim/pallas_call | solution.py:339
  39.5 0.6 collective-permute-start.2
  40.0 0.8 %collective-permute-start.3 = (f32[4,3,8,128]{3,2,1,0:T(8,128)S(1)}, f32[4,3,8,128]{3,2,1,0:T(8,128)S(1)}, u32[]{:S(2)}, u32[]{:S(2)}) collective-permute-start(f32[4,3,8,128]{3,2,1,0:T(8,128)S(1)} %get-tuple-element.42), channel_id=1, source_target_pairs={{0,3},{1,2},{2,1},{3,0},{4,7},{5,6},{6,5},{7,4},{8,11},{9,10},{10,... | collective-permute-start | bytes 147464 | tf_op jit(solution)/shard_map/ppermute | solution.py:284
  40.9 4.6 %inner.3 = (f32[8,3,8,128]{3,2,1,0:T(8,128)S(1)}, bf16[128,32,128]{2,1,0:T(8,128)(2,1)S(1)}, bf16[128,16,128]{2,1,0:T(8,128)(2,1)S(1)}) custom-call(s32[2,128]{1,0:T(2,128)S(1)} %get-tuple-element.33.pairs, f32[16,3,8,128]{3,2,1,0:T(8,128)S(1)} %get-tuple-element.40.field_ref), custom_call_target="tpu_custom_call" | custom-call | flops 8000000000 | tf_op jit(solution)/shard_map/inner/pallas_call | solution.py:345
  45.5 0.0 collective-permute-done.2.rim1_ref
  45.5 0.0 collective-permute-done.3.rim2_ref
  45.5 5.1 %second_rim.1 = (f32[3,128,128]{2,1,0:T(8,128)}, f32[1,384]{1,0:T(1,128)S(1)}) custom-call(s32[2,128]{1,0:T(2,128)S(1)} %get-tuple-element.33.pairs, s32[3]{0:T(128)S(1)} %pad_add_fusion.place, s32[16,128]{1,0:T(8,128)S(1)} %get-tuple-element.35.groups_ref, f32[16,3,8,128]{3,2,1,0:T(8,128)S(1)} %get-tuple-element.40.field_ref, ...), custom_call_target="tpu_custom_call" | custom-call | flops 8000000000 | tf_op jit(solution)/shard_map/second_rim/pallas_call | solution.py:346
  50.6 1.0 %collective-permute-start.6 = (f32[1,384]{1,0:T(1,128)S(1)}, f32[1,384]{1,0:T(1,128)S(1)}, u32[]{:S(2)}, u32[]{:S(2)}) collective-permute-start(f32[1,384]{1,0:T(1,128)S(1)} %get-tuple-element.51.own_ref), channel_id=1, source_target_pairs={{0,3},{1,2},{2,1},{3,0},{4,7},{5,6},{6,5},{7,4},{8,11},{9,10},{10,... | collective-permute-start | bytes 4616 | tf_op jit(solution)/shard_map/ppermute | solution.py:356
  51.6 0.7 collective-permute-start.5
  52.2 0.6 collective-permute-start.4
  52.8 0.9 %collective-permute-done.6.refs_2_ = f32[1,384]{1,0:T(1,128)S(1)} collective-permute-done((f32[1,384]{1,0:T(1,128)S(1)}, f32[1,384]{1,0:T(1,128)S(1)}, u32[]{:S(2)}, u32[]{:S(2)}) %collective-permute-start.6) | collective-permute-done | bytes 1568 | tf_op jit(solution)/shard_map/ppermute | solution.py:356
  53.7 0.3 collective-permute-done.5.refs_1_
  54.0 0.0 collective-permute-done.4.refs_0_
  54.0 19.0 %all_to_all.10 = f32[64,1,384]{2,1,0:T(1,128)S(1)} all-to-all(f32[64,1,384]{2,1,0:T(1,128)S(1)} %spread.1), channel_id=1, replica_groups=mesh['image'=4,'swarm'=16,'domain'=4] {'image','swarm'}, dimensions={0} | all-to-all | bytes 196608 | tf_op jit(solution)/shard_map/all_to_all | solution.py:361
  73.1 0.1 multiply_reduce_fusion
  73.1 0.6 reshape.28
  (7 shorter events, 0.1 us)
Async XLA Ops:
  2.4 11.6 %copy-start = (s32[128,16]{0,1:T(8,128)S(1)}, s32[128,16]{0,1:T(8,128)}, u32[]{:S(2)}) copy-start(s32[128,16]{0,1:T(8,128)} %param.7) | copy-start | bytes 24580
  2.4 23.7 %all-to-all-start = ((f32[16,6,8,128]{3,2,1,0:T(8,128)}), f32[16,6,8,128]{3,2,1,0:T(8,128)S(1)}, u32[]{:S(2)}, u32[]{:S(2)}) async-start(f32[16,6,8,128]{3,2,1,0:T(8,128)} %bitcast.14), calls=%async_computation | async-start | bytes 786432 | tf_op jit(solution)/shard_map/all_to_all | solution.py:311
  14.0 0.7 copy-start.1
  26.2 8.9 %collective-permute-start.1 = (f32[4,3,8,128]{3,2,1,0:T(8,128)S(1)}, f32[4,3,8,128]{3,2,1,0:T(8,128)S(1)}, u32[]{:S(2)}, u32[]{:S(2)}) collective-permute-start(f32[4,3,8,128]{3,2,1,0:T(8,128)S(1)} %get-tuple-element.60), channel_id=1, source_target_pairs={{0,3},{1,2},{2,1},{3,0},{4,7},{5,6},{6,5},{7,4},{8,11},{9,10},{10,... | collective-permute-start | bytes 147464 | tf_op jit(solution)/shard_map/ppermute | solution.py:284
  30.5 4.7 %collective-permute-start = (f32[4,3,8,128]{3,2,1,0:T(8,128)S(1)}, f32[4,3,8,128]{3,2,1,0:T(8,128)S(1)}, u32[]{:S(2)}, u32[]{:S(2)}) collective-permute-start(f32[4,3,8,128]{3,2,1,0:T(8,128)S(1)} %get-tuple-element.61), channel_id=1, source_target_pairs={{0,1},{1,0},{2,3},{3,2},{4,5},{5,4},{6,7},{7,6},{8,9},{9,8},{10,11... | collective-permute-start | bytes 147464 | tf_op jit(solution)/shard_map/ppermute | solution.py:284
  39.5 6.0 %collective-permute-start.2 = (f32[4,3,8,128]{3,2,1,0:T(8,128)S(1)}, f32[4,3,8,128]{3,2,1,0:T(8,128)S(1)}, u32[]{:S(2)}, u32[]{:S(2)}) collective-permute-start(f32[4,3,8,128]{3,2,1,0:T(8,128)S(1)} %get-tuple-element.41), channel_id=1, source_target_pairs={{0,1},{1,0},{2,3},{3,2},{4,5},{5,4},{6,7},{7,6},{8,9},{9,8},{10,11... | collective-permute-start | bytes 147464 | tf_op jit(solution)/shard_map/ppermute | solution.py:284
  40.0 5.4 %collective-permute-start.3 = (f32[4,3,8,128]{3,2,1,0:T(8,128)S(1)}, f32[4,3,8,128]{3,2,1,0:T(8,128)S(1)}, u32[]{:S(2)}, u32[]{:S(2)}) collective-permute-start(f32[4,3,8,128]{3,2,1,0:T(8,128)S(1)} %get-tuple-element.42), channel_id=1, source_target_pairs={{0,3},{1,2},{2,1},{3,0},{4,7},{5,6},{6,5},{7,4},{8,11},{9,10},{10,... | collective-permute-start | bytes 147464 | tf_op jit(solution)/shard_map/ppermute | solution.py:284
  50.6 3.1 %collective-permute-start.6 = (f32[1,384]{1,0:T(1,128)S(1)}, f32[1,384]{1,0:T(1,128)S(1)}, u32[]{:S(2)}, u32[]{:S(2)}) collective-permute-start(f32[1,384]{1,0:T(1,128)S(1)} %get-tuple-element.51.own_ref), channel_id=1, source_target_pairs={{0,3},{1,2},{2,1},{3,0},{4,7},{5,6},{6,5},{7,4},{8,11},{9,10},{10,... | collective-permute-start | bytes 4616 | tf_op jit(solution)/shard_map/ppermute | solution.py:356
  51.6 2.4 %collective-permute-start.5 = (f32[1,384]{1,0:T(1,128)S(1)}, f32[1,384]{1,0:T(1,128)S(1)}, u32[]{:S(2)}, u32[]{:S(2)}) collective-permute-start(f32[1,384]{1,0:T(1,128)S(1)} %get-tuple-element.51.own_ref), channel_id=1, source_target_pairs={{0,2},{1,3},{2,0},{3,1},{4,6},{5,7},{6,4},{7,5},{8,10},{9,11},{10,... | collective-permute-start | bytes 4616 | tf_op jit(solution)/shard_map/ppermute | solution.py:356
  52.2 1.8 %collective-permute-start.4 = (f32[1,384]{1,0:T(1,128)S(1)}, f32[1,384]{1,0:T(1,128)S(1)}, u32[]{:S(2)}, u32[]{:S(2)}) collective-permute-start(f32[1,384]{1,0:T(1,128)S(1)} %get-tuple-element.51.own_ref), channel_id=1, source_target_pairs={{0,1},{1,0},{2,3},{3,2},{4,5},{5,4},{6,7},{7,6},{8,9},{9,8},{10,11... | collective-permute-start | bytes 4616 | tf_op jit(solution)/shard_map/ppermute | solution.py:356

commit v8 on v7

--- a/solution.py
+++ b/solution.py
@@ -216,12 +216,8 @@
     groups_out[...] = groups_ref[...]
 
 
-def spread_kernel(own_ref, *refs):
-    others, out_ref = refs[:-1], refs[-1]
-    total = own_ref[...]
-    for ref in others:
-        total = total + ref[...]
-    out_ref[...] = jnp.broadcast_to(total[None], out_ref.shape)
+def spread_kernel(own_ref, out_ref):
+    out_ref[...] = jnp.broadcast_to(own_ref[...][None], out_ref.shape)
 
 
 def pack_kernel(vel_hbm, conf_hbm, out_ref, vel_ref, conf_ref, arrived):
@@ -285,12 +281,9 @@
 
 
 def string_shares(place):
-    images = lax.axis_size("image")
-    ids = jnp.arange(images)
-    neighbours = (place > 0).astype(F32) + (place < images - 1).astype(F32)
-    return jnp.where(jnp.abs(ids - place) == 1, smoothing, 0.0) + jnp.where(
-        ids == place, 1.0 - smoothing * neighbours, 0.0
-    )
+    before = (place > 0).astype(F32) * smoothing
+    after = (place < lax.axis_size("image") - 1).astype(F32) * smoothing
+    return jnp.stack([1.0 - before - after, before, after])
 
 
 def on_device(configuration, velocities, pairs, cv_atoms):
@@ -352,15 +345,17 @@
     part, shares = lax.optimization_barrier((part, shares))
     final_positions = final.reshape(1, 1, 3, 1, LANES * LANES)
 
-    parts = [part] + [
-        lax.ppermute(part, "domain", [(i, i ^ offset) for i in range(4)]) for offset in (1, 2, 3)
-    ]
+    domains = lax.axis_size("domain")
     copies = call(
-        spread_kernel, "spread", shape(images * members, 1, 3 * LANES), [VMEM] * 4, [], 0, 100_000
-    )(*parts)
-    everyone = lax.all_to_all(copies, ("image", "swarm"), split_axis=0, concat_axis=0, tiled=True)
-    updated = jnp.sum(everyone.reshape(images, members, 3 * LANES), axis=1)
-    new_string = jnp.sum(shares[:, None] * updated, axis=0).reshape(1, 3, LANES)
+        spread_kernel, "spread", shape(members * domains, 1, 3 * LANES), [VMEM], [], 0, 100_000
+    )(part)
+    everyone = lax.all_to_all(copies, ("swarm", "domain"), split_axis=0, concat_axis=0, tiled=True)
+    updated = jnp.sum(everyone, axis=0)
+    up = [(i, (i + 1) % images) for i in range(images)]
+    earlier = lax.ppermute(updated, "image", up)
+    later = lax.ppermute(updated, "image", [(target, source) for source, target in up])
+    new_string = shares[0] * updated + shares[1] * earlier + shares[2] * later
+    new_string = new_string.reshape(1, 3, LANES)
     return (final_positions, new_string)
 
 

time: 74.4 us -> 73.1 us (0.983)
  blocking collectives: 19 us -> 15.5 us
  other arithmetic: 0.2 us -> 2.62 us
  waiting for transfers between devices: 12.7 us -> 11.7 us
    all_to_all x1, blocking collectives: 19 us -> 15.5 us  [on_device(): lax.all_to_all(copies, ('swarm', 'domain'), split_axis=0, concat_axis=0,...]
    reshape x0 -> x1, other arithmetic: none -> 2.36 us  [on_device(): new_string = new_string.reshape(1, 3, LANES)]
    ppermute x3 -> x2, waiting for transfers between devices: 1.21 us -> 0.3 us  [the longest x1 0.27 us: on_device(): earlier = lax.ppermute(updated, 'image', up)]
    ppermute x3 -> x2, starting transfers between devices: 2.23 us -> 2.9 us  [the longest x1 1.53 us: on_device(): lax.ppermute(updated, 'image', [(target, source) for source, target in up])]
  transfers between devices with their start and end apart: 8 -> 7, of which waited for: 3 -> 2; matrix products, arithmetic and copies ran while one was open for 0% -> 1% of each run, Pallas kernels for 12% -> 13%
where the time goes in v8:
time: 73.1 us; the launch traced here: 72.5 us
  Pallas kernels  20.4 us (28%)
  starting transfers between devices  20.2 us (28%)
  blocking collectives  15.5 us (21%)
  waiting for transfers between devices  11.7 us (16%)
  other arithmetic  2.62 us (4%)
  local copies, waits for them, and re-layouts  1.32 us (2%)
  between operations  0.77 us (1%)
    all_to_all x1, blocking collectives, on_device(): lax.all_to_all(copies, ('swarm', 'domain'), split_axis=0, concat_axis=0,...  15.5 us
    all_to_all x1, starting transfers between devices, on_device(): lax.all_to_all(packed.reshape(16, 6, ROWS, LANES), 'swarm', split_axis=0,...  11.6 us
    all_to_all x1, waiting for transfers between devices, on_device(): lax.all_to_all(packed.reshape(16, 6, ROWS, LANES), 'swarm', split_axis=0,...  11.4 us
    pallas_call x1, Pallas kernels, on_device(): call(second_rim_kernel, 'second_rim', (shape(3, LANES, LANES), shape(1, 3...  5.13 us
    ppermute x2, starting transfers between devices, swap_rims(): lax.ppermute(second, 'domain', across)  5.09 us
    pallas_call x1, Pallas kernels, on_device(): inside = inner(partners, middle)  4.57 us
    pallas_call x1, Pallas kernels, on_device(): inside = inner(partners, start_pos)  4.57 us
    pallas_call x1, Pallas kernels, on_device(): call(first_rim_kernel, 'first_rim', (whole, whole, rim, rim), [SMEM, SMEM...  4.33 us
  transfers between devices with their start and end apart: 7, of which 2 were waited for; matrix products, arithmetic and copies ran while one was open for 1% of the time, Pallas kernels for 13%

profile of v8, /device:TPU:1, one launch (start us, length us, event | category | flops | bytes accessed | tf_op | source)
XLA Modules:
  0.0 72.5 jit_solution(17377526472962467297)
XLA Ops:
  0.6 1.7 %pack.1 = f32[768,128]{1,0:T(8,128)} custom-call(f32[3,16,1024]{2,1,0:T(8,128)} %bitcast.22, f32[3,8,128]{2,1,0:T(8,128)} %bitcast.23), custom_call_target="tpu_custom_call" | custom-call | bytes 600000 | tf_op jit(solution)/shard_map/pack/pallas_call | solution.py:295
  2.4 0.0 copy-start
  2.4 11.6 %all-to-all-start = ((f32[16,6,8,128]{3,2,1,0:T(8,128)}), f32[16,6,8,128]{3,2,1,0:T(8,128)S(1)}, u32[]{:S(2)}, u32[]{:S(2)}) async-start(f32[16,6,8,128]{3,2,1,0:T(8,128)} %bitcast.21), calls=%async_computation | async-start | bytes 786432 | tf_op jit(solution)/shard_map/all_to_all | solution.py:304
  14.0 0.0 copy-start.1
  14.0 0.0 copy-done
  14.0 0.7 copy-done.1
  14.7 11.4 %all-to-all-done = f32[16,6,8,128]{3,2,1,0:T(8,128)S(1)} async-done(((f32[16,6,8,128]{3,2,1,0:T(8,128)}), f32[16,6,8,128]{3,2,1,0:T(8,128)S(1)}, u32[]{:S(2)}, u32[]{:S(2)}) %all-to-all-start) | async-done | bytes 393248 | tf_op jit(solution)/shard_map/all_to_all | solution.py:304
  26.2 4.3 %collective-permute-start.1 = (f32[4,3,8,128]{3,2,1,0:T(8,128)S(1)}, f32[4,3,8,128]{3,2,1,0:T(8,128)S(1)}, u32[]{:S(2)}, u32[]{:S(2)}) collective-permute-start(f32[4,3,8,128]{3,2,1,0:T(8,128)S(1)} %get-tuple-element.58), channel_id=1, source_target_pairs={{0,3},{1,2},{2,1},{3,0},{4,7},{5,6},{6,5},{7,4},{8,11},{9,10},{10,... | collective-permute-start | bytes 147464 | tf_op jit(solution)/shard_map/ppermute | solution.py:280
  30.5 0.0 collective-permute-start
  30.5 4.6 %inner.2 = (f32[8,3,8,128]{3,2,1,0:T(8,128)S(1)}, bf16[128,32,128]{2,1,0:T(8,128)(2,1)S(1)}, bf16[128,16,128]{2,1,0:T(8,128)(2,1)S(1)}) custom-call(s32[2,128]{1,0:T(2,128)S(1)} %get-tuple-element.33.pairs, f32[16,3,8,128]{3,2,1,0:T(8,128)S(1)} %get-tuple-element.57.field_ref), custom_call_target="tpu_custom_call" | custom-call | flops 8000000000 | tf_op jit(solution)/shard_map/inner/pallas_call | solution.py:331
  35.0 0.1 maximum_multiply_fusion
  35.1 0.1 pad_add_fusion.place
  35.2 0.0 collective-permute-done.1.rim2_ref
  35.2 0.0 collective-permute-done.rim1_ref
  35.2 4.3 %first_rim.1 = (f32[16,3,8,128]{3,2,1,0:T(8,128)S(1)}, f32[16,3,8,128]{3,2,1,0:T(8,128)S(1)}, f32[4,3,8,128]{3,2,1,0:T(8,128)S(1)}, f32[4,3,8,128]{3,2,1,0:T(8,128)S(1)}) custom-call(s32[2,128]{1,0:T(2,128)S(1)} %get-tuple-element.33.pairs, s32[3]{0:T(128)S(1)} %pad_add_fusion.place, f32[16,3,8,128]{3,2,1,0:T(8,128)S(1)} %get-tuple-element.57.field_ref, ...), custom_call_target="tpu_custom_call" | custom-call | flops 8000000000 | tf_op jit(solution)/shard_map/first_rim/pallas_call | solution.py:332
  39.5 0.6 collective-permute-start.2
  40.1 0.8 %collective-permute-start.3 = (f32[4,3,8,128]{3,2,1,0:T(8,128)S(1)}, f32[4,3,8,128]{3,2,1,0:T(8,128)S(1)}, u32[]{:S(2)}, u32[]{:S(2)}) collective-permute-start(f32[4,3,8,128]{3,2,1,0:T(8,128)S(1)} %get-tuple-element.42), channel_id=1, source_target_pairs={{0,3},{1,2},{2,1},{3,0},{4,7},{5,6},{6,5},{7,4},{8,11},{9,10},{10,... | collective-permute-start | bytes 147464 | tf_op jit(solution)/shard_map/ppermute | solution.py:280
  41.0 4.6 %inner.3 = (f32[8,3,8,128]{3,2,1,0:T(8,128)S(1)}, bf16[128,32,128]{2,1,0:T(8,128)(2,1)S(1)}, bf16[128,16,128]{2,1,0:T(8,128)(2,1)S(1)}) custom-call(s32[2,128]{1,0:T(2,128)S(1)} %get-tuple-element.33.pairs, f32[16,3,8,128]{3,2,1,0:T(8,128)S(1)} %get-tuple-element.40.field_ref), custom_call_target="tpu_custom_call" | custom-call | flops 8000000000 | tf_op jit(solution)/shard_map/inner/pallas_call | solution.py:338
  45.5 0.0 collective-permute-done.2.rim1_ref
  45.5 0.0 collective-permute-done.3.rim2_ref
  45.6 5.1 %second_rim.1 = (f32[3,128,128]{2,1,0:T(8,128)}, f32[1,384]{1,0:T(1,128)S(1)}) custom-call(s32[2,128]{1,0:T(2,128)S(1)} %get-tuple-element.33.pairs, s32[3]{0:T(128)S(1)} %pad_add_fusion.place, s32[16,128]{1,0:T(8,128)S(1)} %get-tuple-element.35.groups_ref, f32[16,3,8,128]{3,2,1,0:T(8,128)S(1)} %get-tuple-element.40.field_ref, ...), custom_call_target="tpu_custom_call" | custom-call | flops 8000000000 | tf_op jit(solution)/shard_map/second_rim/pallas_call | solution.py:339
  50.7 15.5 %all_to_all.10 = f32[64,1,384]{2,1,0:T(1,128)S(1)} all-to-all(f32[64,1,384]{2,1,0:T(1,128)S(1)} %spread.1), channel_id=1, replica_groups=mesh['image'=4,'swarm'=16,'domain'=4] {'swarm','domain'}, dimensions={0} | all-to-all | bytes 196608 | tf_op jit(solution)/shard_map/all_to_all | solution.py:352
  66.3 0.1 reduce_sum.11
  66.4 1.4 %collective-permute-start.4 = (f32[1,384]{1,0:T(1,128)S(1)}, f32[1,384]{1,0:T(1,128)S(1)}, u32[]{:S(2)}, u32[]{:S(2)}) collective-permute-start(f32[1,384]{1,0:T(1,128)S(1)} %reduce_sum.12), channel_id=1, source_target_pairs={{0,64},{64,128},{128,192},{192,0},{1,65},{65,129},{129,193},{193,1... | collective-permute-start | bytes 4616 | tf_op jit(solution)/shard_map/ppermute | solution.py:355
  67.7 1.5 %collective-permute-start.5 = (f32[1,384]{1,0:T(1,128)S(1)}, f32[1,384]{1,0:T(1,128)S(1)}, u32[]{:S(2)}, u32[]{:S(2)}) collective-permute-start(f32[1,384]{1,0:T(1,128)S(1)} %reduce_sum.12), channel_id=1, source_target_pairs={{64,0},{128,64},{192,128},{0,192},{65,1},{129,65},{193,129},{1,193... | collective-permute-start | bytes 4616 | tf_op jit(solution)/shard_map/ppermute | solution.py:356
  69.3 0.6 fusion.1
  69.9 0.3 collective-permute-done.4
  70.1 0.0 collective-permute-done.5
  70.2 2.4 %add_bitcast_fusion = f32[1,3,128]{2,0,1:T(1,128)} fusion(f32[1,384]{1,0:T(1,128)S(1)} %collective-permute-done.5, f32[1,384]{1,0:T(1,128)S(1)} %collective-permute-done.4, f32[]{:T(128)} %bitcast.15, f32[]{:T(128)} %bitcast.14, f32[]{:T(128)} %bitcast.13, f32[384]{0:T(512)S(1)} %reduce_sum.11), kind=kLoop, calls=%fused_computation | loop fusion | flops 1920 | bytes 6156 | tf_op jit(solution)/shard_map/reshape | solution.py:358
  (5 shorter events, 0.1 us)
Async XLA Ops:
  2.4 11.6 %copy-start = (s32[128,16]{0,1:T(8,128)S(1)}, s32[128,16]{0,1:T(8,128)}, u32[]{:S(2)}) copy-start(s32[128,16]{0,1:T(8,128)} %param.7) | copy-start | bytes 24580
  2.4 23.7 %all-to-all-start = ((f32[16,6,8,128]{3,2,1,0:T(8,128)}), f32[16,6,8,128]{3,2,1,0:T(8,128)S(1)}, u32[]{:S(2)}, u32[]{:S(2)}) async-start(f32[16,6,8,128]{3,2,1,0:T(8,128)} %bitcast.21), calls=%async_computation | async-start | bytes 786432 | tf_op jit(solution)/shard_map/all_to_all | solution.py:304
  14.0 0.7 copy-start.1
  26.2 9.0 %collective-permute-start.1 = (f32[4,3,8,128]{3,2,1,0:T(8,128)S(1)}, f32[4,3,8,128]{3,2,1,0:T(8,128)S(1)}, u32[]{:S(2)}, u32[]{:S(2)}) collective-permute-start(f32[4,3,8,128]{3,2,1,0:T(8,128)S(1)} %get-tuple-element.58), channel_id=1, source_target_pairs={{0,3},{1,2},{2,1},{3,0},{4,7},{5,6},{6,5},{7,4},{8,11},{9,10},{10,... | collective-permute-start | bytes 147464 | tf_op jit(solution)/shard_map/ppermute | solution.py:280
  30.5 4.7 %collective-permute-start = (f32[4,3,8,128]{3,2,1,0:T(8,128)S(1)}, f32[4,3,8,128]{3,2,1,0:T(8,128)S(1)}, u32[]{:S(2)}, u32[]{:S(2)}) collective-permute-start(f32[4,3,8,128]{3,2,1,0:T(8,128)S(1)} %get-tuple-element.59), channel_id=1, source_target_pairs={{0,1},{1,0},{2,3},{3,2},{4,5},{5,4},{6,7},{7,6},{8,9},{9,8},{10,11... | collective-permute-start | bytes 147464 | tf_op jit(solution)/shard_map/ppermute | solution.py:280
  39.5 6.0 %collective-permute-start.2 = (f32[4,3,8,128]{3,2,1,0:T(8,128)S(1)}, f32[4,3,8,128]{3,2,1,0:T(8,128)S(1)}, u32[]{:S(2)}, u32[]{:S(2)}) collective-permute-start(f32[4,3,8,128]{3,2,1,0:T(8,128)S(1)} %get-tuple-element.41), channel_id=1, source_target_pairs={{0,1},{1,0},{2,3},{3,2},{4,5},{5,4},{6,7},{7,6},{8,9},{9,8},{10,11... | collective-permute-start | bytes 147464 | tf_op jit(solution)/shard_map/ppermute | solution.py:280
  40.1 5.4 %collective-permute-start.3 = (f32[4,3,8,128]{3,2,1,0:T(8,128)S(1)}, f32[4,3,8,128]{3,2,1,0:T(8,128)S(1)}, u32[]{:S(2)}, u32[]{:S(2)}) collective-permute-start(f32[4,3,8,128]{3,2,1,0:T(8,128)S(1)} %get-tuple-element.42), channel_id=1, source_target_pairs={{0,3},{1,2},{2,1},{3,0},{4,7},{5,6},{6,5},{7,4},{8,11},{9,10},{10,... | collective-permute-start | bytes 147464 | tf_op jit(solution)/shard_map/ppermute | solution.py:280
  66.4 3.8 %collective-permute-start.4 = (f32[1,384]{1,0:T(1,128)S(1)}, f32[1,384]{1,0:T(1,128)S(1)}, u32[]{:S(2)}, u32[]{:S(2)}) collective-permute-start(f32[1,384]{1,0:T(1,128)S(1)} %reduce_sum.12), channel_id=1, source_target_pairs={{0,64},{64,128},{128,192},{192,0},{1,65},{65,129},{129,193},{193,1... | collective-permute-start | bytes 4616 | tf_op jit(solution)/shard_map/ppermute | solution.py:355
  67.7 2.4 %collective-permute-start.5 = (f32[1,384]{1,0:T(1,128)S(1)}, f32[1,384]{1,0:T(1,128)S(1)}, u32[]{:S(2)}, u32[]{:S(2)}) collective-permute-start(f32[1,384]{1,0:T(1,128)S(1)} %reduce_sum.12), channel_id=1, source_target_pairs={{64,0},{128,64},{192,128},{0,192},{65,1},{129,65},{193,129},{1,193... | collective-permute-start | bytes 4616 | tf_op jit(solution)/shard_map/ppermute | solution.py:356

commit v9 on v8

--- a/solution.py
+++ b/solution.py
@@ -218,6 +218,12 @@
 
 def spread_kernel(own_ref, out_ref):
     out_ref[...] = jnp.broadcast_to(own_ref[...][None], out_ref.shape)
+
+
+def string_kernel(shares, own_ref, before_ref, after_ref, out_ref):
+    mixed = shares[0] * own_ref[...] + shares[1] * before_ref[...] + shares[2] * after_ref[...]
+    for c in range(3):
+        out_ref[c] = mixed[:, c * LANES:(c + 1) * LANES]
 
 
 def pack_kernel(vel_hbm, conf_hbm, out_ref, vel_ref, conf_ref, arrived):
@@ -354,8 +360,10 @@
     up = [(i, (i + 1) % images) for i in range(images)]
     earlier = lax.ppermute(updated, "image", up)
     later = lax.ppermute(updated, "image", [(target, source) for source, target in up])
-    new_string = shares[0] * updated + shares[1] * earlier + shares[2] * later
-    new_string = new_string.reshape(1, 3, LANES)
+    new_string = call(
+        string_kernel, "string", shape(3, 1, LANES), [SMEM] + [VMEM] * 3, [], 0, 10_000
+    )(shares, updated, earlier, later)
+    new_string = new_string.transpose(1, 0, 2)
     return (final_positions, new_string)
 
 

time: 73.1 us -> 74.2 us (1.015)
  waiting for transfers between devices: 11.7 us -> 15.1 us
  other arithmetic: 2.62 us -> 0.25 us
  Pallas kernels: 20.4 us -> 21.5 us
    ppermute x1, waiting for transfers between devices: 0.27 us -> 2.91 us  [on_device(): earlier = lax.ppermute(updated, 'image', up)]
    reshape x1 -> x0, other arithmetic: 2.36 us -> none  [on_device(): new_string = new_string.reshape(1, 3, LANES)]
    ppermute x1, starting transfers between devices: 1.37 us -> 0.01 us  [on_device(): earlier = lax.ppermute(updated, 'image', up)]
    ppermute x1, starting transfers between devices: 1.53 us -> 2.81 us  [on_device(): lax.ppermute(updated, 'image', [(target, source) for source, target in up])]
    pallas_call x0 -> x1, Pallas kernels: none -> 1.11 us  [on_device(): call(string_kernel, 'string', shape(3, 1, LANES), [SMEM] + [VMEM] * 3, []...]
  transfers between devices with their start and end apart: 7 -> 7, of which waited for: 2 -> 3; matrix products, arithmetic and copies ran while one was open for 1% -> 0% of each run, Pallas kernels for 13% -> 12%
where the time goes in v9:
time: 74.2 us; the launch traced here: 73.9 us
  Pallas kernels  21.5 us (29%)
  starting transfers between devices  20.1 us (27%)
  blocking collectives  15.5 us (21%)
  waiting for transfers between devices  15.1 us (20%)
  between operations  0.77 us (1%)
    all_to_all x1, blocking collectives, on_device(): lax.all_to_all(copies, ('swarm', 'domain'), split_axis=0, concat_axis=0,...  15.5 us
    all_to_all x1, starting transfers between devices, on_device(): lax.all_to_all(packed.reshape(16, 6, ROWS, LANES), 'swarm', split_axis=0,...  11.6 us
    all_to_all x1, waiting for transfers between devices, on_device(): lax.all_to_all(packed.reshape(16, 6, ROWS, LANES), 'swarm', split_axis=0,...  11.4 us
    pallas_call x1, Pallas kernels, on_device(): call(second_rim_kernel, 'second_rim', (shape(3, LANES, LANES), shape(1, 3...  5.12 us
    ppermute x2, starting transfers between devices, swap_rims(): lax.ppermute(second, 'domain', across)  5.1 us
    pallas_call x1, Pallas kernels, on_device(): inside = inner(partners, middle)  4.57 us
    pallas_call x1, Pallas kernels, on_device(): inside = inner(partners, start_pos)  4.57 us
    pallas_call x1, Pallas kernels, on_device(): call(first_rim_kernel, 'first_rim', (whole, whole, rim, rim), [SMEM, SMEM...  4.33 us
  transfers between devices with their start and end apart: 7, of which 3 were waited for; matrix products, arithmetic and copies ran while one was open for 0% of the time, Pallas kernels for 12%

profile of v9, /device:TPU:1, one launch (start us, length us, event | category | flops | bytes accessed | tf_op | source)
XLA Modules:
  0.0 73.9 jit_solution(15645988208120958719)
XLA Ops:
  0.6 1.7 %pack.1 = f32[768,128]{1,0:T(8,128)} custom-call(f32[3,16,1024]{2,1,0:T(8,128)} %bitcast.18, f32[3,8,128]{2,1,0:T(8,128)} %bitcast.19), custom_call_target="tpu_custom_call" | custom-call | bytes 600000 | tf_op jit(solution)/shard_map/pack/pallas_call | solution.py:301
  2.4 0.0 copy-start
  2.4 11.6 %all-to-all-start = ((f32[16,6,8,128]{3,2,1,0:T(8,128)}), f32[16,6,8,128]{3,2,1,0:T(8,128)S(1)}, u32[]{:S(2)}, u32[]{:S(2)}) async-start(f32[16,6,8,128]{3,2,1,0:T(8,128)} %bitcast.17), calls=%async_computation | async-start | bytes 786432 | tf_op jit(solution)/shard_map/all_to_all | solution.py:310
  14.0 0.0 copy-start.1
  14.0 0.0 copy-done
  14.0 0.7 copy-done.1
  14.7 11.4 %all-to-all-done = f32[16,6,8,128]{3,2,1,0:T(8,128)S(1)} async-done(((f32[16,6,8,128]{3,2,1,0:T(8,128)}), f32[16,6,8,128]{3,2,1,0:T(8,128)S(1)}, u32[]{:S(2)}, u32[]{:S(2)}) %all-to-all-start) | async-done | bytes 393248 | tf_op jit(solution)/shard_map/all_to_all | solution.py:310
  26.2 4.3 %collective-permute-start.1 = (f32[4,3,8,128]{3,2,1,0:T(8,128)S(1)}, f32[4,3,8,128]{3,2,1,0:T(8,128)S(1)}, u32[]{:S(2)}, u32[]{:S(2)}) collective-permute-start(f32[4,3,8,128]{3,2,1,0:T(8,128)S(1)} %get-tuple-element.58), channel_id=1, source_target_pairs={{0,3},{1,2},{2,1},{3,0},{4,7},{5,6},{6,5},{7,4},{8,11},{9,10},{10,... | collective-permute-start | bytes 147464 | tf_op jit(solution)/shard_map/ppermute | solution.py:286
  30.5 0.0 collective-permute-start
  30.5 4.6 %inner.2 = (f32[8,3,8,128]{3,2,1,0:T(8,128)S(1)}, bf16[128,32,128]{2,1,0:T(8,128)(2,1)S(1)}, bf16[128,16,128]{2,1,0:T(8,128)(2,1)S(1)}) custom-call(s32[2,128]{1,0:T(2,128)S(1)} %get-tuple-element.33.pairs, f32[16,3,8,128]{3,2,1,0:T(8,128)S(1)} %get-tuple-element.57.field_ref), custom_call_target="tpu_custom_call" | custom-call | flops 8000000000 | tf_op jit(solution)/shard_map/inner/pallas_call | solution.py:337
  35.0 0.1 maximum_multiply_fusion.shares
  35.1 0.1 pad_add_fusion.place
  35.2 0.0 collective-permute-done.1.rim2_ref
  35.2 0.0 collective-permute-done.rim1_ref
  35.2 4.3 %first_rim.1 = (f32[16,3,8,128]{3,2,1,0:T(8,128)S(1)}, f32[16,3,8,128]{3,2,1,0:T(8,128)S(1)}, f32[4,3,8,128]{3,2,1,0:T(8,128)S(1)}, f32[4,3,8,128]{3,2,1,0:T(8,128)S(1)}) custom-call(s32[2,128]{1,0:T(2,128)S(1)} %get-tuple-element.33.pairs, s32[3]{0:T(128)S(1)} %pad_add_fusion.place, f32[16,3,8,128]{3,2,1,0:T(8,128)S(1)} %get-tuple-element.57.field_ref, ...), custom_call_target="tpu_custom_call" | custom-call | flops 8000000000 | tf_op jit(solution)/shard_map/first_rim/pallas_call | solution.py:338
  39.5 0.6 collective-permute-start.2
  40.1 0.8 %collective-permute-start.3 = (f32[4,3,8,128]{3,2,1,0:T(8,128)S(1)}, f32[4,3,8,128]{3,2,1,0:T(8,128)S(1)}, u32[]{:S(2)}, u32[]{:S(2)}) collective-permute-start(f32[4,3,8,128]{3,2,1,0:T(8,128)S(1)} %get-tuple-element.42), channel_id=1, source_target_pairs={{0,3},{1,2},{2,1},{3,0},{4,7},{5,6},{6,5},{7,4},{8,11},{9,10},{10,... | collective-permute-start | bytes 147464 | tf_op jit(solution)/shard_map/ppermute | solution.py:286
  41.0 4.6 %inner.3 = (f32[8,3,8,128]{3,2,1,0:T(8,128)S(1)}, bf16[128,32,128]{2,1,0:T(8,128)(2,1)S(1)}, bf16[128,16,128]{2,1,0:T(8,128)(2,1)S(1)}) custom-call(s32[2,128]{1,0:T(2,128)S(1)} %get-tuple-element.33.pairs, f32[16,3,8,128]{3,2,1,0:T(8,128)S(1)} %get-tuple-element.40.field_ref), custom_call_target="tpu_custom_call" | custom-call | flops 8000000000 | tf_op jit(solution)/shard_map/inner/pallas_call | solution.py:344
  45.5 0.0 collective-permute-done.2.rim1_ref
  45.6 0.0 collective-permute-done.3.rim2_ref
  45.6 5.1 %second_rim.1 = (f32[3,128,128]{2,1,0:T(8,128)}, f32[1,384]{1,0:T(1,128)S(1)}) custom-call(s32[2,128]{1,0:T(2,128)S(1)} %get-tuple-element.33.pairs, s32[3]{0:T(128)S(1)} %pad_add_fusion.place, s32[16,128]{1,0:T(8,128)S(1)} %get-tuple-element.35.groups_ref, f32[16,3,8,128]{3,2,1,0:T(8,128)S(1)} %get-tuple-element.40.field_ref, ...), custom_call_target="tpu_custom_call" | custom-call | flops 8000000000 | tf_op jit(solution)/shard_map/second_rim/pallas_call | solution.py:345
  50.7 15.5 %all_to_all.10 = f32[64,1,384]{2,1,0:T(1,128)S(1)} all-to-all(f32[64,1,384]{2,1,0:T(1,128)S(1)} %spread.1), channel_id=1, replica_groups=mesh['image'=4,'swarm'=16,'domain'=4] {'swarm','domain'}, dimensions={0} | all-to-all | bytes 196608 | tf_op jit(solution)/shard_map/all_to_all | solution.py:358
  66.2 0.1 reduce_sum.11
  66.3 2.8 %collective-permute-start.5 = (f32[1,384]{1,0:T(1,128)S(1)}, f32[1,384]{1,0:T(1,128)S(1)}, u32[]{:S(2)}, u32[]{:S(2)}) collective-permute-start(f32[1,384]{1,0:T(1,128)S(1)} %reduce_sum.12.own_ref), channel_id=1, source_target_pairs={{64,0},{128,64},{192,128},{0,192},{65,1},{129,65},{193,129},{1,193... | collective-permute-start | bytes 4616 | tf_op jit(solution)/shard_map/ppermute | solution.py:362
  69.1 0.0 collective-permute-start.4
  69.1 0.7 collective-permute-done.5.after_ref
  69.9 2.9 %collective-permute-done.4.before_ref = f32[1,384]{1,0:T(1,128)S(1)} collective-permute-done((f32[1,384]{1,0:T(1,128)S(1)}, f32[1,384]{1,0:T(1,128)S(1)}, u32[]{:S(2)}, u32[]{:S(2)}) %collective-permute-start.4) | collective-permute-done | bytes 1568 | tf_op jit(solution)/shard_map/ppermute | solution.py:361
  72.8 1.1 %string.1 = f32[3,1,128]{2,1,0:T(1,128)} custom-call(f32[3]{0:T(128)S(1)} %maximum_multiply_fusion.shares, f32[1,384]{1,0:T(1,128)S(1)} %reduce_sum.12.own_ref, f32[1,384]{1,0:T(1,128)S(1)} %collective-permute-done.4.before_ref, f32[1,384]{1,0:T(1,128)S(1)} %collective-permute-done.5.after_ref), custom_call_target="tpu_custom_call" | custom-call | bytes 10000 | tf_op jit(solution)/shard_map/string/pallas_call | solution.py:363
  (5 shorter events, 0.1 us)
Async XLA Ops:
  2.4 11.6 %copy-start = (s32[128,16]{0,1:T(8,128)S(1)}, s32[128,16]{0,1:T(8,128)}, u32[]{:S(2)}) copy-start(s32[128,16]{0,1:T(8,128)} %param.7) | copy-start | bytes 24580
  2.4 23.7 %all-to-all-start = ((f32[16,6,8,128]{3,2,1,0:T(8,128)}), f32[16,6,8,128]{3,2,1,0:T(8,128)S(1)}, u32[]{:S(2)}, u32[]{:S(2)}) async-start(f32[16,6,8,128]{3,2,1,0:T(8,128)} %bitcast.17), calls=%async_computation | async-start | bytes 786432 | tf_op jit(solution)/shard_map/all_to_all | solution.py:310
  14.0 0.7 copy-start.1
  26.2 9.0 %collective-permute-start.1 = (f32[4,3,8,128]{3,2,1,0:T(8,128)S(1)}, f32[4,3,8,128]{3,2,1,0:T(8,128)S(1)}, u32[]{:S(2)}, u32[]{:S(2)}) collective-permute-start(f32[4,3,8,128]{3,2,1,0:T(8,128)S(1)} %get-tuple-element.58), channel_id=1, source_target_pairs={{0,3},{1,2},{2,1},{3,0},{4,7},{5,6},{6,5},{7,4},{8,11},{9,10},{10,... | collective-permute-start | bytes 147464 | tf_op jit(solution)/shard_map/ppermute | solution.py:286
  30.5 4.8 %collective-permute-start = (f32[4,3,8,128]{3,2,1,0:T(8,128)S(1)}, f32[4,3,8,128]{3,2,1,0:T(8,128)S(1)}, u32[]{:S(2)}, u32[]{:S(2)}) collective-permute-start(f32[4,3,8,128]{3,2,1,0:T(8,128)S(1)} %get-tuple-element.59), channel_id=1, source_target_pairs={{0,1},{1,0},{2,3},{3,2},{4,5},{5,4},{6,7},{7,6},{8,9},{9,8},{10,11... | collective-permute-start | bytes 147464 | tf_op jit(solution)/shard_map/ppermute | solution.py:286
  39.5 6.0 %collective-permute-start.2 = (f32[4,3,8,128]{3,2,1,0:T(8,128)S(1)}, f32[4,3,8,128]{3,2,1,0:T(8,128)S(1)}, u32[]{:S(2)}, u32[]{:S(2)}) collective-permute-start(f32[4,3,8,128]{3,2,1,0:T(8,128)S(1)} %get-tuple-element.41), channel_id=1, source_target_pairs={{0,1},{1,0},{2,3},{3,2},{4,5},{5,4},{6,7},{7,6},{8,9},{9,8},{10,11... | collective-permute-start | bytes 147464 | tf_op jit(solution)/shard_map/ppermute | solution.py:286
  40.1 5.4 %collective-permute-start.3 = (f32[4,3,8,128]{3,2,1,0:T(8,128)S(1)}, f32[4,3,8,128]{3,2,1,0:T(8,128)S(1)}, u32[]{:S(2)}, u32[]{:S(2)}) collective-permute-start(f32[4,3,8,128]{3,2,1,0:T(8,128)S(1)} %get-tuple-element.42), channel_id=1, source_target_pairs={{0,3},{1,2},{2,1},{3,0},{4,7},{5,6},{6,5},{7,4},{8,11},{9,10},{10,... | collective-permute-start | bytes 147464 | tf_op jit(solution)/shard_map/ppermute | solution.py:286
  66.3 3.5 %collective-permute-start.5 = (f32[1,384]{1,0:T(1,128)S(1)}, f32[1,384]{1,0:T(1,128)S(1)}, u32[]{:S(2)}, u32[]{:S(2)}) collective-permute-start(f32[1,384]{1,0:T(1,128)S(1)} %reduce_sum.12.own_ref), channel_id=1, source_target_pairs={{64,0},{128,64},{192,128},{0,192},{65,1},{129,65},{193,129},{1,193... | collective-permute-start | bytes 4616 | tf_op jit(solution)/shard_map/ppermute | solution.py:362
  69.1 3.6 %collective-permute-start.4 = (f32[1,384]{1,0:T(1,128)S(1)}, f32[1,384]{1,0:T(1,128)S(1)}, u32[]{:S(2)}, u32[]{:S(2)}) collective-permute-start(f32[1,384]{1,0:T(1,128)S(1)} %reduce_sum.12.own_ref), channel_id=1, source_target_pairs={{0,64},{64,128},{128,192},{192,0},{1,65},{65,129},{129,193},{193,1... | collective-permute-start | bytes 4616 | tf_op jit(solution)/shard_map/ppermute | solution.py:361

commit v10 on v8

--- a/solution.py
+++ b/solution.py
@@ -283,7 +283,7 @@
 def string_shares(place):
     before = (place > 0).astype(F32) * smoothing
     after = (place < lax.axis_size("image") - 1).astype(F32) * smoothing
-    return jnp.stack([1.0 - before - after, before, after])
+    return 1.0 - before - after, before, after
 
 
 def on_device(configuration, velocities, pairs, cv_atoms):
@@ -341,7 +341,7 @@
         [SMEM, SMEM] + [VMEM] * 8, ROW_SCRATCH + TABLES, WORK, 0,
     )(partners, place, groups, middle, rim1, rim2, *inside, base)
     images, members = lax.axis_size("image"), lax.axis_size("swarm")
-    shares = string_shares(image) / (members * GSIZE)
+    shares = tuple(share / (members * GSIZE) for share in string_shares(image))
     part, shares = lax.optimization_barrier((part, shares))
     final_positions = final.reshape(1, 1, 3, 1, LANES * LANES)
 

time: 73.1 us -> 71.2 us (0.974)
  other arithmetic: 2.62 us -> 0.74 us
    ppermute x2, starting transfers between devices: 0.6 us -> 4.1 us  [swap_rims(): lax.ppermute(first, 'domain', inside)]
    ppermute x2, starting transfers between devices: 5.09 us -> 1.6 us  [swap_rims(): lax.ppermute(second, 'domain', across)]
    reshape x1, other arithmetic: 2.36 us -> 0.57 us  [on_device(): new_string = new_string.reshape(1, 3, LANES)]
  transfers between devices with their start and end apart: 7 -> 7, of which waited for: 2 -> 2; matrix products, arithmetic and copies ran while one was open for 1% -> 0% of each run, Pallas kernels for 13% -> 13%
where the time goes in v10:
time: 71.2 us; the launch traced here: 70.7 us
  Pallas kernels  20.3 us (29%)
  starting transfers between devices  20.2 us (28%)
  blocking collectives  15.6 us (22%)
  waiting for transfers between devices  12.3 us (17%)
  between operations  0.76 us (1%)
  other arithmetic  0.74 us (1%)
  local copies, waits for them, and re-layouts  0.72 us (1%)
    all_to_all x1, blocking collectives, on_device(): lax.all_to_all(copies, ('swarm', 'domain'), split_axis=0, concat_axis=0,...  15.6 us
    all_to_all x1, starting transfers between devices, on_device(): lax.all_to_all(packed.reshape(16, 6, ROWS, LANES), 'swarm', split_axis=0,...  11.6 us
    all_to_all x1, waiting for transfers between devices, on_device(): lax.all_to_all(packed.reshape(16, 6, ROWS, LANES), 'swarm', split_axis=0,...  11.4 us
    pallas_call x1, Pallas kernels, on_device(): call(second_rim_kernel, 'second_rim', (shape(3, LANES, LANES), shape(1, 3...  5.11 us
    pallas_call x1, Pallas kernels, on_device(): inside = inner(partners, middle)  4.57 us
    pallas_call x1, Pallas kernels, on_device(): inside = inner(partners, start_pos)  4.56 us
    pallas_call x1, Pallas kernels, on_device(): call(first_rim_kernel, 'first_rim', (whole, whole, rim, rim), [SMEM, SMEM...  4.33 us
    ppermute x2, starting transfers between devices, swap_rims(): lax.ppermute(first, 'domain', inside)  4.1 us
  transfers between devices with their start and end apart: 7, of which 2 were waited for; matrix products, arithmetic and copies ran while one was open for 0% of the time, Pallas kernels for 13%

profile of v10, /device:TPU:1, one launch (start us, length us, event | category | flops | bytes accessed | tf_op | source)
XLA Modules:
  0.0 70.7 jit_solution(9083813088536888234)
XLA Ops:
  0.6 1.7 %pack.1 = f32[768,128]{1,0:T(8,128)} custom-call(f32[3,16,1024]{2,1,0:T(8,128)} %bitcast.16, f32[3,8,128]{2,1,0:T(8,128)} %bitcast.17), custom_call_target="tpu_custom_call" | custom-call | bytes 600000 | tf_op jit(solution)/shard_map/pack/pallas_call | solution.py:295
  2.4 0.0 copy-start
  2.4 11.6 %all-to-all-start = ((f32[16,6,8,128]{3,2,1,0:T(8,128)}), f32[16,6,8,128]{3,2,1,0:T(8,128)S(1)}, u32[]{:S(2)}, u32[]{:S(2)}) async-start(f32[16,6,8,128]{3,2,1,0:T(8,128)} %bitcast.15), calls=%async_computation | async-start | bytes 786432 | tf_op jit(solution)/shard_map/all_to_all | solution.py:304
  14.0 0.0 copy-start.1
  14.0 0.0 copy-done
  14.0 0.7 copy-done.1
  14.7 11.4 %all-to-all-done = f32[16,6,8,128]{3,2,1,0:T(8,128)S(1)} async-done(((f32[16,6,8,128]{3,2,1,0:T(8,128)}), f32[16,6,8,128]{3,2,1,0:T(8,128)S(1)}, u32[]{:S(2)}, u32[]{:S(2)}) %all-to-all-start) | async-done | bytes 393248 | tf_op jit(solution)/shard_map/all_to_all | solution.py:304
  26.2 3.6 %collective-permute-start = (f32[4,3,8,128]{3,2,1,0:T(8,128)S(1)}, f32[4,3,8,128]{3,2,1,0:T(8,128)S(1)}, u32[]{:S(2)}, u32[]{:S(2)}) collective-permute-start(f32[4,3,8,128]{3,2,1,0:T(8,128)S(1)} %get-tuple-element.63), channel_id=1, source_target_pairs={{0,1},{1,0},{2,3},{3,2},{4,5},{5,4},{6,7},{7,6},{8,9},{9,8},{10,11... | collective-permute-start | bytes 147464 | tf_op jit(solution)/shard_map/ppermute | solution.py:280
  29.8 0.8 %collective-permute-start.1 = (f32[4,3,8,128]{3,2,1,0:T(8,128)S(1)}, f32[4,3,8,128]{3,2,1,0:T(8,128)S(1)}, u32[]{:S(2)}, u32[]{:S(2)}) collective-permute-start(f32[4,3,8,128]{3,2,1,0:T(8,128)S(1)} %get-tuple-element.62), channel_id=1, source_target_pairs={{0,3},{1,2},{2,1},{3,0},{4,7},{5,6},{6,5},{7,4},{8,11},{9,10},{10,... | collective-permute-start | bytes 147464 | tf_op jit(solution)/shard_map/ppermute | solution.py:280
  30.6 4.6 %inner.2 = (f32[8,3,8,128]{3,2,1,0:T(8,128)S(1)}, bf16[128,32,128]{2,1,0:T(8,128)(2,1)S(1)}, bf16[128,16,128]{2,1,0:T(8,128)(2,1)S(1)}) custom-call(s32[2,128]{1,0:T(2,128)S(1)} %get-tuple-element.35.pairs, f32[16,3,8,128]{3,2,1,0:T(8,128)S(1)} %get-tuple-element.61.field_ref), custom_call_target="tpu_custom_call" | custom-call | flops 8000000000 | tf_op jit(solution)/shard_map/inner/pallas_call | solution.py:331
  35.1 0.1 pad_add_fusion.place
  35.2 0.0 collective-permute-done.rim1_ref
  35.2 0.0 collective-permute-done.1.rim2_ref
  35.2 4.3 %first_rim.1 = (f32[16,3,8,128]{3,2,1,0:T(8,128)S(1)}, f32[16,3,8,128]{3,2,1,0:T(8,128)S(1)}, f32[4,3,8,128]{3,2,1,0:T(8,128)S(1)}, f32[4,3,8,128]{3,2,1,0:T(8,128)S(1)}) custom-call(s32[2,128]{1,0:T(2,128)S(1)} %get-tuple-element.35.pairs, s32[3]{0:T(128)S(1)} %pad_add_fusion.place, f32[16,3,8,128]{3,2,1,0:T(8,128)S(1)} %get-tuple-element.61.field_ref, ...), custom_call_target="tpu_custom_call" | custom-call | flops 8000000000 | tf_op jit(solution)/shard_map/first_rim/pallas_call | solution.py:332
  39.5 0.5 collective-permute-start.2
  40.1 0.8 %collective-permute-start.3 = (f32[4,3,8,128]{3,2,1,0:T(8,128)S(1)}, f32[4,3,8,128]{3,2,1,0:T(8,128)S(1)}, u32[]{:S(2)}, u32[]{:S(2)}) collective-permute-start(f32[4,3,8,128]{3,2,1,0:T(8,128)S(1)} %get-tuple-element.44), channel_id=1, source_target_pairs={{0,3},{1,2},{2,1},{3,0},{4,7},{5,6},{6,5},{7,4},{8,11},{9,10},{10,... | collective-permute-start | bytes 147464 | tf_op jit(solution)/shard_map/ppermute | solution.py:280
  40.9 4.6 %inner.3 = (f32[8,3,8,128]{3,2,1,0:T(8,128)S(1)}, bf16[128,32,128]{2,1,0:T(8,128)(2,1)S(1)}, bf16[128,16,128]{2,1,0:T(8,128)(2,1)S(1)}) custom-call(s32[2,128]{1,0:T(2,128)S(1)} %get-tuple-element.35.pairs, f32[16,3,8,128]{3,2,1,0:T(8,128)S(1)} %get-tuple-element.42.field_ref), custom_call_target="tpu_custom_call" | custom-call | flops 8000000000 | tf_op jit(solution)/shard_map/inner/pallas_call | solution.py:338
  45.5 0.0 collective-permute-done.2.rim1_ref
  45.5 0.0 collective-permute-done.3.rim2_ref
  45.5 5.1 %second_rim.1 = (f32[3,128,128]{2,1,0:T(8,128)}, f32[1,384]{1,0:T(1,128)S(1)}) custom-call(s32[2,128]{1,0:T(2,128)S(1)} %get-tuple-element.35.pairs, s32[3]{0:T(128)S(1)} %pad_add_fusion.place, s32[16,128]{1,0:T(8,128)S(1)} %get-tuple-element.37.groups_ref, f32[16,3,8,128]{3,2,1,0:T(8,128)S(1)} %get-tuple-element.42.field_ref, ...), custom_call_target="tpu_custom_call" | custom-call | flops 8000000000 | tf_op jit(solution)/shard_map/second_rim/pallas_call | solution.py:339
  50.6 15.6 %all_to_all.10 = f32[64,1,384]{2,1,0:T(1,128)S(1)} all-to-all(f32[64,1,384]{2,1,0:T(1,128)S(1)} %spread.1), channel_id=1, replica_groups=mesh['image'=4,'swarm'=16,'domain'=4] {'swarm','domain'}, dimensions={0} | all-to-all | bytes 196608 | tf_op jit(solution)/shard_map/all_to_all | solution.py:352
  66.2 0.1 reduce_sum.11
  66.3 1.4 %collective-permute-start.4 = (f32[1,384]{1,0:T(1,128)S(1)}, f32[1,384]{1,0:T(1,128)S(1)}, u32[]{:S(2)}, u32[]{:S(2)}) collective-permute-start(f32[1,384]{1,0:T(1,128)S(1)} %reduce_sum.12), channel_id=1, source_target_pairs={{0,64},{64,128},{128,192},{192,0},{1,65},{65,129},{129,193},{193,1... | collective-permute-start | bytes 4616 | tf_op jit(solution)/shard_map/ppermute | solution.py:355
  67.7 1.5 %collective-permute-start.5 = (f32[1,384]{1,0:T(1,128)S(1)}, f32[1,384]{1,0:T(1,128)S(1)}, u32[]{:S(2)}, u32[]{:S(2)}) collective-permute-start(f32[1,384]{1,0:T(1,128)S(1)} %reduce_sum.12), channel_id=1, source_target_pairs={{64,0},{128,64},{192,128},{0,192},{65,1},{129,65},{193,129},{1,193... | collective-permute-start | bytes 4616 | tf_op jit(solution)/shard_map/ppermute | solution.py:356
  69.2 0.9 %collective-permute-done.4 = f32[1,384]{1,0:T(1,128)S(1)} collective-permute-done((f32[1,384]{1,0:T(1,128)S(1)}, f32[1,384]{1,0:T(1,128)S(1)}, u32[]{:S(2)}, u32[]{:S(2)}) %collective-permute-start.4) | collective-permute-done | bytes 1568 | tf_op jit(solution)/shard_map/ppermute | solution.py:355
  70.1 0.0 collective-permute-done.5
  70.1 0.6 add_bitcast_fusion
  (5 shorter events, 0.1 us)
Async XLA Ops:
  2.4 11.6 %copy-start = (s32[128,16]{0,1:T(8,128)S(1)}, s32[128,16]{0,1:T(8,128)}, u32[]{:S(2)}) copy-start(s32[128,16]{0,1:T(8,128)} %param.7) | copy-start | bytes 24580
  2.4 23.7 %all-to-all-start = ((f32[16,6,8,128]{3,2,1,0:T(8,128)}), f32[16,6,8,128]{3,2,1,0:T(8,128)S(1)}, u32[]{:S(2)}, u32[]{:S(2)}) async-start(f32[16,6,8,128]{3,2,1,0:T(8,128)} %bitcast.15), calls=%async_computation | async-start | bytes 786432 | tf_op jit(solution)/shard_map/all_to_all | solution.py:304
  14.0 0.7 copy-start.1
  26.2 9.0 %collective-permute-start = (f32[4,3,8,128]{3,2,1,0:T(8,128)S(1)}, f32[4,3,8,128]{3,2,1,0:T(8,128)S(1)}, u32[]{:S(2)}, u32[]{:S(2)}) collective-permute-start(f32[4,3,8,128]{3,2,1,0:T(8,128)S(1)} %get-tuple-element.63), channel_id=1, source_target_pairs={{0,1},{1,0},{2,3},{3,2},{4,5},{5,4},{6,7},{7,6},{8,9},{9,8},{10,11... | collective-permute-start | bytes 147464 | tf_op jit(solution)/shard_map/ppermute | solution.py:280
  29.8 5.4 %collective-permute-start.1 = (f32[4,3,8,128]{3,2,1,0:T(8,128)S(1)}, f32[4,3,8,128]{3,2,1,0:T(8,128)S(1)}, u32[]{:S(2)}, u32[]{:S(2)}) collective-permute-start(f32[4,3,8,128]{3,2,1,0:T(8,128)S(1)} %get-tuple-element.62), channel_id=1, source_target_pairs={{0,3},{1,2},{2,1},{3,0},{4,7},{5,6},{6,5},{7,4},{8,11},{9,10},{10,... | collective-permute-start | bytes 147464 | tf_op jit(solution)/shard_map/ppermute | solution.py:280
  39.5 5.9 %collective-permute-start.2 = (f32[4,3,8,128]{3,2,1,0:T(8,128)S(1)}, f32[4,3,8,128]{3,2,1,0:T(8,128)S(1)}, u32[]{:S(2)}, u32[]{:S(2)}) collective-permute-start(f32[4,3,8,128]{3,2,1,0:T(8,128)S(1)} %get-tuple-element.43), channel_id=1, source_target_pairs={{0,1},{1,0},{2,3},{3,2},{4,5},{5,4},{6,7},{7,6},{8,9},{9,8},{10,11... | collective-permute-start | bytes 147464 | tf_op jit(solution)/shard_map/ppermute | solution.py:280
  40.1 5.4 %collective-permute-start.3 = (f32[4,3,8,128]{3,2,1,0:T(8,128)S(1)}, f32[4,3,8,128]{3,2,1,0:T(8,128)S(1)}, u32[]{:S(2)}, u32[]{:S(2)}) collective-permute-start(f32[4,3,8,128]{3,2,1,0:T(8,128)S(1)} %get-tuple-element.44), channel_id=1, source_target_pairs={{0,3},{1,2},{2,1},{3,0},{4,7},{5,6},{6,5},{7,4},{8,11},{9,10},{10,... | collective-permute-start | bytes 147464 | tf_op jit(solution)/shard_map/ppermute | solution.py:280
  66.3 3.8 %collective-permute-start.4 = (f32[1,384]{1,0:T(1,128)S(1)}, f32[1,384]{1,0:T(1,128)S(1)}, u32[]{:S(2)}, u32[]{:S(2)}) collective-permute-start(f32[1,384]{1,0:T(1,128)S(1)} %reduce_sum.12), channel_id=1, source_target_pairs={{0,64},{64,128},{128,192},{192,0},{1,65},{65,129},{129,193},{193,1... | collective-permute-start | bytes 4616 | tf_op jit(solution)/shard_map/ppermute | solution.py:355
  67.7 2.4 %collective-permute-start.5 = (f32[1,384]{1,0:T(1,128)S(1)}, f32[1,384]{1,0:T(1,128)S(1)}, u32[]{:S(2)}, u32[]{:S(2)}) collective-permute-start(f32[1,384]{1,0:T(1,128)S(1)} %reduce_sum.12), channel_id=1, source_target_pairs={{64,0},{128,64},{192,128},{0,192},{65,1},{129,65},{193,129},{1,193... | collective-permute-start | bytes 4616 | tf_op jit(solution)/shard_map/ppermute | solution.py:356
